TPU v7x, 32 devices: a whole 2x2x4 slice. The times are simulated.
32 devices in a mesh: grp: 2 (over y), lay: 4 (over z), wid: 2 (over x), rep: 2 (over core).
Axes of the slice: x: 2, y: 2, z: 4, core: 2. Of those that a mesh axis runs over, the one named last changes fastest.
Arguments:
- acts: bfloat16 [4, 1024, 2048], P(None, ('grp', 'rep'), 'wid'), parts along dimension 1, may hold values from -6 to 6
- targets: bfloat16 [4, 1024, 2048], P(None, ('grp', 'rep'), 'wid'), parts along dimension 1, may hold values from -6 to 6
- enc_weight: bfloat16 [2048, 8192], P('wid', 'lay'), may hold values from -0.125 to 0.125
- enc_bias: float32 [8192], P('lay'), may hold values from -3 to 3
- gate_mask: int32 [1024, 32], P(('grp', 'rep'), 'lay'), parts along dimension 0, may hold values 0 or 1
- dec_list: int32 [84, 3], P('lay'), may hold values from -1 to 7, as said below
- dec_weight: bfloat16 [84, 256, 2048], P('lay', None, 'wid'), may hold values from -0.125 to 0.125
Outputs:
- grad_enc: float32 [4096, 8192], P(('grp', 'wid'), ('lay', 'rep')), parts along dimension 0
- grad_bias: float32 [16384], P(('grp', 'lay', 'rep')), parts along dimension 0
- grad_dec: float32 [168, 256, 2048], P(('grp', 'lay'), 'rep', 'wid'), parts along dimension 0
There are 2 independent parts, one for each index of `grp`. A program takes and returns all parts, laid end to end along the dimension named above; an argument that names none is the same for every part. Nothing has to cross between parts.
Inputs may be any that keep to these rules, and one draw needn't show every extreme that they name: `dec_list`: each row is (source layer, target layer, latent block within the layer's slab); every triple with source <= target < 4 and block < 8 stands in exactly one row; every other row is (-1, -1, -1).
All inputs are finite; a program needn't handle non-finite values. No bound on the sum of `gate_mask` on one device may be relied on, other than what follows from the above.
Results may differ from a plain program's by a relative error of at most 0.019.
Values may be sent and summed in bfloat16 or wider, within the bound.
No kernel may reach another device: no remote copies, remote signals or barrier semaphores. Data moves between devices by JAX's collectives and lax.ppermute only.
A program may use at most 128 MiB of HBM per device.

v0:
```python
import jax
import jax.numpy as jnp
from jax import lax
from jax.sharding import PartitionSpec as P

ROOT = 0.7978845608028654
CUBIC = 0.044715


def smooth_gate(shifted):
    inside_arg = ROOT * (shifted + CUBIC * shifted * shifted * shifted)
    return 0.5 * shifted * (1.0 + jnp.tanh(inside_arg))


def gate_slope(shifted):
    inside_arg = ROOT * (shifted + CUBIC * shifted * shifted * shifted)
    tanh_part = jnp.tanh(inside_arg)
    return 0.5 * (1.0 + tanh_part) + 0.5 * shifted * (1.0 - tanh_part * tanh_part) * ROOT * (
        1.0 + 3.0 * CUBIC * shifted * shifted
    )


def local(acts, targets, enc_weight, enc_bias, gate_mask, dec_list, dec_weight):
    layers, tok_rows, width_part = acts.shape
    lat_dev = enc_weight.shape[1]
    block_size = dec_weight.shape[1]
    per_dev = lat_dev // block_size
    lay_count = lax.axis_size("lay")
    lay_index = lax.axis_index("lay")
    lat_total = lat_dev * lay_count
    blocks_total = lat_total // block_size
    latents_layer = lat_total // layers
    blocks_layer = latents_layer // block_size
    layer_here = lay_index * lat_dev // latents_layer
    inputs = lax.dynamic_index_in_dim(acts, layer_here, 0, keepdims=False)
    partial_pre = jnp.dot(inputs, enc_weight, preferred_element_type=jnp.float32)
    pre_sum = lax.psum(partial_pre.astype(jnp.bfloat16), "wid").astype(jnp.float32)
    shifted = (pre_sum + enc_bias[None, :]).reshape(tok_rows, per_dev, block_size)
    keep_mask = gate_mask.astype(jnp.float32)[:, :, None]
    latent = (smooth_gate(shifted) * keep_mask).astype(jnp.bfloat16).reshape(tok_rows, lat_dev)
    all_latent = lax.all_gather(latent, "lay", axis=1, tiled=True).reshape(
        tok_rows, blocks_total, block_size
    )
    block_id = dec_list[:, 0] * blocks_layer + dec_list[:, 2]
    target_layer = dec_list[:, 1]
    slot_valid = (target_layer >= 0).astype(jnp.float32)
    target_hot = (target_layer[:, None] == jnp.arange(layers, dtype=jnp.int32)[None, :]).astype(
        jnp.float32
    )
    block_hot = (block_id[:, None] == jnp.arange(blocks_total, dtype=jnp.int32)[None, :]).astype(
        jnp.float32
    )
    slot_lat = jnp.take(all_latent, jnp.maximum(block_id, 0), axis=1)
    contrib = jnp.einsum("tkb,kbd->ktd", slot_lat, dec_weight, preferred_element_type=jnp.float32)
    recon_part = jnp.einsum("kl,ktd->ltd", target_hot, contrib, precision=lax.Precision.HIGHEST)
    recon = lax.psum_scatter(
        recon_part.astype(jnp.bfloat16), "lay", scatter_dimension=1, tiled=True
    ).astype(jnp.float32)
    row_count = recon.shape[1]
    own_target = lax.dynamic_slice_in_dim(targets, lay_index * row_count, row_count, 1)
    scale = float(tok_rows * lax.axis_size("rep")) ** (-0.5)
    scaled_error = ((recon - own_target.astype(jnp.float32)) * scale).astype(jnp.bfloat16)
    error_full = lax.all_gather(scaled_error, "lay", axis=1, tiled=True)
    err_slot = jnp.take(error_full, jnp.maximum(target_layer, 0), axis=0)
    dec_grad = (
        jnp.einsum("tkb,ktd->kbd", slot_lat, err_slot, preferred_element_type=jnp.float32)
        * slot_valid[:, None, None]
    )
    slot_error = jnp.einsum(
        "ktd,kbd->tkb", err_slot, dec_weight, preferred_element_type=jnp.float32
    )
    summed = lax.psum(slot_error.astype(jnp.bfloat16), "wid").astype(jnp.float32)
    outgoing = jnp.einsum("tkb,kg->tgb", summed, block_hot, precision=lax.Precision.HIGHEST).astype(
        jnp.bfloat16
    )
    incoming = lax.all_to_all(outgoing, "lay", split_axis=1, concat_axis=1, tiled=True)
    latent_error = jnp.sum(
        incoming.reshape(tok_rows, lay_count, per_dev, block_size), axis=1, dtype=jnp.float32
    )
    pre_grad = (latent_error * keep_mask * gate_slope(shifted)).astype(jnp.bfloat16)
    pre_flat = pre_grad.reshape(tok_rows, lat_dev)
    enc_grad = lax.dot_general(
        inputs, pre_flat, (((0,), (0,)), ((), ())), preferred_element_type=jnp.float32
    )
    bias_grad = jnp.sum(pre_flat, axis=0, dtype=jnp.float32)
    enc_out, bias_out, dec_out = (
        lax.psum_scatter(
            enc_grad.astype(jnp.bfloat16), "rep", scatter_dimension=1, tiled=True
        ).astype(jnp.float32),
        lax.psum_scatter(
            bias_grad.astype(jnp.bfloat16), "rep", scatter_dimension=0, tiled=True
        ).astype(jnp.float32),
        lax.psum_scatter(
            dec_grad.astype(jnp.bfloat16), "rep", scatter_dimension=1, tiled=True
        ).astype(jnp.float32),
    )
    return (enc_out, bias_out, dec_out)


def solution(mesh):
    return jax.shard_map(
        local,
        mesh=mesh,
        in_specs=(
            P(None, ("grp", "rep"), "wid"),
            P(None, ("grp", "rep"), "wid"),
            P("wid", "lay"),
            P("lay"),
            P(("grp", "rep"), "lay"),
            P("lay", None),
            P("lay", None, "wid"),
        ),
        out_specs=(
            P(("grp", "wid"), ("lay", "rep")),
            P(("grp", "lay", "rep")),
            P(("grp", "lay"), "rep", "wid"),
        ),
        check_vma=False,
    )
```

profile of v0, /device:TPU:0, one launch (start us, length us, event | category | flops | bytes accessed | tf_op | source)
XLA Modules:
  0.0 588.5 jit_solution(1712257840101359199)
XLA Ops:
  7.2 0.0 copy-start
  7.2 0.0 all-reduce.6.cloned.1.call-start
  7.2 1.5 copy-done
  8.8 0.0 copy-start.4
  8.8 4.4 convolution_convert_fusion.1
  13.2 0.0 all-reduce.6.cloned.1.call-update
  13.2 0.0 all-gather.3.cloned.1.call-start
  13.3 0.0 copy-done.4
  13.3 0.1 copy.26
  13.4 0.0 copy-start.3
  13.4 0.3 mul.121
  13.8 2.3 copy.39
  16.0 0.0 copy-start.5
  16.0 40.1 %all-reduce.6.cloned.1.call-done = bf16[256,2048]{1,0:T(8,128)(2,1)} async-done(((bf16[256,2048]{1,0:T(8,128)(2,1)}), bf16[256,2048]{1,0:T(8,128)(2,1)}) %all-reduce.6.cloned.1.call-update) | async-done | bytes 1048592 | tf_op jit(solution)/shard_map/psum | solution.py:37
  56.1 0.0 copy-done.3
  56.1 3.7 multiply_convert_fusion.1
  59.8 0.0 all-gather.3.cloned.1.call-update
  59.8 0.0 all-reduce.10.cloned.1.call-start
  59.9 0.0 copy-done.5
  59.9 80.8 %all-gather.3.cloned.1.call-done = bf16[256,8192]{1,0:T(8,128)(2,1)} async-done(((bf16[256,2048]{1,0:T(8,128)(2,1)}), bf16[256,8192]{1,0:T(8,128)(2,1)}) %all-gather.3.cloned.1.call-update) | async-done | bytes 4194320 | tf_op jit(solution)/shard_map/all_gather | solution.py:41
  140.7 4.7 copy.50
  145.5 4.6 gather_fusion
  150.0 15.3 %fusion.6 = f32[21,256,1024]{2,1,0:T(8,128)} fusion(bf16[21,256,1024]{2,1,0:T(8,128)(2,1)} %param.13, bf16[21,256,256]{2,1,0:T(8,128)(2,1)} %gather_fusion, pred[21]{0:T(512)(128)(4,1)S(1)} %get-tuple-element.5), kind=kOutput, calls=%fused_computation.16 | convolution fusion | flops 2819948544 | bytes 35782676 | tf_op jit(solution)/shard_map/tkb,kbd->ktd/dot_general | solution.py:54
  165.4 0.0 copy-start.7
  165.4 28.4 %fusion.19 = bf16[4,256,1024]{2,0,1:T(4,128)(2,1)} fusion(f32[21,256,1024]{2,1,0:T(8,128)} %fusion.6, s32[21]{0:T(128)S(1)} %get-tuple-element.9), kind=kOutput, calls=%fused_computation.32 | convolution fusion | flops 265289808 | bytes 24117332 | tf_op jit(solution)/shard_map/kl,ktd->ltd/dot_general | solution.py:55
  193.8 0.0 all-reduce.10.cloned.1.call-update
  193.8 0.0 all-gather.5.cloned.1.call-start
  193.8 0.0 copy-done.7
  193.8 0.6 dynamic-slice
  195.1 1.1 constant_dynamic-slice_fusion
  196.2 82.8 %all-reduce.10.cloned.1.call-done = bf16[4,256,1024]{2,0,1:T(4,128)(2,1)} async-done(((bf16[4,256,1024]{2,0,1:T(4,128)(2,1)}), bf16[4,256,1024]{2,0,1:T(4,128)(2,1)}) %all-reduce.10.cloned.1.call-update) | async-done | bytes 2097168
  279.0 2.5 multiply_convert_fusion.2
  281.4 0.0 all-gather.5.cloned.1.call-update
  281.4 0.0 all-reduce.8.cloned.1.call-start
  281.5 45.0 %all-gather.5.cloned.1.call-done = bf16[4,256,1024]{2,0,1:T(4,128)(2,1)} async-done(((bf16[4,64,1024]{2,0,1:T(4,128)(2,1)}), bf16[4,256,1024]{2,0,1:T(4,128)(2,1)}) %all-gather.5.cloned.1.call-update) | async-done | bytes 2097168 | tf_op jit(solution)/shard_map/all_gather | solution.py:63
  326.5 3.5 copy.30
  330.0 7.4 %gather_fusion.1 = bf16[21,256,1024]{2,1,0:T(8,128)(2,1)} fusion(bf16[4,256,1024]{2,1,0:T(8,128)(2,1)} %copy.30, s32[1024]{0:T(1024)S(1)} %pad_clamp_fusion), kind=kCustom, calls=%fused_computation.1 | custom fusion | bytes 22020180 | tf_op jit(solution)/shard_map/jit(_take)/gather | solution.py:64
  337.5 14.4 %convert_bitcast_fusion.1 = bf16[256,21,256]{2,0,1:T(8,128)(2,1)} fusion(bf16[21,256,1024]{2,1,0:T(8,128)(2,1)} %param.13, bf16[21,256,1024]{2,1,0:T(8,128)(2,1)} %gather_fusion.1, pred[21]{0:T(512)(128)(4,1)S(1)} %get-tuple-element.7), kind=kOutput, calls=%fused_computation.18 | convolution fusion | flops 2825453568 | bytes 24772628 | tf_op jit(solution)/shard_map/ktd,kbd->tkb/dot_general | solution.py:69
  351.9 0.0 all-reduce.8.cloned.1.call-update
  351.9 0.0 reduce-scatter.3.cloned.1.call-start
  352.0 76.0 %all-reduce.8.cloned.1.call-done = bf16[256,21,256]{2,0,1:T(8,128)(2,1)} async-done(((bf16[256,21,256]{2,0,1:T(8,128)(2,1)}), bf16[256,21,256]{2,0,1:T(8,128)(2,1)}) %all-reduce.8.cloned.1.call-update) | async-done | bytes 2752528 | tf_op jit(solution)/shard_map/psum | solution.py:72
  428.0 4.1 convert_bitcast_fusion
  432.1 2.4 copy.32
  434.6 97.5 %all_to_all.5 = bf16[256,32,256]{2,0,1:T(8,128)(2,1)S(1)} all-to-all(bf16[256,32,256]{2,0,1:T(8,128)(2,1)S(1)} %copy.32), channel_id=1, replica_groups=mesh['grp'=2,'lay'=4,'wid'=2,'rep'=2] {'lay'}, dimensions={1} | all-to-all | bytes 8388608 | tf_op jit(solution)/shard_map/all_to_all | solution.py:76
  532.1 0.7 convert_reduce_fusion
  532.8 0.0 copy-start.1
  532.8 0.0 copy-start.2
  532.8 0.3 copy.38
  533.1 1.3 copy-done.1
  534.4 0.3 copy-done.2
  534.7 1.6 fusion.37
  536.3 3.3 convolution_convert_fusion
  539.6 0.0 reduce-scatter.3.cloned.1.call-update
  539.6 0.0 reduce-scatter.5.cloned.1.call-start
  539.7 10.7 %multiply_convert_fusion = bf16[21,256,1024]{2,1,0:T(8,128)(2,1)} fusion(f32[21]{0:T(128)S(1)} %compare_convert_fusion, bf16[21,256,1024]{2,1,0:T(8,128)(2,1)} %gather_fusion.1, pred[21]{0:T(512)(128)(4,1)S(1)} %get-tuple-element.7, bf16[21,256,256]{2,1,0:T(8,128)(2,1)} %gather_fusion, pred[21]{0:T(512)(128)(4,1)S(1)} %get-tuple-element.5), kind=kOutput, calls=%fused_computation.4 | convolution fusion | flops 2836463616 | bytes 24772734 | tf_op jit(solution)/shard_map/tkb,ktd->kbd/dot_general | solution.py:66
  550.4 0.0 copy-start.6
  550.4 0.0 reduce-scatter.5.cloned.1.call-update
  550.4 0.6 copy-done.6
  551.0 0.6 dynamic-slice.2
  552.3 2.5 all-reduce.1
  554.7 0.6 dynamic-slice_convert_fusion
  555.3 4.1 convert_element_type.90
  559.4 14.1 %reduce-scatter.5.cloned.1.call-done = bf16[21,128,1024]{2,1,0:T(8,128)(2,1)} async-done(((bf16[21,256,1024]{2,1,0:T(8,128)(2,1)}), bf16[21,128,1024]{2,1,0:T(8,128)(2,1)}) %reduce-scatter.5.cloned.1.call-update) | async-done | bytes 5505040 | tf_op jit(solution)/shard_map/reduce_scatter | solution.py:93
  573.5 8.2 %convert_element_type.94 = f32[21,128,1024]{2,1,0:T(8,128)} convert(bf16[21,128,1024]{2,1,0:T(8,128)(2,1)} %reduce-scatter.5.cloned.1.call-done) | non-fusion elementwise | flops 2752512 | bytes 16515072 | tf_op jit(solution)/shard_map/convert_element_type | solution.py:95
  (8 shorter events, 0.0 us)
Async XLA Ops:
  7.2 1.6 copy-start
  7.2 48.9 %all-reduce.6.cloned.1.call-start = ((), (), s32[]{:S(2)}) async-start(), calls=%async_computation.3 | async-start | bytes 2097152 | tf_op jit(solution)/shard_map/psum | solution.py:37
  8.8 4.5 copy-start.4
  13.2 127.5 %all-gather.3.cloned.1.call-start = ((), (), s32[]{:S(2)}) async-start(), calls=%async_computation.4 | async-start | bytes 5242880 | tf_op jit(solution)/shard_map/all_gather | solution.py:41
  13.4 42.7 %copy-start.3 = (f32[2048]{0:T(1024)S(1)}, f32[2048]{0:T(1024)}, u32[]{:S(2)}) copy-start(f32[2048]{0:T(1024)} %param.10) | copy-start | bytes 24580
  16.0 43.8 %copy-start.5 = (s32[21,3]{0,1:T(4,128)S(1)}, s32[21,3]{0,1:T(4,128)}, u32[]{:S(2)}) copy-start(s32[21,3]{0,1:T(4,128)} %param.12) | copy-start | bytes 760
  59.8 219.1 %all-reduce.10.cloned.1.call-start = ((), (), s32[]{:S(2)}) async-start(), calls=%async_computation.9 | async-start | bytes 4194304
  165.4 28.5 %copy-start.7 = (u32[32]{0:T(128)S(1)}, u32[32]{0:T(128)}, u32[]{:S(2)}) copy-start(u32[32]{0:T(128)} %constant.86) | copy-start | bytes 388
  193.8 132.7 %all-gather.5.cloned.1.call-start = ((), (), s32[]{:S(2)}) async-start(), calls=%async_computation.5 | async-start | bytes 2621440 | tf_op jit(solution)/shard_map/all_gather | solution.py:63
  281.4 146.5 %all-reduce.8.cloned.1.call-start = ((), (), s32[]{:S(2)}) async-start(), calls=%async_computation.6 | async-start | bytes 5505024 | tf_op jit(solution)/shard_map/psum | solution.py:72
  351.9 203.4 %reduce-scatter.3.cloned.1.call-start = ((), (), s32[]{:S(2)}) async-start(), calls=%async_computation.7 | async-start | bytes 6291456 | tf_op jit(solution)/shard_map/reduce_scatter | solution.py:87
  532.8 1.6 copy-start.1
  532.8 1.8 copy-start.2
  539.6 33.8 %reduce-scatter.5.cloned.1.call-start = ((), (), s32[]{:S(2)}) async-start(), calls=%async_computation.8 | async-start | bytes 16515072 | tf_op jit(solution)/shard_map/reduce_scatter | solution.py:93
  550.4 0.7 copy-start.6
Sparse Core Ops, SparseCore 0:
  13.3 42.7 all-reduce.5
  59.9 80.7 all-gather.2
  193.9 85.0 all-reduce.9
  281.6 44.8 all-gather.4
  352.0 75.9 all-reduce.7
  539.8 10.4 reduce-scatter.2
  552.5 20.8 reduce-scatter.4
where the time goes:
time: 589 us; the launch traced here: 588 us
  waiting for transfers between devices  339 us (58%)
  blocking collectives  100 us (17%)
  matrix products  80.7 us (14%)
  local copies, waits for them, and re-layouts  31.6 us (5%)
  other arithmetic  21.3 us (4%)
  between operations  15.6 us (3%)
    all_to_all x1, blocking collectives, local(): lax.all_to_all(outgoing, 'lay', split_axis=1, concat_axis=1, tiled=True)  97.5 us
    unnamed x8, waiting for transfers between devices  82.9 us
    all_gather x1, waiting for transfers between devices, local(): lax.all_gather(latent, 'lay', axis=1, tiled=True)  80.8 us
    psum x1, waiting for transfers between devices, local(): lax.psum(slot_error.astype(jnp.bfloat16), 'wid').astype(jnp.float32)  76 us
    all_gather x1, waiting for transfers between devices, local(): error_full = lax.all_gather(scaled_error, 'lay', axis=1, tiled=True)  45 us
    psum x1, waiting for transfers between devices, local(): lax.psum(partial_pre.astype(jnp.bfloat16), 'wid').astype(jnp.float32)  40.1 us
    dot_general x1, matrix products, local(): jnp.einsum('kl,ktd->ltd', target_hot, contrib, precision=lax.Precision.HI...  28.4 us
    dot_general x1, matrix products, local(): jnp.einsum('tkb,kbd->ktd', slot_lat, dec_weight, preferred_element_type=j...  15.3 us
  transfers between devices with their start and end apart: 7, of which 6 were waited for; matrix products, arithmetic and copies ran while one was open for 3% of the time, Pallas kernels for 0%

commit v1 on v0

v1 whole, which is shorter than its diff:
```python
import functools

import jax
import jax.numpy as jnp
from jax import lax
from jax.experimental import pallas as pl
from jax.experimental.pallas import tpu as pltpu
from jax.sharding import PartitionSpec as P

ROOT = 0.7978845608028654
CUBIC = 0.044715
F32 = jnp.float32
BF16 = jnp.bfloat16
VMEM_LIMIT = 48 * 1024 * 1024
CHUNKS = 1


def params():
    return pltpu.CompilerParams(vmem_limit_bytes=VMEM_LIMIT)


def cost(flops, nbytes):
    return pl.CostEstimate(flops=int(flops), bytes_accessed=int(nbytes), transcendentals=0)


def ring_shift(axis, by):
    count = lax.axis_size(axis)
    return [(src, (src + by) % count) for src in range(count)]


def divisor(total, most):
    return max(d for d in range(1, most + 1) if total % d == 0)


def whole(shape):
    return pl.BlockSpec(shape, lambda *_: (0,) * len(shape))


def line_gather(own):
    count = lax.axis_size("lay")
    from_left, from_right = [], []
    right, left = own, own
    for step in range(count - 1):
        right = lax.ppermute(right, "lay", [(i, i + 1) for i in range(step, count - 1)])
        left = lax.ppermute(left, "lay", [(i, i - 1) for i in range(1, count - step)])
        from_left.append(right)
        from_right.append(left)
    return from_left, from_right


def line_scatter_sum(part):
    count = lax.axis_size("lay")
    here = lax.axis_index("lay")
    right = left = None
    for step in range(count - 1):
        to_right = jnp.clip(count - 1 - step + here, 0, count - 1)
        to_left = jnp.clip(step - (count - 1 - here), 0, count - 1)
        send_right, send_left = part(to_right), part(to_left)
        if step:
            send_right = send_right + right.astype(F32)
            send_left = send_left + left.astype(F32)
        right = lax.ppermute(
            send_right.astype(BF16), "lay", [(i, i + 1) for i in range(min(step + 1, count - 1))]
        )
        left = lax.ppermute(
            send_left.astype(BF16),
            "lay",
            [(count - 1 - i, count - 2 - i) for i in range(min(step + 1, count - 1))],
        )
    return part(here) + right.astype(F32) + left.astype(F32)


def line_place(owner, here):
    count = lax.axis_size("lay")
    return jnp.where(
        owner == here, 0, jnp.where(owner < here, here - owner, count - 1 + owner - here)
    )


def encode_kernel(chunks, width, rows, scal, acts, weight, *outs):
    w = scal[1]
    for c in range(chunks):
        for m in range(width):
            piece = lax.rem(w + m, width)
            start = pl.multiple_of(c * width * rows + piece * rows, rows)
            res = jnp.dot(acts[0, pl.ds(start, rows), :], weight[...], preferred_element_type=F32)
            out = outs[c * width + m]
            out[0] = res.astype(out.dtype)


def encode(acts, weight, scal, chunks, width, block):
    layers, tok, d = acts.shape
    lat = weight.shape[1]
    rows = tok // (chunks * width)
    blocks = lat // block
    shapes, specs = [], []
    for c in range(chunks):
        for m in range(width):
            shapes.append(jax.ShapeDtypeStruct((blocks, rows, block), F32 if m == 0 else BF16))
            specs.append(pl.BlockSpec((1, rows, block), lambda b, s: (b, 0, 0)))
    return pl.pallas_call(
        functools.partial(encode_kernel, chunks, width, rows),
        grid_spec=pltpu.PrefetchScalarGridSpec(
            num_scalar_prefetch=1,
            grid=(blocks,),
            in_specs=[
                pl.BlockSpec((1, tok, d), lambda b, s: (s[0], 0, 0)),
                pl.BlockSpec((d, block), lambda b, s: (0, b)),
            ],
            out_specs=specs,
        ),
        out_shape=shapes,
        compiler_params=params(),
        cost_estimate=cost(2 * tok * d * lat, 2 * (tok * d + d * lat) + 6 * tok * lat // 2),
        name="encode",
    )(scal, acts, weight)


def gate_kernel(count, own, bias, mask, *refs):
    recv, (lat, slope) = refs[:count], refs[count:]
    v = own[...]
    for r in recv:
        v = v + r[...].astype(F32)
    v = v + bias[...]
    keep = mask[...]
    tanh_part = jnp.tanh(ROOT * (v + CUBIC * v * v * v))
    lat[...] = (0.5 * v * (1.0 + tanh_part) * keep).astype(lat.dtype)
    slope[...] = keep * (
        0.5 * (1.0 + tanh_part)
        + 0.5 * v * (1.0 - tanh_part * tanh_part) * ROOT * (1.0 + 3.0 * CUBIC * v * v)
    )


def gate(own, recv, bias, mask):
    blocks, rows, block = own.shape
    per = divisor(blocks, 4)
    spec = pl.BlockSpec((per, rows, block), lambda b: (b, 0, 0))
    return pl.pallas_call(
        functools.partial(gate_kernel, len(recv)),
        grid=(blocks // per,),
        in_specs=[
            spec,
            pl.BlockSpec((per, 1, block), lambda b: (b, 0, 0)),
            pl.BlockSpec((per, rows, 1), lambda b: (b, 0, 0)),
        ]
        + [spec] * len(recv),
        out_specs=[spec, spec],
        out_shape=[
            jax.ShapeDtypeStruct(own.shape, BF16),
            jax.ShapeDtypeStruct(own.shape, F32),
        ],
        compiler_params=params(),
        cost_estimate=cost(20 * own.size, 12 * own.size),
        name="gate",
    )(own, bias, mask, *recv)


def pick_kernel(slots, count, meta, *refs):
    bufs, out = refs[:count], refs[count]

    def one(k, carry):
        place, row = meta[k], meta[slots + k]
        for q in range(count):

            @pl.when(place == q)
            def _():
                out[k] = bufs[q][row]

        return carry

    lax.fori_loop(0, slots, one, 0)


def pick(meta, bufs, slots):
    shape = (slots,) + bufs[0].shape[1:]
    return pl.pallas_call(
        functools.partial(pick_kernel, slots, len(bufs)),
        grid_spec=pltpu.PrefetchScalarGridSpec(
            num_scalar_prefetch=1,
            grid=(1,),
            in_specs=[whole(b.shape) for b in bufs],
            out_specs=whole(shape),
        ),
        out_shape=jax.ShapeDtypeStruct(shape, BF16),
        compiler_params=params(),
        cost_estimate=cost(0, 2 * sum(b.size for b in bufs) + 4 * slots * bufs[0][0].size),
        name="pick",
    )(meta, *bufs)


def decode_kernel(slots, per, count, steps, meta, *refs):
    lats, weight, out, acc = refs[:count], refs[count], refs[count + 1], refs[count + 2]
    g = pl.program_id(0)

    @pl.when(g == 0)
    def _():
        acc[...] = jnp.zeros_like(acc)

    for j in range(per):
        target = meta[2 * slots + g * per + j]

        @pl.when(target >= 0)
        def _():
            lat = jnp.concatenate([ref[j] for ref in lats], axis=0)
            acc[target] += jnp.dot(lat, weight[j], preferred_element_type=F32)

    @pl.when(g == steps - 1)
    def _():
        out[...] = acc[...].astype(out.dtype)


def decode(meta, lats, weight, layers):
    slots, rows, block = lats[0].shape
    d = weight.shape[2]
    tok = rows * len(lats)
    per = divisor(slots, 4)
    return pl.pallas_call(
        functools.partial(decode_kernel, slots, per, len(lats), slots // per),
        grid_spec=pltpu.PrefetchScalarGridSpec(
            num_scalar_prefetch=1,
            grid=(slots // per,),
            in_specs=[pl.BlockSpec((per, rows, block), lambda g, s: (g, 0, 0))] * len(lats)
            + [pl.BlockSpec((per, block, d), lambda g, s: (g, 0, 0))],
            out_specs=whole((layers, tok, d)),
            scratch_shapes=[pltpu.VMEM((layers, tok, d), F32)],
        ),
        out_shape=jax.ShapeDtypeStruct((layers, tok, d), BF16),
        compiler_params=params(),
        cost_estimate=cost(2 * slots * tok * block * d, 2 * (weight.size + slots * tok * block)),
        name="decode",
    )(meta, *lats, weight)


def spread_kernel(slots, per, width, count, scal, meta, *refs):
    parts, weight = refs[:count], refs[count]
    error, acc = refs[count + 1], refs[count + 2]
    sends = refs[count + 3 :]
    layers, tok, d = error.shape
    rows = tok // width
    lays = (count + 1) // 2
    share = layers * tok // lays
    here = scal[2]
    g = pl.program_id(0)

    @pl.when(g == 0)
    def _():
        acc[...] = jnp.zeros_like(acc)
        for q in range(count):
            if q == 0:
                owner = here
            elif q < lays:
                owner = here - q
            else:
                owner = here + q - lays + 1

            @pl.when((owner >= 0) & (owner < lays))
            def _():
                if share >= tok:
                    full = share // tok
                    for f in range(full):
                        error[owner * full + f] = parts[q][f * tok : (f + 1) * tok, :]
                else:
                    cuts = tok // share
                    start = pl.multiple_of(lax.rem(owner, cuts) * share, share)
                    error[owner // cuts, pl.ds(start, share), :] = parts[q][...]

    for j in range(per):
        k = g * per + j
        target = meta[2 * slots + k]
        block = meta[3 * slots + k]

        @pl.when(target >= 0)
        def _():
            res = lax.dot_general(
                error[target],
                weight[j],
                (((1,), (1,)), ((), ())),
                preferred_element_type=F32,
            )
            acc[block] += res[:rows]
            for m in range(1, width):
                sends[m - 1][j] = res[m * rows : (m + 1) * rows].astype(BF16)

        @pl.when(target < 0)
        def _():
            for m in range(1, width):
                sends[m - 1][j] = jnp.zeros_like(sends[m - 1][j])


def spread(scal, meta, parts, weight, layers, tok, blocks_total, width):
    slots, block, d = weight.shape
    rows = tok // width
    per = divisor(slots, 4)
    return pl.pallas_call(
        functools.partial(spread_kernel, slots, per, width, len(parts)),
        grid_spec=pltpu.PrefetchScalarGridSpec(
            num_scalar_prefetch=2,
            grid=(slots // per,),
            in_specs=[whole(p.shape) for p in parts]
            + [pl.BlockSpec((per, block, d), lambda g, *_: (g, 0, 0))],
            out_specs=[whole((layers, tok, d)), whole((blocks_total, rows, block))]
            + [pl.BlockSpec((per, rows, block), lambda g, *_: (g, 0, 0))] * (width - 1),
        ),
        out_shape=[
            jax.ShapeDtypeStruct((layers, tok, d), BF16),
            jax.ShapeDtypeStruct((blocks_total, rows, block), F32),
        ]
        + [jax.ShapeDtypeStruct((slots, rows, block), BF16)] * (width - 1),
        compiler_params=params(),
        cost_estimate=cost(2 * slots * tok * block * d, 2 * (weight.size + 3 * layers * tok * d)),
        name="spread",
    )(scal, meta, *parts, weight)


def merge_kernel(slots, count, meta, own, *refs):
    recv, out, acc = refs[:count], refs[count], refs[count + 1]
    acc[...] = own[...]

    def one(k, carry):
        block = meta[3 * slots + k]

        @pl.when(block >= 0)
        def _():
            for r in recv:
                acc[block] += r[k].astype(F32)

        return carry

    lax.fori_loop(0, slots, one, 0)
    out[...] = acc[...].astype(out.dtype)


def merge(meta, own, recv):
    slots = recv[0].shape[0]
    return pl.pallas_call(
        functools.partial(merge_kernel, slots, len(recv)),
        grid_spec=pltpu.PrefetchScalarGridSpec(
            num_scalar_prefetch=1,
            grid=(1,),
            in_specs=[whole(own.shape)] + [whole(r.shape) for r in recv],
            out_specs=whole(own.shape),
            scratch_shapes=[pltpu.VMEM(own.shape, F32)],
        ),
        out_shape=jax.ShapeDtypeStruct(own.shape, BF16),
        compiler_params=params(),
        cost_estimate=cost(own.size, 6 * own.size + sum(2 * r.size for r in recv)),
        name="merge",
    )(meta, own, *recv)


def dec_grad_kernel(slots, per, groups, scal, meta, *refs):
    total = sum(groups)
    lats, errs, out = refs[:total], refs[total : total + len(groups)], refs[total + len(groups)]
    g = pl.program_id(0)
    for j in range(per):
        target = meta[2 * slots + g * per + j]

        @pl.when(target >= 0)
        def _():
            res = None
            at = 0
            for err, many in zip(errs, groups):
                lat = jnp.concatenate([ref[j] for ref in lats[at : at + many]], axis=0)
                at += many
                term = lax.dot_general(
                    lat, err[target], (((0,), (0,)), ((), ())), preferred_element_type=F32
                )
                res = term if res is None else res + term
            out[j] = res

        @pl.when(target < 0)
        def _():
            out[j] = jnp.zeros_like(out[j])


def dec_grad(scal, meta, pieces, cols, slots):
    lats, errs, specs, groups = [], [], [], []
    per = divisor(slots, 4)
    for arrays, all_columns, err in pieces:
        groups.append(len(arrays))
        errs.append(err)
        for a in arrays:
            lats.append(a)
            specs.append(
                pl.BlockSpec(
                    (per, a.shape[1], cols),
                    (lambda g, s, _: (g, 0, s[3])) if all_columns else (lambda g, s, _: (g, 0, 0)),
                )
            )
    d = errs[0].shape[2]
    tok = sum(e.shape[1] for e in errs)
    return pl.pallas_call(
        functools.partial(dec_grad_kernel, slots, per, tuple(groups)),
        grid_spec=pltpu.PrefetchScalarGridSpec(
            num_scalar_prefetch=2,
            grid=(slots // per,),
            in_specs=specs + [whole(e.shape) for e in errs],
            out_specs=pl.BlockSpec((per, cols, d), lambda g, s, _: (g, 0, 0)),
        ),
        out_shape=jax.ShapeDtypeStruct((slots, cols, d), F32),
        compiler_params=params(),
        cost_estimate=cost(
            2 * slots * tok * cols * d, 4 * slots * cols * d + sum(2 * e.size for e in errs)
        ),
        name="dec_grad",
    )(scal, meta, *lats, *errs)


def local(acts, targets, enc_weight, enc_bias, gate_mask, dec_list, dec_weight):
    layers, tok_rows, d = acts.shape
    lat_dev = enc_weight.shape[1]
    slots, block, _ = dec_weight.shape
    per_dev = lat_dev // block
    lays, width, reps = lax.axis_size("lay"), lax.axis_size("wid"), lax.axis_size("rep")
    lay, wid, rep = lax.axis_index("lay"), lax.axis_index("wid"), lax.axis_index("rep")
    blocks_total = per_dev * lays
    latents_layer = lat_dev * lays // layers
    blocks_layer = latents_layer // block
    layer_here = lay * lat_dev // latents_layer
    chunks = CHUNKS
    tok = tok_rows // chunks
    rows = tok // width
    share = layers * tok // lays
    cols = block // reps
    scale = float(tok_rows * reps) ** (-0.5)

    scal = jnp.stack([layer_here, wid, lay, rep]).astype(jnp.int32)
    listed = dec_list[:, 1] >= 0
    block_id = jnp.where(listed, dec_list[:, 0] * blocks_layer + dec_list[:, 2], 0)
    meta = jnp.concatenate(
        [
            line_place(block_id // per_dev, lay),
            block_id % per_dev,
            dec_list[:, 1],
            jnp.where(listed, block_id, -1),
        ]
    ).astype(jnp.int32)

    def relative(array, axis):
        out = []
        for c in range(chunks):
            pieces = [
                lax.dynamic_slice_in_dim(
                    array, c * tok + ((wid + m) % width) * rows, rows, axis
                )
                for m in range(width)
            ]
            out.append(jnp.concatenate(pieces, axis))
        return out

    inputs = lax.dynamic_index_in_dim(acts, layer_here, 0, keepdims=False)
    inputs_rel = jnp.concatenate(relative(inputs, 0), 0)
    targets_rel = relative(targets, 1)
    bias = enc_bias.reshape(per_dev, 1, block)
    keep = gate_mask.astype(F32).T[:, :, None]

    partial = encode(acts, enc_weight, scal, chunks, width, block)
    lat_pieces, slopes, errors, lat_other = [], [], [], []
    for c in range(chunks):
        part = partial[c * width : (c + 1) * width]
        recv = [
            lax.ppermute(part[m], "wid", ring_shift("wid", m)) for m in range(1, width)
        ]
        keep_own = lax.dynamic_slice_in_dim(keep, c * tok + wid * rows, rows, 1)
        latent, slope = gate(part[0], recv, bias, keep_own)
        slopes.append(slope)
        from_left, from_right = line_gather(latent)
        own_slots = pick(meta, [latent] + from_left + from_right, slots)
        lat_pieces.append(
            [own_slots]
            + [
                lax.ppermute(own_slots, "wid", ring_shift("wid", -m)) for m in range(1, width)
            ]
        )

    for c in range(chunks):
        recon = decode(meta, lat_pieces[c], dec_weight, layers).reshape(lays, share, d)

        def addend(dest, recon=recon):
            return lax.dynamic_index_in_dim(recon, dest, 0, keepdims=False).astype(F32)

        summed = line_scatter_sum(addend)
        own_target = lax.dynamic_slice_in_dim(
            targets_rel[c].reshape(layers * tok, d), lay * share, share, 0
        )
        own_error = ((summed - own_target.astype(F32)) * scale).astype(BF16)
        from_left, from_right = line_gather(own_error)
        errors.append([own_error] + from_left + from_right)

    pieces, grads = [], []
    for c in range(chunks):
        error, acc, *sends = spread(
            scal, meta, errors[c], dec_weight, layers, tok, blocks_total, width
        )
        recv = [
            lax.ppermute(sends[m - 1], "wid", ring_shift("wid", m)) for m in range(1, width)
        ]
        pieces.append((lat_pieces[c], True, error))
        whole_lat = jnp.concatenate(lat_pieces[c], 1)
        for m in range(1, reps):
            theirs = ((rep - m) % reps) * cols
            sent = lax.dynamic_slice_in_dim(whole_lat, theirs, cols, 2)
            pieces.append(
                (
                    [lax.ppermute(sent, "rep", ring_shift("rep", -m))],
                    False,
                    lax.ppermute(error, "rep", ring_shift("rep", -m)),
                )
            )
        merged = merge(meta, acc, recv).reshape(lays, per_dev, rows, block)

        def addend(dest, merged=merged):
            return lax.dynamic_index_in_dim(merged, dest, 0, keepdims=False).astype(F32)

        latent_error = line_scatter_sum(addend)
        pre_grad = (latent_error * slopes[c]).astype(BF16).transpose(1, 0, 2).reshape(rows, lat_dev)
        grads.append(
            jnp.concatenate(
                [pre_grad]
                + [
                    lax.ppermute(pre_grad, "wid", ring_shift("wid", -m)) for m in range(1, width)
                ],
                0,
            )
        )
    dec_out = dec_grad(scal, meta, pieces, cols, slots)

    grad_rel = jnp.concatenate(grads, 0)
    part_cols = lat_dev // reps
    acts_all, grads_all = [inputs_rel], [
        lax.dynamic_slice_in_dim(grad_rel, rep * part_cols, part_cols, 1)
    ]
    for m in range(1, reps):
        acts_all.append(lax.ppermute(inputs_rel, "rep", ring_shift("rep", -m)))
        sent = lax.dynamic_slice_in_dim(grad_rel, ((rep - m) % reps) * part_cols, part_cols, 1)
        grads_all.append(lax.ppermute(sent, "rep", ring_shift("rep", -m)))
    acts_cat = jnp.concatenate(acts_all, 0)
    grads_cat = jnp.concatenate(grads_all, 0)
    enc_out = lax.dot_general(
        acts_cat, grads_cat, (((0,), (0,)), ((), ())), preferred_element_type=F32
    )
    bias_out = jnp.sum(grads_cat, axis=0, dtype=F32)
    return enc_out, bias_out, dec_out


def solution(mesh):
    return jax.shard_map(
        local,
        mesh=mesh,
        in_specs=(
            P(None, ("grp", "rep"), "wid"),
            P(None, ("grp", "rep"), "wid"),
            P("wid", "lay"),
            P("lay"),
            P(("grp", "rep"), "lay"),
            P("lay", None),
            P("lay", None, "wid"),
        ),
        out_specs=(
            P(("grp", "wid"), ("lay", "rep")),
            P(("grp", "lay", "rep")),
            P(("grp", "lay"), "rep", "wid"),
        ),
        check_vma=False,
    )
```

time: 589 us -> 325 us (0.55)
  waiting for transfers between devices: 339 us -> 185 us
  blocking collectives: 100 us -> 0 us
  matrix products: 80.7 us -> 3.32 us
  starting transfers between devices: 0.29 us -> 58.9 us
  Pallas kernels: 0 us -> 48.3 us
  local copies, waits for them, and re-layouts: 31.6 us -> 10.7 us
  between operations: 15.6 us -> 1.08 us
    ppermute x0 -> x32, waiting for transfers between devices: none -> 185 us  [the longest x6 65.6 us: line_gather(): lax.ppermute(left, 'lay', [(i, i - 1) for i in range(1, count - step)])]
    all_gather x2 -> x0, waiting for transfers between devices: 126 us -> none  [the longest x1 80.8 us: local(): lax.all_gather(latent, 'lay', axis=1, tiled=True)]
    psum x2 -> x0, waiting for transfers between devices: 116 us -> none  [the longest x1 76 us: local(): lax.psum(slot_error.astype(jnp.bfloat16), 'wid').astype(jnp.float32)]
    all_to_all x1 -> x0, blocking collectives: 97.5 us -> none  [local(): lax.all_to_all(outgoing, 'lay', split_axis=1, concat_axis=1, tiled=True)]
    unnamed x8 -> x0, waiting for transfers between devices: 82.9 us -> none
    dot_general x7 -> x1, matrix products: 80.7 us -> 3.32 us  [local(): lax.dot_general(acts_cat, grads_cat, (((0,), (0,)), ((), ())), preferred_...]
    ppermute x0 -> x32, starting transfers between devices: none -> 58.9 us  [the longest x6 24.3 us: line_scatter_sum(): lax.ppermute(send_right.astype(BF16), 'lay', [(i, i + 1) for i in range(m...]
    pallas_call x0 -> x7, Pallas kernels: none -> 48.3 us  [the longest x1 13.5 us: spread(): pl.pallas_call(functools.partial(spread_kernel, slots, per, width, len(pa...]
  transfers between devices with their start and end apart: 7 -> 32, of which waited for: 6 -> 18; matrix products, arithmetic and copies ran while one was open for 3% -> 5% of each run, Pallas kernels for 0% -> 4%
where the time goes in v1:
time: 325 us; the launch traced here: 324 us
  waiting for transfers between devices  185 us (57%)
  starting transfers between devices  58.9 us (18%)
  Pallas kernels  48.3 us (15%)
  other arithmetic  16.7 us (5%)
  local copies, waits for them, and re-layouts  10.7 us (3%)
  matrix products  3.32 us (1%)
    ppermute x6, waiting for transfers between devices, line_gather(): lax.ppermute(left, 'lay', [(i, i - 1) for i in range(1, count - step)])  65.6 us
    ppermute x6, waiting for transfers between devices, line_scatter_sum(): lax.ppermute(send_right.astype(BF16), 'lay', [(i, i + 1) for i in range(m...  32.9 us
    ppermute x1, waiting for transfers between devices, local(): lax.ppermute(own_slots, 'wid', ring_shift('wid', -m))  27.8 us
    ppermute x6, starting transfers between devices, line_scatter_sum(): lax.ppermute(send_right.astype(BF16), 'lay', [(i, i + 1) for i in range(m...  24.3 us
    ppermute x6, waiting for transfers between devices, line_scatter_sum(): lax.ppermute(send_left.astype(BF16), 'lay', [(count - 1 - i, count - 2 -...  21.4 us
    ppermute x1, waiting for transfers between devices, local(): lax.ppermute(sends[m - 1], 'wid', ring_shift('wid', m))  18.9 us
    pallas_call x1, Pallas kernels, spread(): pl.pallas_call(functools.partial(spread_kernel, slots, per, width, len(pa...  13.5 us
    ppermute x6, starting transfers between devices, line_gather(): lax.ppermute(right, 'lay', [(i, i + 1) for i in range(step, count - 1)])  12.2 us
  transfers between devices with their start and end apart: 32, of which 18 were waited for; matrix products, arithmetic and copies ran while one was open for 5% of the time, Pallas kernels for 4%

profile of v1, /device:TPU:0, one launch (start us, length us, event | category | flops | bytes accessed | tf_op | source)
XLA Modules:
  0.0 323.9 jit_solution(2316451960143452066)
XLA Ops:
  0.7 1.6 copy-done.3
  2.3 6.4 %encode.1 = (f32[8,128,256]{2,1,0:T(8,128)S(1)}, bf16[8,128,256]{2,1,0:T(8,128)(2,1)S(1)}) custom-call(s32[4]{0:T(128)S(1)} %pad_add_fusion.1.scal, bf16[4,256,1024]{2,1,0:T(8,128)(2,1)S(1)} %copy-done.3, bf16[1024,2048]{1,0:T(8,128)(2,1)} %weight.1), custom_call_target="tpu_custom_call" | custom-call | flops 1073741824 | bytes 6291456 | tf_op jit(solution)/shard_map/encode/pallas_call | solution.py:101
  8.8 3.0 collective-permute-start.1
  12.0 11.7 %collective-permute-done.1.refs_0_ = bf16[8,128,256]{2,1,0:T(8,128)(2,1)S(1)} collective-permute-done((bf16[8,128,256]{2,1,0:T(8,128)(2,1)S(1)}, bf16[8,128,256]{2,1,0:T(8,128)(2,1)S(1)}, u32[]{:S(2)}, u32[]{:S(2)}) %collective-permute-start.1) | collective-permute-done | bytes 524320 | tf_op jit(solution)/shard_map/ppermute | solution.py:462
  23.7 0.9 gate.1
  24.6 1.0 copy-done.4
  25.6 1.3 collective-permute-start.5
  26.9 4.6 %collective-permute-start.2 = (bf16[8,128,256]{2,1,0:T(8,128)(2,1)S(1)}, bf16[8,128,256]{2,1,0:T(8,128)(2,1)S(1)}, u32[]{:S(2)}, u32[]{:S(2)}) collective-permute-start(bf16[8,128,256]{2,1,0:T(8,128)(2,1)S(1)} %get-tuple-element.12.refs_0_), channel_id=1, source_target_pairs={{0,4},{4,8},{8,12},{1,5},{5,9},{9,13},{2,6},{6,10},{10,14},{3,7},{... | collective-permute-start | bytes 1572872 | tf_op jit(solution)/shard_map/ppermute | solution.py:44
  31.5 9.1 %collective-permute-done.5.refs_4_ = bf16[8,128,256]{2,1,0:T(8,128)(2,1)S(1)} collective-permute-done((bf16[8,128,256]{2,1,0:T(8,128)(2,1)S(1)}, bf16[8,128,256]{2,1,0:T(8,128)(2,1)S(1)}, u32[]{:S(2)}, u32[]{:S(2)}) %collective-permute-start.5) | collective-permute-done | bytes 524320 | tf_op jit(solution)/shard_map/ppermute | solution.py:45
  40.6 1.3 collective-permute-start.6
  42.6 12.0 %collective-permute-done.6.refs_5_ = bf16[8,128,256]{2,1,0:T(8,128)(2,1)S(1)} collective-permute-done((bf16[8,128,256]{2,1,0:T(8,128)(2,1)S(1)}, bf16[8,128,256]{2,1,0:T(8,128)(2,1)S(1)}, u32[]{:S(2)}, u32[]{:S(2)}) %collective-permute-start.6) | collective-permute-done | bytes 524320 | tf_op jit(solution)/shard_map/ppermute | solution.py:45
  54.7 1.3 collective-permute-start.7
  56.8 11.0 %collective-permute-done.7.refs_6_ = bf16[8,128,256]{2,1,0:T(8,128)(2,1)S(1)} collective-permute-done((bf16[8,128,256]{2,1,0:T(8,128)(2,1)S(1)}, bf16[8,128,256]{2,1,0:T(8,128)(2,1)S(1)}, u32[]{:S(2)}, u32[]{:S(2)}) %collective-permute-start.7) | collective-permute-done | bytes 524320 | tf_op jit(solution)/shard_map/ppermute | solution.py:45
  67.8 1.5 pick.1.refs_0_
  69.4 0.9 collective-permute-start.8
  70.2 27.8 %collective-permute-done.8.refs_1_ = bf16[21,128,256]{2,1,0:T(8,128)(2,1)S(1)} collective-permute-done((bf16[21,128,256]{2,1,0:T(8,128)(2,1)S(1)}, bf16[21,128,256]{2,1,0:T(8,128)(2,1)S(1)}, u32[]{:S(2)}, u32[]{:S(2)}) %collective-permute-start.8) | collective-permute-done | bytes 1376288 | tf_op jit(solution)/shard_map/ppermute | solution.py:472
  98.0 1.1 copy-done
  99.1 1.3 copy-done.1
  100.5 10.4 %decode.1 = bf16[4,256,1024]{2,1,0:T(8,128)(2,1)S(1)} custom-call(s32[84]{0:T(128)S(1)} %pad_add_fusion.meta, bf16[21,128,256]{2,1,0:T(8,128)(2,1)S(1)} %pick.1.refs_0_, bf16[21,128,256]{2,1,0:T(8,128)(2,1)S(1)} %copy-done.1, bf16[21,256,1024]{2,1,0:T(8,128)(2,1)} %refs_7_.1), custom_call_target="tpu_custom_call" | custom-call | flops 2818572288 | bytes 13762560 | tf_op jit(solution)/shard_map/decode/pallas_call | solution.py:217
  110.9 1.1 dynamic-slice_bitcast_fusion.3
  111.9 2.3 collective-permute-start.9
  114.2 1.5 collective-permute-start.12
  115.7 5.0 %collective-permute-done.9 = bf16[256,1024]{1,0:T(8,128)(2,1)} collective-permute-done((bf16[256,1024]{1,0:T(8,128)(2,1)}, bf16[256,1024]{1,0:T(8,128)(2,1)}, u32[]{:S(2)}, u32[]{:S(2)}) %collective-permute-start.9) | collective-permute-done | bytes 524320 | tf_op jit(solution)/shard_map/ppermute | solution.py:62
  120.7 2.0 fusion.16
  122.7 5.2 %collective-permute-start.10 = (bf16[256,1024]{1,0:T(8,128)(2,1)}, bf16[256,1024]{1,0:T(8,128)(2,1)}, u32[]{:S(2)}, u32[]{:S(2)}) collective-permute-start(bf16[256,1024]{1,0:T(8,128)(2,1)} %fusion.16), channel_id=1, source_target_pairs={{0,4},{4,8},{1,5},{5,9},{2,6},{6,10},{3,7},{7,11},{16,20},{20,24},... | collective-permute-start | bytes 1572872 | tf_op jit(solution)/shard_map/ppermute | solution.py:62
  127.9 6.2 %collective-permute-done.10 = bf16[256,1024]{1,0:T(8,128)(2,1)} collective-permute-done((bf16[256,1024]{1,0:T(8,128)(2,1)}, bf16[256,1024]{1,0:T(8,128)(2,1)}, u32[]{:S(2)}, u32[]{:S(2)}) %collective-permute-start.10) | collective-permute-done | bytes 524320 | tf_op jit(solution)/shard_map/ppermute | solution.py:62
  134.1 2.6 fusion.17
  136.7 1.5 collective-permute-start.13
  138.2 5.0 %collective-permute-start.11 = (bf16[256,1024]{1,0:T(8,128)(2,1)}, bf16[256,1024]{1,0:T(8,128)(2,1)}, u32[]{:S(2)}, u32[]{:S(2)}) collective-permute-start(bf16[256,1024]{1,0:T(8,128)(2,1)} %get-tuple-element.25), channel_id=1, source_target_pairs={{0,4},{4,8},{8,12},{1,5},{5,9},{9,13},{2,6},{6,10},{10,14},{3,7},{... | collective-permute-start | bytes 1572872 | tf_op jit(solution)/shard_map/ppermute | solution.py:62
  143.2 2.1 fusion.15
  145.3 1.3 collective-permute-start.14
  146.6 1.7 constant_dynamic-slice_fusion.1
  148.5 0.9 collective-permute-done.11
  149.4 15.4 %collective-permute-done.14 = bf16[256,1024]{1,0:T(8,128)(2,1)} collective-permute-done((bf16[256,1024]{1,0:T(8,128)(2,1)}, bf16[256,1024]{1,0:T(8,128)(2,1)}, u32[]{:S(2)}, u32[]{:S(2)}) %collective-permute-start.14) | collective-permute-done | bytes 524320 | tf_op jit(solution)/shard_map/ppermute | solution.py:65
  164.8 1.6 fusion.21.refs_0_
  166.4 1.3 collective-permute-start.18
  167.7 4.9 %collective-permute-start.15 = (bf16[256,1024]{1,0:T(8,128)(2,1)S(1)}, bf16[256,1024]{1,0:T(8,128)(2,1)S(1)}, u32[]{:S(2)}, u32[]{:S(2)}) collective-permute-start(bf16[256,1024]{1,0:T(8,128)(2,1)S(1)} %fusion.21.refs_0_), channel_id=1, source_target_pairs={{0,4},{4,8},{8,12},{1,5},{5,9},{9,13},{2,6},{6,10},{10,14},{3,7},{... | collective-permute-start | bytes 1572872 | tf_op jit(solution)/shard_map/ppermute | solution.py:44
  172.6 10.2 %collective-permute-done.18.refs_4_ = bf16[256,1024]{1,0:T(8,128)(2,1)S(1)} collective-permute-done((bf16[256,1024]{1,0:T(8,128)(2,1)S(1)}, bf16[256,1024]{1,0:T(8,128)(2,1)S(1)}, u32[]{:S(2)}, u32[]{:S(2)}) %collective-permute-start.18) | collective-permute-done | bytes 524320 | tf_op jit(solution)/shard_map/ppermute | solution.py:45
  182.8 1.3 collective-permute-start.19
  184.8 14.1 %collective-permute-done.19.refs_5_ = bf16[256,1024]{1,0:T(8,128)(2,1)S(1)} collective-permute-done((bf16[256,1024]{1,0:T(8,128)(2,1)S(1)}, bf16[256,1024]{1,0:T(8,128)(2,1)S(1)}, u32[]{:S(2)}, u32[]{:S(2)}) %collective-permute-start.19) | collective-permute-done | bytes 524320 | tf_op jit(solution)/shard_map/ppermute | solution.py:45
  198.9 1.3 collective-permute-start.20
  200.9 9.1 %collective-permute-done.20.refs_6_ = bf16[256,1024]{1,0:T(8,128)(2,1)S(1)} collective-permute-done((bf16[256,1024]{1,0:T(8,128)(2,1)S(1)}, bf16[256,1024]{1,0:T(8,128)(2,1)S(1)}, u32[]{:S(2)}, u32[]{:S(2)}) %collective-permute-start.20) | collective-permute-done | bytes 524320 | tf_op jit(solution)/shard_map/ppermute | solution.py:45
  210.0 13.5 %spread.1 = (bf16[4,256,1024]{2,1,0:T(8,128)(2,1)}, f32[32,128,256]{2,1,0:T(8,128)}, bf16[21,128,256]{2,1,0:T(8,128)(2,1)S(1)}) custom-call(s32[4]{0:T(128)S(1)} %pad_add_fusion.1.scal, s32[84]{0:T(128)S(1)} %pad_add_fusion.meta, bf16[256,1024]{1,0:T(8,128)(2,1)S(1)} %fusion.21.refs_0_, bf16[256,1024]{1,0:T(8,128)(2,1)S(1)} %collective-permute-done.15.refs_1_, ...), custom_call_target="tpu_custom_call" | custom-call | flops 2818572288 | bytes 17301504 | tf_op jit(solution)/shard_map/spread/pallas_call | solution.py:294
  223.5 1.4 collective-permute-start.21
  224.9 18.9 %collective-permute-done.21.refs_0_ = bf16[21,128,256]{2,1,0:T(8,128)(2,1)S(1)} collective-permute-done((bf16[21,128,256]{2,1,0:T(8,128)(2,1)S(1)}, bf16[21,128,256]{2,1,0:T(8,128)(2,1)S(1)}, u32[]{:S(2)}, u32[]{:S(2)}) %collective-permute-start.21) | collective-permute-done | bytes 1376288 | tf_op jit(solution)/shard_map/ppermute | solution.py:496
  243.8 3.7 %merge.1 = bf16[32,128,256]{2,1,0:T(8,128)(2,1)S(1)} custom-call(s32[84]{0:T(128)S(1)} %pad_add_fusion.meta, f32[32,128,256]{2,1,0:T(8,128)} %get-tuple-element.13.own, bf16[21,128,256]{2,1,0:T(8,128)(2,1)S(1)} %collective-permute-done.21.refs_0_), custom_call_target="tpu_custom_call" | custom-call | flops 1048576 | bytes 7667712 | tf_op jit(solution)/shard_map/merge/pallas_call | solution.py:335
  247.6 1.6 collective-permute-start.22
  249.9 8.0 %collective-permute-done.22 = bf16[8,128,256]{2,1,0:T(8,128)(2,1)S(1)} collective-permute-done((bf16[8,128,256]{2,1,0:T(8,128)(2,1)S(1)}, bf16[8,128,256]{2,1,0:T(8,128)(2,1)S(1)}, u32[]{:S(2)}, u32[]{:S(2)}) %collective-permute-start.22) | collective-permute-done | bytes 524320 | tf_op jit(solution)/shard_map/ppermute | solution.py:62
  258.1 4.4 %collective-permute-start.23 = (bf16[8,128,256]{2,1,0:T(8,128)(2,1)S(1)}, bf16[8,128,256]{2,1,0:T(8,128)(2,1)S(1)}, u32[]{:S(2)}, u32[]{:S(2)}) collective-permute-start(bf16[8,128,256]{2,1,0:T(8,128)(2,1)S(1)} %fusion.9), channel_id=1, source_target_pairs={{0,4},{4,8},{1,5},{5,9},{2,6},{6,10},{3,7},{7,11},{16,20},{20,24},... | collective-permute-start | bytes 1572872 | tf_op jit(solution)/shard_map/ppermute | solution.py:62
  262.5 6.6 %collective-permute-done.23 = bf16[8,128,256]{2,1,0:T(8,128)(2,1)S(1)} collective-permute-done((bf16[8,128,256]{2,1,0:T(8,128)(2,1)S(1)}, bf16[8,128,256]{2,1,0:T(8,128)(2,1)S(1)}, u32[]{:S(2)}, u32[]{:S(2)}) %collective-permute-start.23) | collective-permute-done | bytes 524320 | tf_op jit(solution)/shard_map/ppermute | solution.py:62
  269.1 1.2 fusion.10
  271.1 5.8 %collective-permute-start.24 = (bf16[8,128,256]{2,1,0:T(8,128)(2,1)}, bf16[8,128,256]{2,1,0:T(8,128)(2,1)}, u32[]{:S(2)}, u32[]{:S(2)}) collective-permute-start(bf16[8,128,256]{2,1,0:T(8,128)(2,1)} %get-tuple-element.19), channel_id=1, source_target_pairs={{0,4},{4,8},{8,12},{1,5},{5,9},{9,13},{2,6},{6,10},{10,14},{3,7},{... | collective-permute-start | bytes 1572872 | tf_op jit(solution)/shard_map/ppermute | solution.py:62
  276.9 1.0 fusion.8
  277.8 1.5 collective-permute-start.27
  279.3 2.5 fusion
  282.0 6.2 %collective-permute-done.24 = bf16[8,128,256]{2,1,0:T(8,128)(2,1)} collective-permute-done((bf16[8,128,256]{2,1,0:T(8,128)(2,1)}, bf16[8,128,256]{2,1,0:T(8,128)(2,1)}, u32[]{:S(2)}, u32[]{:S(2)}) %collective-permute-start.24) | collective-permute-done | bytes 524320 | tf_op jit(solution)/shard_map/ppermute | solution.py:62
  288.2 6.0 %collective-permute-done.27 = bf16[8,128,256]{2,1,0:T(8,128)(2,1)} collective-permute-done((bf16[8,128,256]{2,1,0:T(8,128)(2,1)}, bf16[8,128,256]{2,1,0:T(8,128)(2,1)}, u32[]{:S(2)}, u32[]{:S(2)}) %collective-permute-start.27) | collective-permute-done | bytes 524320 | tf_op jit(solution)/shard_map/ppermute | solution.py:65
  294.2 2.3 fusion.22
  296.5 1.3 copy.11
  297.8 1.4 collective-permute-start.28
  299.3 1.3 dynamic-slice_bitcast_fusion.5
  300.6 6.5 %collective-permute-done.28 = bf16[128,2048]{0,1:T(8,128)(2,1)S(1)} collective-permute-done((bf16[128,2048]{0,1:T(8,128)(2,1)S(1)}, bf16[128,2048]{0,1:T(8,128)(2,1)S(1)}, u32[]{:S(2)}, u32[]{:S(2)}) %collective-permute-start.28) | collective-permute-done | bytes 524320 | tf_op jit(solution)/shard_map/ppermute | solution.py:521
  307.9 11.9 %dec_grad.1 = f32[21,128,1024]{2,1,0:T(8,128)} custom-call(s32[4]{0:T(128)S(1)} %pad_add_fusion.1.scal, s32[84]{0:T(128)S(1)} %pad_add_fusion.meta, bf16[21,128,256]{2,1,0:T(8,128)(2,1)S(1)} %pick.1.refs_0_, bf16[21,128,256]{2,1,0:T(8,128)(2,1)S(1)} %copy-done.2, bf16[21,256,128]{2,1,0:T(8,128)(2,1)} %collective-permute-done.30.refs_2_, ...), custom_call_target="tpu_custom_call" | custom-call | flops 2818572288 | bytes 15204352 | tf_op jit(solution)/shard_map/dec_grad/pallas_call | solution.py:392
  320.6 3.3 %fusion.1 = f32[1024,1024]{1,0:T(8,128)} fusion(bf16[256,1024]{1,0:T(8,128)(2,1)S(1)} %collective-permute-done, bf16[128,1024]{1,0:T(8,128)(2,1)S(1)} %get-tuple-element.30, bf16[128,1024]{1,0:T(8,128)(2,1)S(1)} %get-tuple-element.29, bf16[256,1024]{0,1:T(8,128)(2,1)S(1)} %collective-permute-done.29, bf16[256,1024]{0,1:T(8,128)(2,1)S(1)} %get-tuple-element.31), kind=kOutput, calls=%fused_computation.9 | convolution fusion | flops 1078984704 | bytes 6291456 | tf_op jit(solution)/shard_map/dot_general | solution.py:539
  (51 shorter events, 6.9 us)
Async XLA Ops:
  0.7 1.6 copy-start.3
  2.3 9.5 %copy-start.7 = (s32[256,8]{0,1:T(8,128)S(1)}, s32[256,8]{0,1:T(8,128)}, u32[]{:S(2)}) copy-start(s32[256,8]{0,1:T(8,128)} %param.11) | copy-start | bytes 24580
  2.3 21.4 %copy-start.6 = (f32[2048]{0:T(1024)S(1)}, f32[2048]{0:T(1024)}, u32[]{:S(2)}) copy-start(f32[2048]{0:T(1024)} %param.10) | copy-start | bytes 24580
  8.8 33.9 %copy-start.8 = (s32[21,3]{0,1:T(4,128)S(1)}, s32[21,3]{0,1:T(4,128)}, u32[]{:S(2)}) copy-start(s32[21,3]{0,1:T(4,128)} %param.12) | copy-start | bytes 760
  8.8 14.9 %collective-permute-start.1 = (bf16[8,128,256]{2,1,0:T(8,128)(2,1)S(1)}, bf16[8,128,256]{2,1,0:T(8,128)(2,1)S(1)}, u32[]{:S(2)}, u32[]{:S(2)}) collective-permute-start(bf16[8,128,256]{2,1,0:T(8,128)(2,1)S(1)} %get-tuple-element.11), channel_id=1, source_target_pairs={{0,2},{2,0},{1,3},{3,1},{4,6},{6,4},{5,7},{7,5},{8,10},{10,8},{9,1... | collective-permute-start | bytes 1572872 | tf_op jit(solution)/shard_map/ppermute | solution.py:462
  24.6 1.0 copy-start.4
  25.6 15.0 %collective-permute-start.5 = (bf16[8,128,256]{2,1,0:T(8,128)(2,1)S(1)}, bf16[8,128,256]{2,1,0:T(8,128)(2,1)S(1)}, u32[]{:S(2)}, u32[]{:S(2)}) collective-permute-start(bf16[8,128,256]{2,1,0:T(8,128)(2,1)S(1)} %get-tuple-element.12.refs_0_), channel_id=1, source_target_pairs={{4,0},{8,4},{12,8},{5,1},{9,5},{13,9},{6,2},{10,6},{14,10},{7,3},{... | collective-permute-start | bytes 1572872 | tf_op jit(solution)/shard_map/ppermute | solution.py:45
  26.9 15.0 %collective-permute-start.2 = (bf16[8,128,256]{2,1,0:T(8,128)(2,1)S(1)}, bf16[8,128,256]{2,1,0:T(8,128)(2,1)S(1)}, u32[]{:S(2)}, u32[]{:S(2)}) collective-permute-start(bf16[8,128,256]{2,1,0:T(8,128)(2,1)S(1)} %get-tuple-element.12.refs_0_), channel_id=1, source_target_pairs={{0,4},{4,8},{8,12},{1,5},{5,9},{9,13},{2,6},{6,10},{10,14},{3,7},{... | collective-permute-start | bytes 1572872 | tf_op jit(solution)/shard_map/ppermute | solution.py:44
  40.6 14.1 %collective-permute-start.6 = (bf16[8,128,256]{2,1,0:T(8,128)(2,1)S(1)}, bf16[8,128,256]{2,1,0:T(8,128)(2,1)S(1)}, u32[]{:S(2)}, u32[]{:S(2)}) collective-permute-start(bf16[8,128,256]{2,1,0:T(8,128)(2,1)S(1)} %collective-permute-done.5.refs_4_), channel_id=1, source_target_pairs={{4,0},{8,4},{5,1},{9,5},{6,2},{10,6},{7,3},{11,7},{20,16},{24,20},... | collective-permute-start | bytes 1572872 | tf_op jit(solution)/shard_map/ppermute | solution.py:45
  41.9 14.1 %collective-permute-start.3 = (bf16[8,128,256]{2,1,0:T(8,128)(2,1)S(1)}, bf16[8,128,256]{2,1,0:T(8,128)(2,1)S(1)}, u32[]{:S(2)}, u32[]{:S(2)}) collective-permute-start(bf16[8,128,256]{2,1,0:T(8,128)(2,1)S(1)} %collective-permute-done.2.refs_1_), channel_id=1, source_target_pairs={{4,8},{8,12},{5,9},{9,13},{6,10},{10,14},{7,11},{11,15},{20,24},{2... | collective-permute-start | bytes 1572872 | tf_op jit(solution)/shard_map/ppermute | solution.py:44
  54.7 13.1 %collective-permute-start.7 = (bf16[8,128,256]{2,1,0:T(8,128)(2,1)S(1)}, bf16[8,128,256]{2,1,0:T(8,128)(2,1)S(1)}, u32[]{:S(2)}, u32[]{:S(2)}) collective-permute-start(bf16[8,128,256]{2,1,0:T(8,128)(2,1)S(1)} %collective-permute-done.6.refs_5_), channel_id=1, source_target_pairs={{4,0},{5,1},{6,2},{7,3},{20,16},{21,17},{22,18},{23,19}} | collective-permute-start | bytes 1572872 | tf_op jit(solution)/shard_map/ppermute | solution.py:45
  56.0 11.9 %collective-permute-start.4 = (bf16[8,128,256]{2,1,0:T(8,128)(2,1)S(1)}, bf16[8,128,256]{2,1,0:T(8,128)(2,1)S(1)}, u32[]{:S(2)}, u32[]{:S(2)}) collective-permute-start(bf16[8,128,256]{2,1,0:T(8,128)(2,1)S(1)} %collective-permute-done.3.refs_2_), channel_id=1, source_target_pairs={{8,12},{9,13},{10,14},{11,15},{24,28},{25,29},{26,30},{27,31}} | collective-permute-start | bytes 1572872 | tf_op jit(solution)/shard_map/ppermute | solution.py:44
  69.4 28.7 %collective-permute-start.8 = (bf16[21,128,256]{2,1,0:T(8,128)(2,1)S(1)}, bf16[21,128,256]{2,1,0:T(8,128)(2,1)S(1)}, u32[]{:S(2)}, u32[]{:S(2)}) collective-permute-start(bf16[21,128,256]{2,1,0:T(8,128)(2,1)S(1)} %pick.1.refs_0_), channel_id=1, source_target_pairs={{0,2},{2,0},{1,3},{3,1},{4,6},{6,4},{5,7},{7,5},{8,10},{10,8},{9,1... | collective-permute-start | bytes 4128776 | tf_op jit(solution)/shard_map/ppermute | solution.py:472
  98.0 1.1 copy-start
  99.1 1.3 copy-start.1
  111.9 8.8 %collective-permute-start.9 = (bf16[256,1024]{1,0:T(8,128)(2,1)}, bf16[256,1024]{1,0:T(8,128)(2,1)}, u32[]{:S(2)}, u32[]{:S(2)}) collective-permute-start(bf16[256,1024]{1,0:T(8,128)(2,1)} %get-tuple-element.27), channel_id=1, source_target_pairs={{0,4},{1,5},{2,6},{3,7},{16,20},{17,21},{18,22},{19,23}} | collective-permute-start | bytes 1572872 | tf_op jit(solution)/shard_map/ppermute | solution.py:62
  114.2 13.7 %collective-permute-start.12 = (bf16[256,1024]{1,0:T(8,128)(2,1)}, bf16[256,1024]{1,0:T(8,128)(2,1)}, u32[]{:S(2)}, u32[]{:S(2)}) collective-permute-start(bf16[256,1024]{1,0:T(8,128)(2,1)} %get-tuple-element.28), channel_id=1, source_target_pairs={{12,8},{13,9},{14,10},{15,11},{28,24},{29,25},{30,26},{31,27}} | collective-permute-start | bytes 1572872 | tf_op jit(solution)/shard_map/ppermute | solution.py:65
  122.7 11.4 %collective-permute-start.10 = (bf16[256,1024]{1,0:T(8,128)(2,1)}, bf16[256,1024]{1,0:T(8,128)(2,1)}, u32[]{:S(2)}, u32[]{:S(2)}) collective-permute-start(bf16[256,1024]{1,0:T(8,128)(2,1)} %fusion.16), channel_id=1, source_target_pairs={{0,4},{4,8},{1,5},{5,9},{2,6},{6,10},{3,7},{7,11},{16,20},{20,24},... | collective-permute-start | bytes 1572872 | tf_op jit(solution)/shard_map/ppermute | solution.py:62
  136.7 6.5 %collective-permute-start.13 = (bf16[256,1024]{1,0:T(8,128)(2,1)}, bf16[256,1024]{1,0:T(8,128)(2,1)}, u32[]{:S(2)}, u32[]{:S(2)}) collective-permute-start(bf16[256,1024]{1,0:T(8,128)(2,1)} %get-tuple-element.26), channel_id=1, source_target_pairs={{12,8},{8,4},{13,9},{9,5},{14,10},{10,6},{15,11},{11,7},{28,24},{2... | collective-permute-start | bytes 1572872 | tf_op jit(solution)/shard_map/ppermute | solution.py:65
  138.2 11.2 %collective-permute-start.11 = (bf16[256,1024]{1,0:T(8,128)(2,1)}, bf16[256,1024]{1,0:T(8,128)(2,1)}, u32[]{:S(2)}, u32[]{:S(2)}) collective-permute-start(bf16[256,1024]{1,0:T(8,128)(2,1)} %get-tuple-element.25), channel_id=1, source_target_pairs={{0,4},{4,8},{8,12},{1,5},{5,9},{9,13},{2,6},{6,10},{10,14},{3,7},{... | collective-permute-start | bytes 1572872 | tf_op jit(solution)/shard_map/ppermute | solution.py:62
  145.3 19.5 %collective-permute-start.14 = (bf16[256,1024]{1,0:T(8,128)(2,1)}, bf16[256,1024]{1,0:T(8,128)(2,1)}, u32[]{:S(2)}, u32[]{:S(2)}) collective-permute-start(bf16[256,1024]{1,0:T(8,128)(2,1)} %fusion.15), channel_id=1, source_target_pairs={{12,8},{8,4},{4,0},{13,9},{9,5},{5,1},{14,10},{10,6},{6,2},{15,11}... | collective-permute-start | bytes 1572872 | tf_op jit(solution)/shard_map/ppermute | solution.py:65
  166.4 16.4 %collective-permute-start.18 = (bf16[256,1024]{1,0:T(8,128)(2,1)S(1)}, bf16[256,1024]{1,0:T(8,128)(2,1)S(1)}, u32[]{:S(2)}, u32[]{:S(2)}) collective-permute-start(bf16[256,1024]{1,0:T(8,128)(2,1)S(1)} %fusion.21.refs_0_), channel_id=1, source_target_pairs={{4,0},{8,4},{12,8},{5,1},{9,5},{13,9},{6,2},{10,6},{14,10},{7,3},{... | collective-permute-start | bytes 1572872 | tf_op jit(solution)/shard_map/ppermute | solution.py:45
  167.7 16.4 %collective-permute-start.15 = (bf16[256,1024]{1,0:T(8,128)(2,1)S(1)}, bf16[256,1024]{1,0:T(8,128)(2,1)S(1)}, u32[]{:S(2)}, u32[]{:S(2)}) collective-permute-start(bf16[256,1024]{1,0:T(8,128)(2,1)S(1)} %fusion.21.refs_0_), channel_id=1, source_target_pairs={{0,4},{4,8},{8,12},{1,5},{5,9},{9,13},{2,6},{6,10},{10,14},{3,7},{... | collective-permute-start | bytes 1572872 | tf_op jit(solution)/shard_map/ppermute | solution.py:44
  182.8 16.1 %collective-permute-start.19 = (bf16[256,1024]{1,0:T(8,128)(2,1)S(1)}, bf16[256,1024]{1,0:T(8,128)(2,1)S(1)}, u32[]{:S(2)}, u32[]{:S(2)}) collective-permute-start(bf16[256,1024]{1,0:T(8,128)(2,1)S(1)} %collective-permute-done.18.refs_4_), channel_id=1, source_target_pairs={{4,0},{8,4},{5,1},{9,5},{6,2},{10,6},{7,3},{11,7},{20,16},{24,20},... | collective-permute-start | bytes 1572872 | tf_op jit(solution)/shard_map/ppermute | solution.py:45
  184.1 16.1 %collective-permute-start.16 = (bf16[256,1024]{1,0:T(8,128)(2,1)S(1)}, bf16[256,1024]{1,0:T(8,128)(2,1)S(1)}, u32[]{:S(2)}, u32[]{:S(2)}) collective-permute-start(bf16[256,1024]{1,0:T(8,128)(2,1)S(1)} %collective-permute-done.15.refs_1_), channel_id=1, source_target_pairs={{4,8},{8,12},{5,9},{9,13},{6,10},{10,14},{7,11},{11,15},{20,24},{2... | collective-permute-start | bytes 1572872 | tf_op jit(solution)/shard_map/ppermute | solution.py:44
  198.9 11.1 %collective-permute-start.20 = (bf16[256,1024]{1,0:T(8,128)(2,1)S(1)}, bf16[256,1024]{1,0:T(8,128)(2,1)S(1)}, u32[]{:S(2)}, u32[]{:S(2)}) collective-permute-start(bf16[256,1024]{1,0:T(8,128)(2,1)S(1)} %collective-permute-done.19.refs_5_), channel_id=1, source_target_pairs={{4,0},{5,1},{6,2},{7,3},{20,16},{21,17},{22,18},{23,19}} | collective-permute-start | bytes 1572872 | tf_op jit(solution)/shard_map/ppermute | solution.py:45
  200.2 9.8 %collective-permute-start.17 = (bf16[256,1024]{1,0:T(8,128)(2,1)S(1)}, bf16[256,1024]{1,0:T(8,128)(2,1)S(1)}, u32[]{:S(2)}, u32[]{:S(2)}) collective-permute-start(bf16[256,1024]{1,0:T(8,128)(2,1)S(1)} %collective-permute-done.16.refs_2_), channel_id=1, source_target_pairs={{8,12},{9,13},{10,14},{11,15},{24,28},{25,29},{26,30},{27,31}} | collective-permute-start | bytes 1572872 | tf_op jit(solution)/shard_map/ppermute | solution.py:44
  223.5 20.3 %collective-permute-start.21 = (bf16[21,128,256]{2,1,0:T(8,128)(2,1)S(1)}, bf16[21,128,256]{2,1,0:T(8,128)(2,1)S(1)}, u32[]{:S(2)}, u32[]{:S(2)}) collective-permute-start(bf16[21,128,256]{2,1,0:T(8,128)(2,1)S(1)} %get-tuple-element.14), channel_id=1, source_target_pairs={{0,2},{2,0},{1,3},{3,1},{4,6},{6,4},{5,7},{7,5},{8,10},{10,8},{9,1... | collective-permute-start | bytes 4128776 | tf_op jit(solution)/shard_map/ppermute | solution.py:496
  247.6 10.3 %collective-permute-start.22 = (bf16[8,128,256]{2,1,0:T(8,128)(2,1)S(1)}, bf16[8,128,256]{2,1,0:T(8,128)(2,1)S(1)}, u32[]{:S(2)}, u32[]{:S(2)}) collective-permute-start(bf16[8,128,256]{2,1,0:T(8,128)(2,1)S(1)} %get-tuple-element.21), channel_id=1, source_target_pairs={{0,4},{1,5},{2,6},{3,7},{16,20},{17,21},{18,22},{19,23}} | collective-permute-start | bytes 1572872 | tf_op jit(solution)/shard_map/ppermute | solution.py:62
  249.2 13.3 %collective-permute-start.25 = (bf16[8,128,256]{2,1,0:T(8,128)(2,1)S(1)}, bf16[8,128,256]{2,1,0:T(8,128)(2,1)S(1)}, u32[]{:S(2)}, u32[]{:S(2)}) collective-permute-start(bf16[8,128,256]{2,1,0:T(8,128)(2,1)S(1)} %get-tuple-element.22), channel_id=1, source_target_pairs={{12,8},{13,9},{14,10},{15,11},{28,24},{29,25},{30,26},{31,27}} | collective-permute-start | bytes 1572872 | tf_op jit(solution)/shard_map/ppermute | solution.py:65
  258.1 11.1 %collective-permute-start.23 = (bf16[8,128,256]{2,1,0:T(8,128)(2,1)S(1)}, bf16[8,128,256]{2,1,0:T(8,128)(2,1)S(1)}, u32[]{:S(2)}, u32[]{:S(2)}) collective-permute-start(bf16[8,128,256]{2,1,0:T(8,128)(2,1)S(1)} %fusion.9), channel_id=1, source_target_pairs={{0,4},{4,8},{1,5},{5,9},{2,6},{6,10},{3,7},{7,11},{16,20},{20,24},... | collective-permute-start | bytes 1572872 | tf_op jit(solution)/shard_map/ppermute | solution.py:62
  270.3 6.5 %collective-permute-start.26 = (bf16[8,128,256]{2,1,0:T(8,128)(2,1)S(1)}, bf16[8,128,256]{2,1,0:T(8,128)(2,1)S(1)}, u32[]{:S(2)}, u32[]{:S(2)}) collective-permute-start(bf16[8,128,256]{2,1,0:T(8,128)(2,1)S(1)} %get-tuple-element.20), channel_id=1, source_target_pairs={{12,8},{8,4},{13,9},{9,5},{14,10},{10,6},{15,11},{11,7},{28,24},{2... | collective-permute-start | bytes 1572872 | tf_op jit(solution)/shard_map/ppermute | solution.py:65
  271.0 36.9 %collective-permute-start.31 = (bf16[4,256,1024]{2,1,0:T(8,128)(2,1)}, bf16[4,256,1024]{2,1,0:T(8,128)(2,1)}, u32[]{:S(2)}, u32[]{:S(2)}) collective-permute-start(bf16[4,256,1024]{2,1,0:T(8,128)(2,1)} %get-tuple-element.16.refs_3_), channel_id=1, source_target_pairs={{0,1},{1,0},{2,3},{3,2},{4,5},{5,4},{6,7},{7,6},{8,9},{9,8},{10,11... | collective-permute-start | bytes 6291464 | tf_op jit(solution)/shard_map/ppermute | solution.py:507
  271.1 17.1 %collective-permute-start.24 = (bf16[8,128,256]{2,1,0:T(8,128)(2,1)}, bf16[8,128,256]{2,1,0:T(8,128)(2,1)}, u32[]{:S(2)}, u32[]{:S(2)}) collective-permute-start(bf16[8,128,256]{2,1,0:T(8,128)(2,1)} %get-tuple-element.19), channel_id=1, source_target_pairs={{0,4},{4,8},{8,12},{1,5},{5,9},{9,13},{2,6},{6,10},{10,14},{3,7},{... | collective-permute-start | bytes 1572872 | tf_op jit(solution)/shard_map/ppermute | solution.py:62
  277.8 16.4 %collective-permute-start.27 = (bf16[8,128,256]{2,1,0:T(8,128)(2,1)}, bf16[8,128,256]{2,1,0:T(8,128)(2,1)}, u32[]{:S(2)}, u32[]{:S(2)}) collective-permute-start(bf16[8,128,256]{2,1,0:T(8,128)(2,1)} %fusion.8), channel_id=1, source_target_pairs={{12,8},{8,4},{4,0},{13,9},{9,5},{5,1},{14,10},{10,6},{6,2},{15,11}... | collective-permute-start | bytes 1572872 | tf_op jit(solution)/shard_map/ppermute | solution.py:65
  279.3 14.9 %copy-start.5 = (f32[8,128,256]{2,1,0:T(8,128)S(1)}, f32[8,128,256]{2,1,0:T(8,128)}, u32[]{:S(2)}) copy-start(f32[8,128,256]{2,1,0:T(8,128)} %copy-done.4) | copy-start | bytes 3145732
  281.8 26.1 %collective-permute-start.30 = (bf16[21,256,128]{2,1,0:T(8,128)(2,1)}, bf16[21,256,128]{2,1,0:T(8,128)(2,1)}, u32[]{:S(2)}, u32[]{:S(2)}) collective-permute-start(bf16[21,256,128]{2,1,0:T(8,128)(2,1)} %fusion), channel_id=1, source_target_pairs={{0,1},{1,0},{2,3},{3,2},{4,5},{5,4},{6,7},{7,6},{8,9},{9,8},{10,11... | collective-permute-start | bytes 4128776 | tf_op jit(solution)/shard_map/ppermute | solution.py:505
  297.8 9.2 %collective-permute-start.28 = (bf16[128,2048]{0,1:T(8,128)(2,1)S(1)}, bf16[128,2048]{0,1:T(8,128)(2,1)S(1)}, u32[]{:S(2)}, u32[]{:S(2)}) collective-permute-start(bf16[128,2048]{0,1:T(8,128)(2,1)S(1)} %bitcast.73), channel_id=1, source_target_pairs={{0,2},{2,0},{1,3},{3,1},{4,6},{6,4},{5,7},{7,5},{8,10},{10,8},{9,1... | collective-permute-start | bytes 1572872 | tf_op jit(solution)/shard_map/ppermute | solution.py:521
  299.3 8.6 %copy-start.2 = (bf16[21,128,256]{2,1,0:T(8,128)(2,1)S(1)}, bf16[21,128,256]{2,1,0:T(8,128)(2,1)}, u32[]{:S(2)}) copy-start(bf16[21,128,256]{2,1,0:T(8,128)(2,1)} %copy-done) | copy-start | bytes 4128772
  307.2 12.6 %collective-permute-start.29 = (bf16[256,1024]{0,1:T(8,128)(2,1)S(1)}, bf16[256,1024]{0,1:T(8,128)(2,1)S(1)}, u32[]{:S(2)}, u32[]{:S(2)}) collective-permute-start(bf16[256,1024]{0,1:T(8,128)(2,1)S(1)} %get-tuple-element.32), channel_id=1, source_target_pairs={{0,1},{1,0},{2,3},{3,2},{4,5},{5,4},{6,7},{7,6},{8,9},{9,8},{10,11... | collective-permute-start | bytes 1572872 | tf_op jit(solution)/shard_map/ppermute | solution.py:536
  307.3 13.2 %collective-permute-start = (bf16[256,1024]{1,0:T(8,128)(2,1)S(1)}, bf16[256,1024]{1,0:T(8,128)(2,1)S(1)}, u32[]{:S(2)}, u32[]{:S(2)}) collective-permute-start(bf16[256,1024]{1,0:T(8,128)(2,1)S(1)} %pad_maximum_fusion.3), channel_id=1, source_target_pairs={{0,1},{1,0},{2,3},{3,2},{4,5},{5,4},{6,7},{7,6},{8,9},{9,8},{10,11... | collective-permute-start | bytes 1572872 | tf_op jit(solution)/shard_map/ppermute | solution.py:534

commit v2 on v0

v2 whole, which is shorter than its diff:
```python
import functools

import jax
import jax.numpy as jnp
from jax import lax
from jax.experimental import pallas as pl
from jax.experimental.pallas import tpu as pltpu
from jax.sharding import PartitionSpec as P

ROOT = 0.7978845608028654
CUBIC = 0.044715
F32 = jnp.float32
BF16 = jnp.bfloat16
VMEM_LIMIT = 24 * 1024 * 1024
CHUNKS = 2


def params():
    return pltpu.CompilerParams(vmem_limit_bytes=VMEM_LIMIT)


def cost(flops, nbytes):
    return pl.CostEstimate(flops=int(flops), bytes_accessed=int(nbytes), transcendentals=0)


def ring_shift(axis, by):
    count = lax.axis_size(axis)
    return [(src, (src + by) % count) for src in range(count)]


def divisor(total, most):
    return max(d for d in range(1, most + 1) if total % d == 0)


def whole(shape):
    return pl.BlockSpec(shape, lambda *_: (0,) * len(shape))


def far_first(count):
    return sorted(range(1, count), key=lambda m: (abs(2 * m - count), m))


VMEM = pl.BlockSpec(memory_space=pltpu.VMEM)
SMEM = pl.BlockSpec(memory_space=pltpu.SMEM)
HBM = pl.BlockSpec(memory_space=pltpu.HBM)


def start_fetch(weight, held, sems, per):
    copies = [
        pltpu.make_async_copy(
            weight.at[pl.ds(at, per)], held.at[pl.ds(at, per)], sems.at[at // per]
        )
        for at in range(0, weight.shape[0], per)
    ]
    for copy in copies:
        copy.start()

    def ready(k):
        if k % per == 0:
            copies[k // per].wait()

    return ready


def in_hbm(array):
    return pltpu.with_memory_space_constraint(array, pltpu.HBM)


def encode_kernel(pieces, scal, acts, weight, *refs):
    outs, tokens, held, token_sems, sems = refs[: len(pieces)], *refs[len(pieces) :]
    blocks, rows, block = outs[0].shape
    layer, w, width = scal[0], scal[1], scal[4]
    reads = []
    for n, m in enumerate(pieces):
        start = pl.multiple_of(lax.rem(w + m, width) * rows, rows)
        reads.append(
            pltpu.make_async_copy(
                acts.at[layer, pl.ds(start, rows)], tokens.at[n], token_sems.at[n]
            )
        )
    cut = held.shape[0] // sems.shape[0]
    loads = [
        pltpu.make_async_copy(
            weight.at[pl.ds(n * cut, cut)], held.at[pl.ds(n * cut, cut)], sems.at[n]
        )
        for n in range(sems.shape[0])
    ]
    for copy in reads + loads:
        copy.start()
    for copy in reads + loads:
        copy.wait()
    for b in range(blocks):
        for n, out in enumerate(outs):
            res = jnp.dot(
                tokens[n], held[:, b * block : (b + 1) * block], preferred_element_type=F32
            )
            out[b] = res.astype(out.dtype)


def encode(acts, weight, scal, pieces, rows, block, dtype):
    d, lat = weight.shape
    blocks = lat // block
    pieces = tuple(pieces)
    return pl.pallas_call(
        functools.partial(encode_kernel, pieces),
        in_specs=[SMEM, HBM, HBM],
        out_specs=[VMEM] * len(pieces),
        out_shape=[jax.ShapeDtypeStruct((blocks, rows, block), dtype)] * len(pieces),
        scratch_shapes=[
            pltpu.VMEM((len(pieces), rows, d), BF16),
            pltpu.VMEM((d, lat), BF16),
            pltpu.SemaphoreType.DMA((len(pieces),)),
            pltpu.SemaphoreType.DMA((4,)),
        ],
        compiler_params=params(),
        cost_estimate=cost(2 * len(pieces) * rows * d * lat, 2 * d * lat),
        name="encode",
    )(scal, in_hbm(acts), in_hbm(weight))


def gate_kernel(count, chunks, own, bias, mask, *refs):
    recv, lats, slopes = refs[:count], refs[count : count + chunks], refs[count + chunks :]
    rows = lats[0].shape[1]
    for b in range(own.shape[0]):
        v = own[b]
        for r in recv:
            v = v + r[b].astype(F32)
        v = v + bias[b]
        keep = mask[b]
        tanh_part = jnp.tanh(ROOT * (v + CUBIC * v * v * v))
        lat = (0.5 * v * (1.0 + tanh_part) * keep).astype(BF16)
        slope = keep * (
            0.5 * (1.0 + tanh_part)
            + 0.5 * v * (1.0 - tanh_part * tanh_part) * ROOT * (1.0 + 3.0 * CUBIC * v * v)
        )
        for c in range(chunks):
            lats[c][b] = lat[c * rows : (c + 1) * rows]
            slopes[c][b] = slope[c * rows : (c + 1) * rows]


def gate(own, recv, bias, mask, chunks):
    blocks, rows, block = own.shape
    shape = (blocks, rows // chunks, block)
    out = pl.pallas_call(
        functools.partial(gate_kernel, len(recv), chunks),
        in_specs=[VMEM] * (3 + len(recv)),
        out_specs=[VMEM] * (2 * chunks),
        out_shape=[jax.ShapeDtypeStruct(shape, BF16)] * chunks
        + [jax.ShapeDtypeStruct(shape, F32)] * chunks,
        compiler_params=params(),
        cost_estimate=cost(20 * own.size, 12 * own.size),
        name="gate",
    )(own, bias, mask, *recv)
    return out[:chunks], out[chunks:]


def pick_kernel(slots, count, meta, *refs):
    bufs, out, sems = refs[:count], refs[count], refs[count + 1]

    def copy(k, q, row):
        return pltpu.make_async_copy(bufs[q].at[row], out.at[k], sems.at[k])

    for k in range(slots):
        for q in range(count):

            @pl.when(meta[k] == q)
            def _():
                copy(k, q, meta[slots + k]).start()

    for k in range(slots):
        copy(k, 0, 0).wait()


def pick(meta, bufs, slots):
    return pl.pallas_call(
        functools.partial(pick_kernel, slots, len(bufs)),
        in_specs=[SMEM] + [HBM] * len(bufs),
        out_specs=HBM,
        out_shape=jax.ShapeDtypeStruct((slots,) + bufs[0].shape[1:], BF16),
        scratch_shapes=[pltpu.SemaphoreType.DMA((slots,))],
        compiler_params=params(),
        cost_estimate=cost(0, 4 * slots * bufs[0][0].size),
        name="pick",
    )(meta, *[in_hbm(b) for b in bufs])


def decode_kernel(slots, per, count, layers, meta, *refs):
    lats, weight, out, acc, held, sems = refs[:count], *refs[count:]
    ready = start_fetch(weight, held, sems, per)
    acc[...] = jnp.zeros_like(acc)
    for k in range(slots):
        ready(k)
        target = meta[4 * slots + k]
        lat = jnp.concatenate([ref[k] for ref in lats], axis=0)
        acc[target] += jnp.dot(lat, held[k], preferred_element_type=F32)
    for t in range(layers):
        out[t] = acc[t].astype(out.dtype)


def decode(meta, lats, weight, layers):
    slots, rows, block = lats[0].shape
    d = weight.shape[2]
    tok = rows * len(lats)
    per = divisor(slots, 4)
    return pl.pallas_call(
        functools.partial(decode_kernel, slots, per, len(lats), layers),
        in_specs=[SMEM] + [VMEM] * len(lats) + [HBM],
        out_specs=VMEM,
        scratch_shapes=[
            pltpu.VMEM((layers + 1, tok, d), F32),
            pltpu.VMEM(weight.shape, BF16),
            pltpu.SemaphoreType.DMA((slots // per,)),
        ],
        out_shape=jax.ShapeDtypeStruct((layers, tok, d), BF16),
        compiler_params=params(),
        cost_estimate=cost(2 * slots * tok * block * d, 2 * (weight.size + slots * tok * block)),
        name="decode",
    )(meta, *lats, in_hbm(weight))


def assemble(error, parts, here):
    layers, tok, _ = error.shape
    lays = len(parts)
    share = layers * tok // lays
    for m, part in enumerate(parts):
        owner = lax.rem(here + lays - m, lays)
        if share >= tok:
            full = share // tok
            for f in range(full):
                error[owner * full + f] = part[f * tok : (f + 1) * tok, :]
        else:
            cuts = tok // share
            start = pl.multiple_of(lax.rem(owner, cuts) * share, share)
            error[owner // cuts, pl.ds(start, share), :] = part[...]


def spread_kernel(slots, per, width, lays, scal, meta, *refs):
    parts, weight, error, total = refs[:lays], *refs[lays : lays + 3]
    sends, held, sems = refs[lays + 3 : -2], refs[-2], refs[-1]
    ready = start_fetch(weight, held, sems, per)
    rows = error.shape[1] // width
    dump = total.shape[0] - 1
    total[...] = jnp.zeros_like(total)
    assemble(error, parts, scal[2])
    for k in range(slots):
        ready(k)
        target = meta[2 * slots + k]
        res = lax.dot_general(
            error[jnp.maximum(target, 0)],
            held[k],
            (((1,), (1,)), ((), ())),
            preferred_element_type=F32,
        )
        total[jnp.where(target >= 0, meta[3 * slots + k], dump)] += res[:rows]
        for m in range(1, width):
            sends[m - 1][k] = res[m * rows : (m + 1) * rows].astype(BF16)


def spread(scal, meta, parts, weight, layers, tok, width, blocks_total):
    slots, block, d = weight.shape
    rows = tok // width
    per = divisor(slots, 4)
    return pl.pallas_call(
        functools.partial(spread_kernel, slots, per, width, len(parts)),
        in_specs=[SMEM, SMEM] + [VMEM] * len(parts) + [HBM],
        out_specs=[VMEM] * (width + 1),
        out_shape=[
            jax.ShapeDtypeStruct((layers, tok, d), BF16),
            jax.ShapeDtypeStruct((blocks_total + 1, rows, block), F32),
        ]
        + [jax.ShapeDtypeStruct((slots, rows, block), BF16)] * (width - 1),
        scratch_shapes=[
            pltpu.VMEM(weight.shape, BF16),
            pltpu.SemaphoreType.DMA((slots // per,)),
        ],
        compiler_params=params(),
        cost_estimate=cost(2 * slots * tok * block * d, 2 * (weight.size + 3 * layers * tok * d)),
        name="spread",
    )(scal, meta, *parts, in_hbm(weight))


def merge_kernel(slots, count, meta, own, *refs):
    recv, out, acc = refs[:count], refs[count], refs[count + 1]
    total = out.shape[0]
    acc[...] = own[...]
    for k in range(slots):
        block = jnp.where(meta[2 * slots + k] >= 0, meta[3 * slots + k], total)
        for r in recv:
            acc[block] += r[k].astype(F32)
    for b in range(total):
        out[b] = acc[b].astype(out.dtype)


def merge(meta, own, recv):
    slots = recv[0].shape[0]
    shape = (own.shape[0] - 1,) + own.shape[1:]
    return pl.pallas_call(
        functools.partial(merge_kernel, slots, len(recv)),
        in_specs=[SMEM] + [VMEM] * (1 + len(recv)),
        out_specs=VMEM,
        scratch_shapes=[pltpu.VMEM(own.shape, F32)],
        out_shape=jax.ShapeDtypeStruct(shape, BF16),
        compiler_params=params(),
        cost_estimate=cost(own.size, 6 * own.size + sum(2 * r.size for r in recv)),
        name="merge",
    )(meta, own, *recv)


def dec_grad_kernel(slots, per, count, many, scal, meta, *refs):
    lats, errs, out, held = refs[:count], refs[count : count + many], refs[-2], refs[-1]
    g = pl.program_id(0)

    @pl.when(g == 0)
    def _():
        at = 0
        for err in errs:
            tok = err.shape[1]
            held[:, at : at + tok, :] = err[...]
            at += tok

    for j in range(per):
        target = meta[2 * slots + g * per + j]
        lat = jnp.concatenate([ref[j] for ref in lats], axis=0)
        lat = jnp.where(target >= 0, lat, jnp.zeros_like(lat))
        out[j] = lax.dot_general(
            lat,
            held[jnp.maximum(target, 0)],
            (((0,), (0,)), ((), ())),
            preferred_element_type=F32,
        )


def dec_grad(scal, meta, pieces, cols, slots):
    lats, errs, specs = [], [], []
    per = divisor(slots, 8)
    for arrays, all_columns, err in pieces:
        errs.append(err)
        for a in arrays:
            lats.append(a)
            specs.append(
                pl.BlockSpec(
                    (per, a.shape[1], cols),
                    (lambda g, s, _: (g, 0, s[3])) if all_columns else (lambda g, s, _: (g, 0, 0)),
                )
            )
    layers, _, d = errs[0].shape
    tok = sum(e.shape[1] for e in errs)
    return pl.pallas_call(
        functools.partial(dec_grad_kernel, slots, per, len(lats), len(errs)),
        grid_spec=pltpu.PrefetchScalarGridSpec(
            num_scalar_prefetch=2,
            grid=(slots // per,),
            in_specs=specs + [whole(e.shape) for e in errs],
            out_specs=pl.BlockSpec((per, cols, d), lambda g, s, _: (g, 0, 0)),
            scratch_shapes=[pltpu.VMEM((layers, tok, d), BF16)],
        ),
        out_shape=jax.ShapeDtypeStruct((slots, cols, d), F32),
        compiler_params=params(),
        cost_estimate=cost(
            2 * slots * tok * cols * d, 4 * slots * cols * d + sum(2 * e.size for e in errs)
        ),
        name="dec_grad",
    )(scal, meta, *lats, *errs)


def enc_grad_kernel(count, acts, *refs):
    grads, out, bias = refs[:count], refs[count], refs[count + 1]
    tokens = jnp.concatenate([g[0] for g in grads], axis=0)
    out[...] = jnp.dot(acts[...], tokens, preferred_element_type=F32)
    bias[0] = jnp.sum(tokens.astype(F32), axis=0, keepdims=True)


def enc_grad(acts_t, grads):
    d, tok = acts_t.shape
    blocks, _, block = grads[0].shape
    out, bias = pl.pallas_call(
        functools.partial(enc_grad_kernel, len(grads)),
        grid=(blocks,),
        in_specs=[whole((d, tok))]
        + [pl.BlockSpec((1, g.shape[1], block), lambda b: (b, 0, 0)) for g in grads],
        out_specs=[
            pl.BlockSpec((d, block), lambda b: (0, b)),
            pl.BlockSpec((1, 1, block), lambda b: (b, 0, 0)),
        ],
        out_shape=[
            jax.ShapeDtypeStruct((d, blocks * block), F32),
            jax.ShapeDtypeStruct((blocks, 1, block), F32),
        ],
        compiler_params=params(),
        cost_estimate=cost(2 * d * tok * blocks * block, 6 * d * blocks * block),
        name="enc_grad",
    )(acts_t, *grads)
    return out, bias.reshape(blocks * block)


def local(acts, targets, enc_weight, enc_bias, gate_mask, dec_list, dec_weight):
    layers, tok_rows, d = acts.shape
    lat_dev = enc_weight.shape[1]
    slots, block, _ = dec_weight.shape
    per_dev = lat_dev // block
    lays, width, reps = lax.axis_size("lay"), lax.axis_size("wid"), lax.axis_size("rep")
    lay, wid, rep = lax.axis_index("lay"), lax.axis_index("wid"), lax.axis_index("rep")
    blocks_total = per_dev * lays
    latents_layer = lat_dev * lays // layers
    blocks_layer = latents_layer // block
    layer_here = lay * lat_dev // latents_layer
    chunks = CHUNKS
    tok = tok_rows // chunks
    piece = tok_rows // width
    rows = piece // chunks
    cols = block // reps
    scale = float(tok_rows * reps) ** (-0.5)

    scal = jnp.stack([layer_here, wid, lay, rep, width]).astype(jnp.int32)
    target_layer = dec_list[:, 1]
    listed = target_layer >= 0
    block_id = jnp.where(listed, dec_list[:, 0] * blocks_layer + dec_list[:, 2], 0)
    meta = jnp.concatenate(
        [
            (lay - block_id // per_dev) % lays,
            block_id % per_dev,
            target_layer,
            block_id,
            jnp.where(listed, target_layer, layers),
        ]
    ).astype(jnp.int32)

    def relative(array, axis):
        return [
            jnp.concatenate(
                [
                    lax.dynamic_slice_in_dim(
                        array, ((wid + m) % width) * piece + c * rows, rows, axis
                    )
                    for m in range(width)
                ],
                axis,
            )
            for c in range(chunks)
        ]

    inputs = lax.dynamic_index_in_dim(acts, layer_here, 0, keepdims=False)
    inputs_rel = jnp.concatenate(relative(inputs, 0), 0)
    targets_rel = relative(targets, 1)
    bias = enc_bias.reshape(per_dev, 1, block)
    keep = lax.dynamic_slice_in_dim(
        gate_mask.astype(F32).T[:, :, None], wid * piece, piece, 1
    )

    acts_all = [inputs_rel] + [
        lax.ppermute(inputs_rel, "rep", ring_shift("rep", -m)) for m in range(1, reps)
    ]
    acts_t = jnp.concatenate(acts_all, 0).T

    def tie(values, *others):
        return list(lax.optimization_barrier((*values, *others))[: len(values)])

    shifts = far_first(lays)

    def to_each(part):
        got = {m: lax.ppermute(part(m), "lay", ring_shift("lay", m)) for m in shifts}
        return [got[m] for m in range(1, lays)]

    away = range(1, width)
    sends = encode(acts, enc_weight, scal, away, piece, block, BF16)
    recvs = [lax.ppermute(s, "wid", ring_shift("wid", m)) for s, m in zip(sends, away)]
    [own] = encode(acts, enc_weight, scal, [0], piece, block, F32)
    *recvs, own, keep = lax.optimization_barrier((*recvs, own, keep))
    latents, slopes = gate(own, recvs, bias, keep, chunks)

    share = layers * tok // lays
    own_targets = [
        lax.dynamic_slice_in_dim(t.reshape(layers * tok, d), lay * share, share, 0)
        for t in targets_rel
    ]

    mine, others, got = [], [], []
    for c in range(chunks):
        [latent] = tie([latents[c]], *got)
        got = to_each(lambda m, latent=latent: latent)
        if c == 0:
            acts_t, *rest = tie([acts_t, *own_targets, *got])
            own_targets, got = rest[:chunks], rest[chunks:]
        mine.append(pick(meta, [latent] + got, slots))
        others.append(
            [lax.ppermute(mine[c], "wid", ring_shift("wid", -m)) for m in range(1, width)]
        )
    lat_pieces = [
        [mine[c]] + tie(others[c], *mine[c + 1 : c + 2]) for c in range(chunks)
    ]
    recons = [
        decode(meta, pieces, dec_weight, layers).reshape(lays, share, d)
        for pieces in lat_pieces
    ]
    theirs_lat = []
    for c in range(chunks):
        whole_lat = jnp.concatenate(lat_pieces[c], 1)
        theirs_lat.append(
            [
                lax.ppermute(
                    lax.dynamic_slice_in_dim(whole_lat, ((rep - m) % reps) * cols, cols, 2),
                    "rep",
                    ring_shift("rep", -m),
                )
                for m in range(1, reps)
            ]
        )

    own_errors, errors = [], []
    for c in range(chunks):

        def addend(m, c=c):
            return lax.dynamic_index_in_dim(recons[c], (lay + m) % lays, 0, keepdims=False)

        got = tie(to_each(addend), *recons[c + 1 : c + 2])
        total = addend(0).astype(F32)
        for g in got:
            total = total + g.astype(F32)
        own_errors.append(((total - own_targets[c].astype(F32)) * scale).astype(BF16))
        errors.append(to_each(lambda m, c=c: own_errors[c]))
    errors = [
        [own_errors[c]] + tie(errors[c], *own_errors[c + 1 : c + 2], *theirs_lat[c])
        for c in range(chunks)
    ]

    part_cols = lat_dev // reps
    part_blocks, part_width = max(part_cols // block, 1), min(part_cols, block)
    grads = [[[] for _ in range(chunks)] for _ in range(reps)]
    lat_groups, dec_out = [], None
    for c in range(chunks):
        error, total, *sends = spread(
            scal, meta, errors[c], dec_weight, layers, tok, width, blocks_total
        )
        recvs = [
            lax.ppermute(s, "wid", ring_shift("wid", m + 1)) for m, s in enumerate(sends)
        ]
        lat_groups.append((lat_pieces[c], True, error))
        for m in range(1, reps):
            lat_groups.append(
                (
                    [theirs_lat[c][m - 1]],
                    False,
                    lax.ppermute(error, "rep", ring_shift("rep", -m)),
                )
            )
        merged = merge(meta, total, recvs).reshape(lays, per_dev, rows, block)

        def addend(m, merged=merged):
            return lax.dynamic_index_in_dim(merged, (lay + m) % lays, 0, keepdims=False)

        got = to_each(addend)
        if c == chunks - 1:
            dec_out, *got = tie([dec_grad(scal, meta, lat_groups, cols, slots), *got])
        latent_error = addend(0).astype(F32)
        for g in got:
            latent_error = latent_error + g.astype(F32)
        pre_grad = (latent_error * slopes[c]).astype(BF16)
        for by_rep in range(reps):
            first = ((rep - by_rep) % reps) * part_cols
            sent = lax.dynamic_slice(
                pre_grad,
                (first // block, 0, first % block),
                (part_blocks, rows, part_width),
            )
            for by_wid in range(width):
                moved = sent
                if by_wid or by_rep:
                    pairs = [
                        (w * reps + r, (w - by_wid) % width * reps + (r - by_rep) % reps)
                        for w in range(width)
                        for r in range(reps)
                    ]
                    moved = lax.ppermute(sent, ("wid", "rep"), pairs)
                grads[by_rep][c].append(moved)
    enc_out, bias_out = enc_grad(acts_t, [g for by in grads for row in by for g in row])
    return enc_out, bias_out, dec_out


def solution(mesh):
    return jax.shard_map(
        local,
        mesh=mesh,
        in_specs=(
            P(None, ("grp", "rep"), "wid"),
            P(None, ("grp", "rep"), "wid"),
            P("wid", "lay"),
            P("lay"),
            P(("grp", "rep"), "lay"),
            P("lay", None),
            P("lay", None, "wid"),
        ),
        out_specs=(
            P(("grp", "wid"), ("lay", "rep")),
            P(("grp", "lay", "rep")),
            P(("grp", "lay"), "rep", "wid"),
        ),
        check_vma=False,
    )
```

time: 589 us -> 260 us (0.44)
  waiting for transfers between devices: 339 us -> 116 us
  blocking collectives: 100 us -> 0 us
  matrix products: 80.7 us -> 0 us
  starting transfers between devices: 0.29 us -> 61.3 us
  Pallas kernels: 0 us -> 51.5 us
  other arithmetic: 21.3 us -> 6.19 us
  between operations: 15.6 us -> 1.13 us
  local copies, waits for them, and re-layouts: 31.6 us -> 23.3 us
    all_gather x2 -> x0, waiting for transfers between devices: 126 us -> none  [the longest x1 80.8 us: local(): lax.all_gather(latent, 'lay', axis=1, tiled=True)]
    psum x2 -> x0, waiting for transfers between devices: 116 us -> none  [the longest x1 76 us: local(): lax.psum(slot_error.astype(jnp.bfloat16), 'wid').astype(jnp.float32)]
    ppermute x0 -> x40, waiting for transfers between devices: none -> 116 us  [the longest x24 86.9 us: to_each(): lax.ppermute(part(m), 'lay', ring_shift('lay', m))]
    all_to_all x1 -> x0, blocking collectives: 97.5 us -> none  [local(): lax.all_to_all(outgoing, 'lay', split_axis=1, concat_axis=1, tiled=True)]
    unnamed x8 -> x0, waiting for transfers between devices: 82.9 us -> none
    dot_general x7 -> x0, matrix products: 80.7 us -> none  [the longest x1 28.4 us: local(): jnp.einsum('kl,ktd->ltd', target_hot, contrib, precision=lax.Precision.HI...]
    ppermute x0 -> x40, starting transfers between devices: none -> 61.3 us  [the longest x24 48 us: to_each(): lax.ppermute(part(m), 'lay', ring_shift('lay', m))]
    pallas_call x0 -> x13, Pallas kernels: none -> 51.5 us  [the longest x2 15.1 us: spread(): pl.pallas_call(functools.partial(spread_kernel, slots, per, width, len(pa...]
  transfers between devices with their start and end apart: 7 -> 40, of which waited for: 6 -> 16; matrix products, arithmetic and copies ran while one was open for 3% -> 7% of each run, Pallas kernels for 0% -> 17%
where the time goes in v2:
time: 260 us; the launch traced here: 259 us
  waiting for transfers between devices  116 us (45%)
  starting transfers between devices  61.3 us (24%)
  Pallas kernels  51.5 us (20%)
  local copies, waits for them, and re-layouts  23.3 us (9%)
  other arithmetic  6.19 us (2%)
    ppermute x24, waiting for transfers between devices, to_each(): lax.ppermute(part(m), 'lay', ring_shift('lay', m))  86.9 us
    ppermute x24, starting transfers between devices, to_each(): lax.ppermute(part(m), 'lay', ring_shift('lay', m))  48 us
    pallas_call x2, Pallas kernels, spread(): pl.pallas_call(functools.partial(spread_kernel, slots, per, width, len(pa...  15.1 us
    ppermute x2, waiting for transfers between devices, local(): lax.ppermute(s, 'wid', ring_shift('wid', m + 1))  11.3 us
    pallas_call x2, Pallas kernels, decode(): pl.pallas_call(functools.partial(decode_kernel, slots, per, len(lats), la...  10.6 us
    unnamed x52, local copies, waits for them, and re-layouts  10.5 us
    pallas_call x1, Pallas kernels, dec_grad(): pl.pallas_call(functools.partial(dec_grad_kernel, slots, per, len(lats),...  9.14 us
    ppermute x6, waiting for transfers between devices, local(): moved = lax.ppermute(sent, ('wid', 'rep'), pairs)  8.04 us
  transfers between devices with their start and end apart: 40, of which 16 were waited for; matrix products, arithmetic and copies ran while one was open for 7% of the time, Pallas kernels for 17%

profile of v2, /device:TPU:0, one launch (start us, length us, event | category | flops | bytes accessed | tf_op | source)
XLA Modules:
  0.0 259.3 jit_solution(11250834346854010359)
XLA Ops:
  0.7 3.5 %encode.2 = bf16[8,128,256]{2,1,0:T(8,128)(2,1)S(1)} custom-call(s32[5]{0:T(128)S(1)} %stack.19.scal, bf16[4,256,1024]{2,1,0:T(8,128)(2,1)} %acts.3, bf16[1024,2048]{1,0:T(8,128)(2,1)} %weight.3), custom_call_target="tpu_custom_call" | custom-call | flops 536870912 | bytes 4194304 | tf_op jit(solution)/shard_map/encode/pallas_call | solution.py:104
  4.3 3.0 %collective-permute-start.1 = (bf16[8,128,256]{2,1,0:T(8,128)(2,1)S(1)}, bf16[8,128,256]{2,1,0:T(8,128)(2,1)S(1)}, u32[]{:S(2)}, u32[]{:S(2)}) collective-permute-start(bf16[8,128,256]{2,1,0:T(8,128)(2,1)S(1)} %encode.2), channel_id=1, source_target_pairs={{0,2},{2,0},{1,3},{3,1},{4,6},{6,4},{5,7},{7,5},{8,10},{10,8},{9,1... | collective-permute-start | bytes 1572872 | tf_op jit(solution)/shard_map/ppermute | solution.py:466
  7.3 1.3 constant_dynamic-slice_fusion.11
  9.3 1.2 pad_maximum_fusion.2
  10.5 2.9 %constant_dynamic-slice_fusion.7 = (bf16[4,64,1024]{2,1,0:T(8,128)(2,1)}, bf16[4,64,1024]{2,1,0:T(8,128)(2,1)}, bf16[4,64,1024]{2,1,0:T(8,128)(2,1)}, bf16[4,64,1024]{2,1,0:T(8,128)(2,1)}) fusion(bf16[4,256,1024]{2,1,0:T(8,128)(2,1)} %param.8, s32[]{:T(128)S(6)} %select_n.209, s32[]{:T(128)S(6)} %select_n.207, s32[]{:T(128)S(6)} %select_n.204, s32[]{:T(128)S(6)} %select_n.211), kind=kLoop, calls=%fused_computation.50 | loop fusion | bytes 4194320 | tf_op jit(solution)/shard_map/dynamic_slice | solution.py:432
  13.4 3.5 %encode.3.own = f32[8,128,256]{2,1,0:T(8,128)S(1)} custom-call(s32[5]{0:T(128)S(1)} %stack.19.scal, bf16[4,256,1024]{2,1,0:T(8,128)(2,1)} %acts.3, bf16[1024,2048]{1,0:T(8,128)(2,1)} %weight.3), custom_call_target="tpu_custom_call" | custom-call | flops 536870912 | bytes 4194304 | tf_op jit(solution)/shard_map/encode/pallas_call | solution.py:104
  16.9 2.3 collective-permute-done.1.refs_0_
  19.4 0.9 gate.1
  20.3 0.8 copy-done.8
  21.1 0.8 copy-done.10
  22.0 3.8 %collective-permute-start.4 = (bf16[8,64,256]{2,1,0:T(8,128)(2,1)S(1)}, bf16[8,64,256]{2,1,0:T(8,128)(2,1)S(1)}, u32[]{:S(2)}, u32[]{:S(2)}) collective-permute-start(bf16[8,64,256]{2,1,0:T(8,128)(2,1)S(1)} %get-tuple-element.45.refs_0_), channel_id=1, source_target_pairs={{0,12},{4,0},{8,4},{12,8},{1,13},{5,1},{9,5},{13,9},{2,14},{6,2},{... | collective-permute-start | bytes 786440 | tf_op jit(solution)/shard_map/ppermute | solution.py:461
  25.8 1.0 collective-permute-start.2
  26.8 2.7 %pad_maximum_fusion = (bf16[4,128,1024]{2,1,0:T(8,128)(2,1)}, bf16[4,128,1024]{2,1,0:T(8,128)(2,1)S(1)}) fusion(bf16[4,64,1024]{2,1,0:T(8,128)(2,1)} %get-tuple-element.84, bf16[4,64,1024]{2,1,0:T(8,128)(2,1)} %get-tuple-element.85, bf16[4,64,1024]{2,1,0:T(8,128)(2,1)} %get-tuple-element.86, bf16[4,64,1024]{2,1,0:T(8,128)(2,1)} %get-tuple-element.83), kind=kLoop, calls=%fused_computation.4 | loop fusion | flops 4194304 | bytes 4194304 | tf_op jit(solution)/shard_map/concatenate | solution.py:430
  29.6 1.7 constant_dynamic-slice_fusion.8
  32.0 4.0 %concatenate.23 = bf16[512,1024]{0,1:T(8,128)(2,1)} concatenate(bf16[64,1024]{0,1:T(8,128)(2,1)S(1)} %bitcast.78, bf16[64,1024]{0,1:T(8,128)(2,1)S(1)} %bitcast.76, bf16[64,1024]{0,1:T(8,128)(2,1)S(1)} %bitcast.74, bf16[64,1024]{0,1:T(8,128)(2,1)S(1)} %bitcast.72, bf16[256,1024]{0,1:T(8,128)(2,1)} %collective-permute-done), dimensions={0} | concatenate | bytes 2097152 | tf_op jit(solution)/shard_map/concatenate | solution.py:453
  36.1 11.2 %collective-permute-done.3.refs_2_ = bf16[8,64,256]{2,1,0:T(8,128)(2,1)S(1)} collective-permute-done((bf16[8,64,256]{2,1,0:T(8,128)(2,1)S(1)}, bf16[8,64,256]{2,1,0:T(8,128)(2,1)S(1)}, u32[]{:S(2)}, u32[]{:S(2)}) %collective-permute-start.3) | collective-permute-done | bytes 262176 | tf_op jit(solution)/shard_map/ppermute | solution.py:461
  48.0 1.8 pick.2.refs_0_
  49.8 1.6 collective-permute-start.5
  51.3 2.2 collective-permute-start.7
  53.6 2.0 collective-permute-start.6
  55.6 2.6 %collective-permute-done.8.refs_3_ = bf16[8,64,256]{2,1,0:T(8,128)(2,1)S(1)} collective-permute-done((bf16[8,64,256]{2,1,0:T(8,128)(2,1)S(1)}, bf16[8,64,256]{2,1,0:T(8,128)(2,1)S(1)}, u32[]{:S(2)}, u32[]{:S(2)}) %collective-permute-start.8) | collective-permute-done | bytes 262176 | tf_op jit(solution)/shard_map/ppermute | solution.py:461
  58.2 17.6 %collective-permute-done.7.refs_2_ = bf16[8,64,256]{2,1,0:T(8,128)(2,1)S(1)} collective-permute-done((bf16[8,64,256]{2,1,0:T(8,128)(2,1)S(1)}, bf16[8,64,256]{2,1,0:T(8,128)(2,1)S(1)}, u32[]{:S(2)}, u32[]{:S(2)}) %collective-permute-start.7) | collective-permute-done | bytes 262176 | tf_op jit(solution)/shard_map/ppermute | solution.py:461
  77.2 1.8 pick.3.refs_0_.refs_3_
  79.9 5.3 %decode.2 = bf16[4,128,1024]{2,1,0:T(8,128)(2,1)S(1)} custom-call(s32[105]{0:T(128)S(1)} %concatenate.26.meta, bf16[21,64,256]{2,1,0:T(8,128)(2,1)S(1)} %pick.2.refs_0_, bf16[21,64,256]{2,1,0:T(8,128)(2,1)S(1)} %collective-permute-done.5.refs_1_, bf16[21,256,1024]{2,1,0:T(8,128)(2,1)} %refs_4_.3), custom_call_target="tpu_custom_call" | custom-call | flops 1409286144 | bytes 12386304 | tf_op jit(solution)/shard_map/decode/pallas_call | solution.py:205
  85.4 1.9 collective-permute-start.9
  87.3 7.4 %collective-permute-done.12.refs_1_.refs_4_ = bf16[21,64,256]{2,1,0:T(8,128)(2,1)S(1)} collective-permute-done((bf16[21,64,256]{2,1,0:T(8,128)(2,1)S(1)}, bf16[21,64,256]{2,1,0:T(8,128)(2,1)S(1)}, u32[]{:S(2)}, u32[]{:S(2)}) %collective-permute-start.12) | collective-permute-done | bytes 688160 | tf_op jit(solution)/shard_map/ppermute | solution.py:486
  94.7 5.3 %decode.3 = bf16[4,128,1024]{2,1,0:T(8,128)(2,1)S(1)} custom-call(s32[105]{0:T(128)S(1)} %concatenate.26.meta, bf16[21,64,256]{2,1,0:T(8,128)(2,1)S(1)} %pick.3.refs_0_.refs_3_, bf16[21,64,256]{2,1,0:T(8,128)(2,1)S(1)} %collective-permute-done.12.refs_1_.refs_4_, bf16[21,256,1024]{2,1,0:T(8,128)(2,1)} %refs_4_.3), custom_call_target="tpu_custom_call" | custom-call | flops 1409286144 | bytes 12386304 | tf_op jit(solution)/shard_map/decode/pallas_call | solution.py:205
  100.2 0.7 collective-permute-start.17
  101.0 7.9 %collective-permute-done.10 = bf16[128,1024]{1,0:T(8,128)(2,1)S(1)} collective-permute-done((bf16[128,1024]{1,0:T(8,128)(2,1)S(1)}, bf16[128,1024]{1,0:T(8,128)(2,1)S(1)}, u32[]{:S(2)}, u32[]{:S(2)}) %collective-permute-start.10) | collective-permute-done | bytes 262176 | tf_op jit(solution)/shard_map/ppermute | solution.py:461
  109.4 4.9 %collective-permute-done.18 = bf16[128,1024]{1,0:T(8,128)(2,1)S(1)} collective-permute-done((bf16[128,1024]{1,0:T(8,128)(2,1)S(1)}, bf16[128,1024]{1,0:T(8,128)(2,1)S(1)}, u32[]{:S(2)}, u32[]{:S(2)}) %collective-permute-start.18) | collective-permute-done | bytes 262176 | tf_op jit(solution)/shard_map/ppermute | solution.py:461
  114.3 17.1 %collective-permute-done.17 = bf16[128,1024]{1,0:T(8,128)(2,1)S(1)} collective-permute-done((bf16[128,1024]{1,0:T(8,128)(2,1)S(1)}, bf16[128,1024]{1,0:T(8,128)(2,1)S(1)}, u32[]{:S(2)}, u32[]{:S(2)}) %collective-permute-start.17) | collective-permute-done | bytes 262176 | tf_op jit(solution)/shard_map/ppermute | solution.py:461
  131.4 12.5 %collective-permute-start.13 = (bf16[128,1024]{1,0:T(8,128)(2,1)S(1)}, bf16[128,1024]{1,0:T(8,128)(2,1)S(1)}, u32[]{:S(2)}, u32[]{:S(2)}) collective-permute-start(bf16[128,1024]{1,0:T(8,128)(2,1)S(1)} %fusion.19.refs_0_), channel_id=1, source_target_pairs={{0,4},{4,8},{8,12},{12,0},{1,5},{5,9},{9,13},{13,1},{2,6},{6,10},{... | collective-permute-start | bytes 786440 | tf_op jit(solution)/shard_map/ppermute | solution.py:461
  144.2 15.3 %collective-permute-done.14.refs_2_ = bf16[128,1024]{1,0:T(8,128)(2,1)S(1)} collective-permute-done((bf16[128,1024]{1,0:T(8,128)(2,1)S(1)}, bf16[128,1024]{1,0:T(8,128)(2,1)S(1)}, u32[]{:S(2)}, u32[]{:S(2)}) %collective-permute-start.14) | collective-permute-done | bytes 262176 | tf_op jit(solution)/shard_map/ppermute | solution.py:461
  159.5 6.9 %collective-permute-start.25 = (bf16[128,1024]{1,0:T(8,128)(2,1)S(1)}, bf16[128,1024]{1,0:T(8,128)(2,1)S(1)}, u32[]{:S(2)}, u32[]{:S(2)}) collective-permute-start(bf16[128,1024]{1,0:T(8,128)(2,1)S(1)} %fusion.14.refs_0_), channel_id=1, source_target_pairs={{0,4},{4,8},{8,12},{12,0},{1,5},{5,9},{9,13},{13,1},{2,6},{6,10},{... | collective-permute-start | bytes 786440 | tf_op jit(solution)/shard_map/ppermute | solution.py:461
  166.4 7.5 %spread.2 = (bf16[4,128,1024]{2,1,0:T(8,128)(2,1)}, f32[33,64,256]{2,1,0:T(8,128)S(1)}, bf16[21,64,256]{2,1,0:T(8,128)(2,1)S(1)}) custom-call(s32[5]{0:T(128)S(1)} %stack.19.scal, s32[105]{0:T(128)S(1)} %concatenate.26.meta, bf16[128,1024]{1,0:T(8,128)(2,1)S(1)} %fusion.19.refs_0_, bf16[128,1024]{1,0:T(8,128)(2,1)S(1)} %collective-permute-done.13.refs_1_, ...), custom_call_target="tpu_custom_call" | custom-call | flops 1409286144 | bytes 14155776 | tf_op jit(solution)/shard_map/spread/pallas_call | solution.py:263
  173.9 1.6 collective-permute-start.20
  176.2 0.9 copy-done.4
  177.1 7.5 %spread.3 = (bf16[4,128,1024]{2,1,0:T(8,128)(2,1)}, f32[33,64,256]{2,1,0:T(8,128)S(1)}, bf16[21,64,256]{2,1,0:T(8,128)(2,1)S(1)}) custom-call(s32[5]{0:T(128)S(1)} %stack.19.scal, s32[105]{0:T(128)S(1)} %concatenate.26.meta, bf16[128,1024]{1,0:T(8,128)(2,1)S(1)} %fusion.14.refs_0_, bf16[128,1024]{1,0:T(8,128)(2,1)S(1)} %collective-permute-done.25.refs_1_, ...), custom_call_target="tpu_custom_call" | custom-call | flops 1409286144 | bytes 14155776 | tf_op jit(solution)/shard_map/spread/pallas_call | solution.py:263
  184.6 1.3 copy-done.1
  186.0 1.5 collective-permute-start.29
  188.0 4.4 %collective-permute-done.20.refs_0_ = bf16[21,64,256]{2,1,0:T(8,128)(2,1)S(1)} collective-permute-done((bf16[21,64,256]{2,1,0:T(8,128)(2,1)S(1)}, bf16[21,64,256]{2,1,0:T(8,128)(2,1)S(1)}, u32[]{:S(2)}, u32[]{:S(2)}) %collective-permute-start.20) | collective-permute-done | bytes 688160 | tf_op jit(solution)/shard_map/ppermute | solution.py:535
  192.3 0.9 merge.2
  193.3 1.0 copy-done
  194.3 0.9 dynamic-slice_bitcast_fusion.5
  195.2 2.5 collective-permute-start.21
  197.6 1.3 collective-permute-start.23
  199.0 6.9 %collective-permute-done.29.refs_0_ = bf16[21,64,256]{2,1,0:T(8,128)(2,1)S(1)} collective-permute-done((bf16[21,64,256]{2,1,0:T(8,128)(2,1)S(1)}, bf16[21,64,256]{2,1,0:T(8,128)(2,1)S(1)}, u32[]{:S(2)}, u32[]{:S(2)}) %collective-permute-start.29) | collective-permute-done | bytes 688160 | tf_op jit(solution)/shard_map/ppermute | solution.py:535
  205.9 0.8 copy-done.6
  206.7 2.2 collective-permute-start.22
  208.9 1.6 copy-done.2
  210.5 1.1 copy-done.7
  211.6 0.9 merge.3
  212.7 2.7 %collective-permute-start.34 = (bf16[8,64,256]{2,1,0:T(8,128)(2,1)S(1)}, bf16[8,64,256]{2,1,0:T(8,128)(2,1)S(1)}, u32[]{:S(2)}, u32[]{:S(2)}) collective-permute-start(bf16[8,64,256]{2,1,0:T(8,128)(2,1)S(1)} %get-tuple-element.91), channel_id=1, source_target_pairs={{0,12},{4,0},{8,4},{12,8},{1,13},{5,1},{9,5},{13,9},{2,14},{6,2},{... | collective-permute-start | bytes 786440 | tf_op jit(solution)/shard_map/ppermute | solution.py:461
  215.4 9.4 %collective-permute-done.22 = bf16[8,64,256]{2,1,0:T(8,128)(2,1)} collective-permute-done((bf16[8,64,256]{2,1,0:T(8,128)(2,1)}, bf16[8,64,256]{2,1,0:T(8,128)(2,1)}, u32[]{:S(2)}, u32[]{:S(2)}) %collective-permute-start.22) | collective-permute-done | bytes 262176 | tf_op jit(solution)/shard_map/ppermute | solution.py:461
  224.8 7.9 %collective-permute-start.32 = (bf16[8,64,256]{2,1,0:T(8,128)(2,1)S(1)}, bf16[8,64,256]{2,1,0:T(8,128)(2,1)S(1)}, u32[]{:S(2)}, u32[]{:S(2)}) collective-permute-start(bf16[8,64,256]{2,1,0:T(8,128)(2,1)S(1)} %get-tuple-element.93), channel_id=1, source_target_pairs={{0,4},{4,8},{8,12},{12,0},{1,5},{5,9},{9,13},{13,1},{2,6},{6,10},{... | collective-permute-start | bytes 786440 | tf_op jit(solution)/shard_map/ppermute | solution.py:461
  232.7 1.4 fusion.9
  234.2 1.6 collective-permute-start.36
  235.8 9.1 %dec_grad.1 = f32[21,128,1024]{2,1,0:T(8,128)} custom-call(s32[5]{0:T(128)S(1)} %stack.19.scal, s32[105]{0:T(128)S(1)} %concatenate.26.meta, bf16[21,64,256]{2,1,0:T(8,128)(2,1)S(1)} %pick.2.refs_0_, bf16[21,64,256]{2,1,0:T(8,128)(2,1)S(1)} %collective-permute-done.5.refs_1_, bf16[21,128,128]{2,1,0:T(8,128)(2,1)S(1)} %collective-permute-done.19.refs_2_, ...), custom_call_target="tpu_custom_call" | custom-call | flops 2818572288 | bytes 15204352 | tf_op jit(solution)/shard_map/dec_grad/pallas_call | solution.py:348
  245.8 0.9 collective-permute-start.39
  246.7 0.8 collective-permute-start.38
  248.0 3.4 %collective-permute-done.24.refs_1_ = bf16[4,64,256]{2,1,0:T(8,128)(2,1)S(1)} collective-permute-done((bf16[4,64,256]{2,1,0:T(8,128)(2,1)S(1)}, bf16[4,64,256]{2,1,0:T(8,128)(2,1)S(1)}, u32[]{:S(2)}, u32[]{:S(2)}) %collective-permute-start.24) | collective-permute-done | bytes 131104 | tf_op jit(solution)/shard_map/ppermute | solution.py:573
  251.4 0.9 collective-permute-done.39.refs_7_
  252.3 3.8 %collective-permute-done.35.refs_3_ = bf16[4,64,256]{2,1,0:T(8,128)(2,1)S(1)} collective-permute-done((bf16[4,64,256]{2,1,0:T(8,128)(2,1)S(1)}, bf16[4,64,256]{2,1,0:T(8,128)(2,1)S(1)}, u32[]{:S(2)}, u32[]{:S(2)}) %collective-permute-start.35) | collective-permute-done | bytes 131104 | tf_op jit(solution)/shard_map/ppermute | solution.py:573
  256.0 3.3 %enc_grad.1 = (f32[1024,1024]{1,0:T(8,128)}, f32[4,1,256]{2,1,0:T(1,128)}) custom-call(bf16[1024,512]{1,0:T(8,128)(2,1)S(1)} %bitcast.69, bf16[4,64,256]{2,1,0:T(8,128)(2,1)S(1)} %get-tuple-element.106.refs_0_, bf16[4,64,256]{2,1,0:T(8,128)(2,1)S(1)} %collective-permute-done.24.refs_1_, bf16[4,64,256]{2,1,0:T(8,128)(2,1)S(1)} %get-tuple-element.104.refs_2_, ...), custom_call_target="tpu_custom_call" | custom-call | flops 1073741824 | bytes 6291456 | tf_op jit(solution)/shard_map/enc_grad/pallas_call | solution.py:376
  (111 shorter events, 8.6 us)
Async XLA Ops:
  4.3 14.9 %collective-permute-start.1 = (bf16[8,128,256]{2,1,0:T(8,128)(2,1)S(1)}, bf16[8,128,256]{2,1,0:T(8,128)(2,1)S(1)}, u32[]{:S(2)}, u32[]{:S(2)}) collective-permute-start(bf16[8,128,256]{2,1,0:T(8,128)(2,1)S(1)} %encode.2), channel_id=1, source_target_pairs={{0,2},{2,0},{1,3},{3,1},{4,6},{6,4},{5,7},{7,5},{8,10},{10,8},{9,1... | collective-permute-start | bytes 1572872 | tf_op jit(solution)/shard_map/ppermute | solution.py:466
  7.3 3.2 %copy-start.25 = (s32[21,3]{0,1:T(4,128)S(1)}, s32[21,3]{0,1:T(4,128)}, u32[]{:S(2)}) copy-start(s32[21,3]{0,1:T(4,128)} %param.12) | copy-start | bytes 760
  9.3 4.1 %copy-start.15 = (bf16[1,64,1024]{1,2,0:T(8,128)(2,1)}, bf16[1,64,1024]{1,2,0:T(8,128)(2,1)S(1)}, u32[]{:S(2)}) copy-start(bf16[1,64,1024]{1,2,0:T(8,128)(2,1)S(1)} %copy.14) | copy-start | bytes 393220
  10.4 21.6 %collective-permute-start = (bf16[256,1024]{0,1:T(8,128)(2,1)}, bf16[256,1024]{0,1:T(8,128)(2,1)}, u32[]{:S(2)}, u32[]{:S(2)}) collective-permute-start(bf16[256,1024]{0,1:T(8,128)(2,1)} %pad_maximum_fusion.2), channel_id=1, source_target_pairs={{0,1},{1,0},{2,3},{3,2},{4,5},{5,4},{6,7},{7,6},{8,9},{9,8},{10,11... | collective-permute-start | bytes 1572872 | tf_op jit(solution)/shard_map/ppermute | solution.py:451
  13.3 3.6 %copy-start.24 = (s32[256,8]{0,1:T(8,128)S(1)}, s32[256,8]{0,1:T(8,128)}, u32[]{:S(2)}) copy-start(s32[256,8]{0,1:T(8,128)} %param.11) | copy-start | bytes 24580
  13.4 6.1 %copy-start.14 = (f32[2048]{0:T(1024)S(1)}, f32[2048]{0:T(1024)}, u32[]{:S(2)}) copy-start(f32[2048]{0:T(1024)} %param.10) | copy-start | bytes 24580
  20.3 0.8 copy-start.8
  21.1 0.8 copy-start.10
  22.0 7.6 %copy-start.13 = (bf16[8,64,256]{2,1,0:T(8,128)(2,1)}, bf16[8,64,256]{2,1,0:T(8,128)(2,1)S(1)}, u32[]{:S(2)}) copy-start(bf16[8,64,256]{2,1,0:T(8,128)(2,1)S(1)} %get-tuple-element.45.refs_0_) | copy-start | bytes 786436
  22.0 31.6 %copy-start.12 = (bf16[8,64,256]{2,1,0:T(8,128)(2,1)}, bf16[8,64,256]{2,1,0:T(8,128)(2,1)S(1)}, u32[]{:S(2)}) copy-start(bf16[8,64,256]{2,1,0:T(8,128)(2,1)S(1)} %get-tuple-element.51.refs_0_) | copy-start | bytes 786436
  22.0 14.1 %collective-permute-start.4 = (bf16[8,64,256]{2,1,0:T(8,128)(2,1)S(1)}, bf16[8,64,256]{2,1,0:T(8,128)(2,1)S(1)}, u32[]{:S(2)}, u32[]{:S(2)}) collective-permute-start(bf16[8,64,256]{2,1,0:T(8,128)(2,1)S(1)} %get-tuple-element.45.refs_0_), channel_id=1, source_target_pairs={{0,12},{4,0},{8,4},{12,8},{1,13},{5,1},{9,5},{13,9},{2,14},{6,2},{... | collective-permute-start | bytes 786440 | tf_op jit(solution)/shard_map/ppermute | solution.py:461
  25.8 21.4 %collective-permute-start.3 = (bf16[8,64,256]{2,1,0:T(8,128)(2,1)S(1)}, bf16[8,64,256]{2,1,0:T(8,128)(2,1)S(1)}, u32[]{:S(2)}, u32[]{:S(2)}) collective-permute-start(bf16[8,64,256]{2,1,0:T(8,128)(2,1)S(1)} %get-tuple-element.45.refs_0_), channel_id=1, source_target_pairs={{0,8},{4,12},{8,0},{12,4},{1,9},{5,13},{9,1},{13,5},{2,10},{6,14},... | collective-permute-start | bytes 786440 | tf_op jit(solution)/shard_map/ppermute | solution.py:461
  25.8 21.4 %collective-permute-start.2 = (bf16[8,64,256]{2,1,0:T(8,128)(2,1)S(1)}, bf16[8,64,256]{2,1,0:T(8,128)(2,1)}, u32[]{:S(2)}, u32[]{:S(2)}) collective-permute-start(bf16[8,64,256]{2,1,0:T(8,128)(2,1)S(1)} %get-tuple-element.45.refs_0_), channel_id=1, source_target_pairs={{0,4},{4,8},{8,12},{12,0},{1,5},{5,9},{9,13},{13,1},{2,6},{6,10},{... | collective-permute-start | bytes 786440 | tf_op jit(solution)/shard_map/ppermute | solution.py:461
  26.8 5.2 %copy-start.16 = (bf16[1,64,1024]{1,2,0:T(8,128)(2,1)S(1)}, bf16[1,64,1024]{1,2,0:T(8,128)(2,1)}, u32[]{:S(2)}) copy-start(bf16[1,64,1024]{1,2,0:T(8,128)(2,1)} %copy-done.15) | copy-start | bytes 393220
  36.1 11.2 %copy-start.19 = (bf16[8,64,256]{2,1,0:T(8,128)(2,1)}, bf16[8,64,256]{2,1,0:T(8,128)(2,1)S(1)}, u32[]{:S(2)}) copy-start(bf16[8,64,256]{2,1,0:T(8,128)(2,1)S(1)} %collective-permute-done.4.refs_3_) | copy-start | bytes 786436
  47.3 0.7 copy-start.20
  49.8 29.9 %collective-permute-start.5 = (bf16[21,64,256]{2,1,0:T(8,128)(2,1)S(1)}, bf16[21,64,256]{2,1,0:T(8,128)(2,1)S(1)}, u32[]{:S(2)}, u32[]{:S(2)}) collective-permute-start(bf16[21,64,256]{2,1,0:T(8,128)(2,1)S(1)} %pick.2.refs_0_), channel_id=1, source_target_pairs={{0,2},{2,0},{1,3},{3,1},{4,6},{6,4},{5,7},{7,5},{8,10},{10,8},{9,1... | collective-permute-start | bytes 2064392 | tf_op jit(solution)/shard_map/ppermute | solution.py:486
  51.3 6.9 %collective-permute-start.8 = (bf16[8,64,256]{2,1,0:T(8,128)(2,1)S(1)}, bf16[8,64,256]{2,1,0:T(8,128)(2,1)S(1)}, u32[]{:S(2)}, u32[]{:S(2)}) collective-permute-start(bf16[8,64,256]{2,1,0:T(8,128)(2,1)S(1)} %get-tuple-element.51.refs_0_), channel_id=1, source_target_pairs={{0,12},{4,0},{8,4},{12,8},{1,13},{5,1},{9,5},{13,9},{2,14},{6,2},{... | collective-permute-start | bytes 786440 | tf_op jit(solution)/shard_map/ppermute | solution.py:461
  51.3 24.5 %collective-permute-start.7 = (bf16[8,64,256]{2,1,0:T(8,128)(2,1)S(1)}, bf16[8,64,256]{2,1,0:T(8,128)(2,1)S(1)}, u32[]{:S(2)}, u32[]{:S(2)}) collective-permute-start(bf16[8,64,256]{2,1,0:T(8,128)(2,1)S(1)} %get-tuple-element.51.refs_0_), channel_id=1, source_target_pairs={{0,8},{4,12},{8,0},{12,4},{1,9},{5,13},{9,1},{13,5},{2,10},{6,14},... | collective-permute-start | bytes 786440 | tf_op jit(solution)/shard_map/ppermute | solution.py:461
  53.6 22.3 %collective-permute-start.6 = (bf16[8,64,256]{2,1,0:T(8,128)(2,1)S(1)}, bf16[8,64,256]{2,1,0:T(8,128)(2,1)S(1)}, u32[]{:S(2)}, u32[]{:S(2)}) collective-permute-start(bf16[8,64,256]{2,1,0:T(8,128)(2,1)S(1)} %get-tuple-element.51.refs_0_), channel_id=1, source_target_pairs={{0,4},{4,8},{8,12},{12,0},{1,5},{5,9},{9,13},{13,1},{2,6},{6,10},{... | collective-permute-start | bytes 786440 | tf_op jit(solution)/shard_map/ppermute | solution.py:461
  58.2 17.6 %copy-start.21 = (bf16[8,64,256]{2,1,0:T(8,128)(2,1)}, bf16[8,64,256]{2,1,0:T(8,128)(2,1)S(1)}, u32[]{:S(2)}) copy-start(bf16[8,64,256]{2,1,0:T(8,128)(2,1)S(1)} %collective-permute-done.8.refs_3_) | copy-start | bytes 786436
  79.0 15.7 %collective-permute-start.12 = (bf16[21,64,256]{2,1,0:T(8,128)(2,1)S(1)}, bf16[21,64,256]{2,1,0:T(8,128)(2,1)S(1)}, u32[]{:S(2)}, u32[]{:S(2)}) collective-permute-start(bf16[21,64,256]{2,1,0:T(8,128)(2,1)S(1)} %pick.3.refs_0_.refs_3_), channel_id=1, source_target_pairs={{0,2},{2,0},{1,3},{3,1},{4,6},{6,4},{5,7},{7,5},{8,10},{10,8},{9,1... | collective-permute-start | bytes 2064392 | tf_op jit(solution)/shard_map/ppermute | solution.py:486
  79.8 86.7 %collective-permute-start.19 = (bf16[21,128,128]{2,1,0:T(8,128)(2,1)S(1)}, bf16[21,128,128]{2,1,0:T(8,128)(2,1)S(1)}, u32[]{:S(2)}, u32[]{:S(2)}) collective-permute-start(bf16[21,128,128]{2,1,0:T(8,128)(2,1)S(1)} %fusion.1), channel_id=1, source_target_pairs={{0,1},{1,0},{2,3},{3,2},{4,5},{5,4},{6,7},{7,6},{8,9},{9,8},{10,11... | collective-permute-start | bytes 2064392 | tf_op jit(solution)/shard_map/ppermute | solution.py:500
  85.2 15.0 %collective-permute-start.11 = (bf16[128,1024]{1,0:T(8,128)(2,1)S(1)}, bf16[128,1024]{1,0:T(8,128)(2,1)S(1)}, u32[]{:S(2)}, u32[]{:S(2)}) collective-permute-start(bf16[128,1024]{1,0:T(8,128)(2,1)S(1)} %get-tuple-element.100), channel_id=1, source_target_pairs={{0,12},{4,0},{8,4},{12,8},{1,13},{5,1},{9,5},{13,9},{2,14},{6,2},{... | collective-permute-start | bytes 786440 | tf_op jit(solution)/shard_map/ppermute | solution.py:461
  85.3 23.6 %collective-permute-start.10 = (bf16[128,1024]{1,0:T(8,128)(2,1)S(1)}, bf16[128,1024]{1,0:T(8,128)(2,1)S(1)}, u32[]{:S(2)}, u32[]{:S(2)}) collective-permute-start(bf16[128,1024]{1,0:T(8,128)(2,1)S(1)} %get-tuple-element.101), channel_id=1, source_target_pairs={{0,8},{4,12},{8,0},{12,4},{1,9},{5,13},{9,1},{13,5},{2,10},{6,14},... | collective-permute-start | bytes 786440 | tf_op jit(solution)/shard_map/ppermute | solution.py:461
  85.4 23.6 %collective-permute-start.9 = (bf16[128,1024]{1,0:T(8,128)(2,1)S(1)}, bf16[128,1024]{1,0:T(8,128)(2,1)S(1)}, u32[]{:S(2)}, u32[]{:S(2)}) collective-permute-start(bf16[128,1024]{1,0:T(8,128)(2,1)S(1)} %get-tuple-element.102), channel_id=1, source_target_pairs={{0,4},{4,8},{8,12},{12,0},{1,5},{5,9},{9,13},{13,1},{2,6},{6,10},{... | collective-permute-start | bytes 786440 | tf_op jit(solution)/shard_map/ppermute | solution.py:461
  100.0 9.1 %copy-start.18 = (bf16[128,1024]{1,0:T(8,128)(2,1)S(1)}, bf16[128,1024]{1,0:T(8,128)(2,1)}, u32[]{:S(2)}) copy-start(bf16[128,1024]{1,0:T(8,128)(2,1)} %constant_dynamic-slice_fusion.8) | copy-start | bytes 786436
  100.1 43.8 %copy-start.17 = (bf16[128,1024]{1,0:T(8,128)(2,1)S(1)}, bf16[128,1024]{1,0:T(8,128)(2,1)}, u32[]{:S(2)}) copy-start(bf16[128,1024]{1,0:T(8,128)(2,1)} %constant_dynamic-slice_fusion.5) | copy-start | bytes 786436
  100.1 14.1 %collective-permute-start.18 = (bf16[128,1024]{1,0:T(8,128)(2,1)S(1)}, bf16[128,1024]{1,0:T(8,128)(2,1)S(1)}, u32[]{:S(2)}, u32[]{:S(2)}) collective-permute-start(bf16[128,1024]{1,0:T(8,128)(2,1)S(1)} %get-tuple-element.97), channel_id=1, source_target_pairs={{0,12},{4,0},{8,4},{12,8},{1,13},{5,1},{9,5},{13,9},{2,14},{6,2},{... | collective-permute-start | bytes 786440 | tf_op jit(solution)/shard_map/ppermute | solution.py:461
  100.2 31.2 %collective-permute-start.17 = (bf16[128,1024]{1,0:T(8,128)(2,1)S(1)}, bf16[128,1024]{1,0:T(8,128)(2,1)S(1)}, u32[]{:S(2)}, u32[]{:S(2)}) collective-permute-start(bf16[128,1024]{1,0:T(8,128)(2,1)S(1)} %get-tuple-element.98), channel_id=1, source_target_pairs={{0,8},{4,12},{8,0},{12,4},{1,9},{5,13},{9,1},{13,5},{2,10},{6,14},... | collective-permute-start | bytes 786440 | tf_op jit(solution)/shard_map/ppermute | solution.py:461
  108.9 22.5 %collective-permute-start.16 = (bf16[128,1024]{1,0:T(8,128)(2,1)S(1)}, bf16[128,1024]{1,0:T(8,128)(2,1)S(1)}, u32[]{:S(2)}, u32[]{:S(2)}) collective-permute-start(bf16[128,1024]{1,0:T(8,128)(2,1)S(1)} %get-tuple-element.99), channel_id=1, source_target_pairs={{0,4},{4,8},{8,12},{12,0},{1,5},{5,9},{9,13},{13,1},{2,6},{6,10},{... | collective-permute-start | bytes 786440 | tf_op jit(solution)/shard_map/ppermute | solution.py:461
  109.0 67.2 %collective-permute-start.28 = (bf16[21,128,128]{2,1,0:T(8,128)(2,1)S(1)}, bf16[21,128,128]{2,1,0:T(8,128)(2,1)S(1)}, u32[]{:S(2)}, u32[]{:S(2)}) collective-permute-start(bf16[21,128,128]{2,1,0:T(8,128)(2,1)S(1)} %fusion), channel_id=1, source_target_pairs={{0,1},{1,0},{2,3},{3,2},{4,5},{5,4},{6,7},{7,6},{8,9},{9,8},{10,11... | collective-permute-start | bytes 2064392 | tf_op jit(solution)/shard_map/ppermute | solution.py:500
  114.3 29.9 %collective-permute-start.15 = (bf16[128,1024]{1,0:T(8,128)(2,1)S(1)}, bf16[128,1024]{1,0:T(8,128)(2,1)S(1)}, u32[]{:S(2)}, u32[]{:S(2)}) collective-permute-start(bf16[128,1024]{1,0:T(8,128)(2,1)S(1)} %fusion.19.refs_0_), channel_id=1, source_target_pairs={{0,12},{4,0},{8,4},{12,8},{1,13},{5,1},{9,5},{13,9},{2,14},{6,2},{... | collective-permute-start | bytes 786440 | tf_op jit(solution)/shard_map/ppermute | solution.py:461
  131.4 28.1 %collective-permute-start.14 = (bf16[128,1024]{1,0:T(8,128)(2,1)S(1)}, bf16[128,1024]{1,0:T(8,128)(2,1)S(1)}, u32[]{:S(2)}, u32[]{:S(2)}) collective-permute-start(bf16[128,1024]{1,0:T(8,128)(2,1)S(1)} %fusion.19.refs_0_), channel_id=1, source_target_pairs={{0,8},{4,12},{8,0},{12,4},{1,9},{5,13},{9,1},{13,5},{2,10},{6,14},... | collective-permute-start | bytes 786440 | tf_op jit(solution)/shard_map/ppermute | solution.py:461
  131.4 28.1 %collective-permute-start.13 = (bf16[128,1024]{1,0:T(8,128)(2,1)S(1)}, bf16[128,1024]{1,0:T(8,128)(2,1)S(1)}, u32[]{:S(2)}, u32[]{:S(2)}) collective-permute-start(bf16[128,1024]{1,0:T(8,128)(2,1)S(1)} %fusion.19.refs_0_), channel_id=1, source_target_pairs={{0,4},{4,8},{8,12},{12,0},{1,5},{5,9},{9,13},{13,1},{2,6},{6,10},{... | collective-permute-start | bytes 786440 | tf_op jit(solution)/shard_map/ppermute | solution.py:461
  144.2 31.4 %collective-permute-start.27 = (bf16[128,1024]{1,0:T(8,128)(2,1)S(1)}, bf16[128,1024]{1,0:T(8,128)(2,1)S(1)}, u32[]{:S(2)}, u32[]{:S(2)}) collective-permute-start(bf16[128,1024]{1,0:T(8,128)(2,1)S(1)} %fusion.14.refs_0_), channel_id=1, source_target_pairs={{0,12},{4,0},{8,4},{12,8},{1,13},{5,1},{9,5},{13,9},{2,14},{6,2},{... | collective-permute-start | bytes 786440 | tf_op jit(solution)/shard_map/ppermute | solution.py:461
  159.5 16.7 %collective-permute-start.26 = (bf16[128,1024]{1,0:T(8,128)(2,1)S(1)}, bf16[128,1024]{1,0:T(8,128)(2,1)S(1)}, u32[]{:S(2)}, u32[]{:S(2)}) collective-permute-start(bf16[128,1024]{1,0:T(8,128)(2,1)S(1)} %fusion.14.refs_0_), channel_id=1, source_target_pairs={{0,8},{4,12},{8,0},{12,4},{1,9},{5,13},{9,1},{13,5},{2,10},{6,14},... | collective-permute-start | bytes 786440 | tf_op jit(solution)/shard_map/ppermute | solution.py:461
  159.5 16.7 %collective-permute-start.25 = (bf16[128,1024]{1,0:T(8,128)(2,1)S(1)}, bf16[128,1024]{1,0:T(8,128)(2,1)S(1)}, u32[]{:S(2)}, u32[]{:S(2)}) collective-permute-start(bf16[128,1024]{1,0:T(8,128)(2,1)S(1)} %fusion.14.refs_0_), channel_id=1, source_target_pairs={{0,4},{4,8},{8,12},{12,0},{1,5},{5,9},{9,13},{13,1},{2,6},{6,10},{... | collective-permute-start | bytes 786440 | tf_op jit(solution)/shard_map/ppermute | solution.py:461
  173.9 18.4 %collective-permute-start.20 = (bf16[21,64,256]{2,1,0:T(8,128)(2,1)S(1)}, bf16[21,64,256]{2,1,0:T(8,128)(2,1)S(1)}, u32[]{:S(2)}, u32[]{:S(2)}) collective-permute-start(bf16[21,64,256]{2,1,0:T(8,128)(2,1)S(1)} %get-tuple-element.65), channel_id=1, source_target_pairs={{0,2},{2,0},{1,3},{3,1},{4,6},{6,4},{5,7},{7,5},{8,10},{10,8},{9,1... | collective-permute-start | bytes 2064392 | tf_op jit(solution)/shard_map/ppermute | solution.py:535
  176.2 0.9 copy-start.4
  184.6 1.3 copy-start.1
  186.0 19.9 %collective-permute-start.29 = (bf16[21,64,256]{2,1,0:T(8,128)(2,1)S(1)}, bf16[21,64,256]{2,1,0:T(8,128)(2,1)S(1)}, u32[]{:S(2)}, u32[]{:S(2)}) collective-permute-start(bf16[21,64,256]{2,1,0:T(8,128)(2,1)S(1)} %get-tuple-element.71), channel_id=1, source_target_pairs={{0,2},{2,0},{1,3},{3,1},{4,6},{6,4},{5,7},{7,5},{8,10},{10,8},{9,1... | collective-permute-start | bytes 2064392 | tf_op jit(solution)/shard_map/ppermute | solution.py:535
  187.5 46.7 %collective-permute-start.30 = (bf16[4,128,1024]{2,1,0:T(8,128)(2,1)}, bf16[4,128,1024]{2,1,0:T(8,128)(2,1)}, u32[]{:S(2)}, u32[]{:S(2)}) collective-permute-start(bf16[4,128,1024]{2,1,0:T(8,128)(2,1)} %get-tuple-element.72.refs_6_), channel_id=1, source_target_pairs={{0,1},{1,0},{2,3},{3,2},{4,5},{5,4},{6,7},{7,6},{8,9},{9,8},{10,11... | collective-permute-start | bytes 3145736 | tf_op jit(solution)/shard_map/ppermute | solution.py:543
  187.5 46.8 %collective-permute-start.31 = (bf16[4,128,1024]{2,1,0:T(8,128)(2,1)}, bf16[4,128,1024]{2,1,0:T(8,128)(2,1)}, u32[]{:S(2)}, u32[]{:S(2)}) collective-permute-start(bf16[4,128,1024]{2,1,0:T(8,128)(2,1)} %get-tuple-element.73.refs_8_), channel_id=1, source_target_pairs={{0,1},{1,0},{2,3},{3,2},{4,5},{5,4},{6,7},{7,6},{8,9},{9,8},{10,11... | collective-permute-start | bytes 3145736 | tf_op jit(solution)/shard_map/ppermute | solution.py:543
  193.3 1.0 copy-start
  195.2 17.5 %collective-permute-start.21 = (bf16[8,64,256]{2,1,0:T(8,128)(2,1)}, bf16[8,64,256]{2,1,0:T(8,128)(2,1)}, u32[]{:S(2)}, u32[]{:S(2)}) collective-permute-start(bf16[8,64,256]{2,1,0:T(8,128)(2,1)} %get-tuple-element.94), channel_id=1, source_target_pairs={{0,4},{4,8},{8,12},{12,0},{1,5},{5,9},{9,13},{13,1},{2,6},{6,10},{... | collective-permute-start | bytes 786440 | tf_op jit(solution)/shard_map/ppermute | solution.py:461
  197.6 17.7 %collective-permute-start.23 = (bf16[8,64,256]{2,1,0:T(8,128)(2,1)}, bf16[8,64,256]{2,1,0:T(8,128)(2,1)}, u32[]{:S(2)}, u32[]{:S(2)}) collective-permute-start(bf16[8,64,256]{2,1,0:T(8,128)(2,1)} %get-tuple-element.95), channel_id=1, source_target_pairs={{0,12},{4,0},{8,4},{12,8},{1,13},{5,1},{9,5},{13,9},{2,14},{6,2},{... | collective-permute-start | bytes 786440 | tf_op jit(solution)/shard_map/ppermute | solution.py:461
  205.9 0.8 copy-start.6
  206.7 18.1 %collective-permute-start.22 = (bf16[8,64,256]{2,1,0:T(8,128)(2,1)}, bf16[8,64,256]{2,1,0:T(8,128)(2,1)}, u32[]{:S(2)}, u32[]{:S(2)}) collective-permute-start(bf16[8,64,256]{2,1,0:T(8,128)(2,1)} %get-tuple-element.96), channel_id=1, source_target_pairs={{0,8},{4,12},{8,0},{12,4},{1,9},{5,13},{9,1},{13,5},{2,10},{6,14},... | collective-permute-start | bytes 786440 | tf_op jit(solution)/shard_map/ppermute | solution.py:461
  208.9 1.6 copy-start.2
  210.5 1.1 copy-start.7
  211.6 21.1 %copy-start.11 = (f32[8,64,256]{2,1,0:T(8,128)S(1)}, f32[8,64,256]{2,1,0:T(8,128)}, u32[]{:S(2)}) copy-start(f32[8,64,256]{2,1,0:T(8,128)} %copy-done.10) | copy-start | bytes 1572868
  212.6 23.3 %copy-start.5 = (bf16[21,128,128]{2,1,0:T(8,128)(2,1)S(1)}, bf16[21,128,128]{2,1,0:T(8,128)(2,1)}, u32[]{:S(2)}) copy-start(bf16[21,128,128]{2,1,0:T(8,128)(2,1)} %copy-done.4) | copy-start | bytes 2064388
  212.7 32.3 %collective-permute-start.34 = (bf16[8,64,256]{2,1,0:T(8,128)(2,1)S(1)}, bf16[8,64,256]{2,1,0:T(8,128)(2,1)S(1)}, u32[]{:S(2)}, u32[]{:S(2)}) collective-permute-start(bf16[8,64,256]{2,1,0:T(8,128)(2,1)S(1)} %get-tuple-element.91), channel_id=1, source_target_pairs={{0,12},{4,0},{8,4},{12,8},{1,13},{5,1},{9,5},{13,9},{2,14},{6,2},{... | collective-permute-start | bytes 786440 | tf_op jit(solution)/shard_map/ppermute | solution.py:461
  215.4 30.2 %collective-permute-start.33 = (bf16[8,64,256]{2,1,0:T(8,128)(2,1)S(1)}, bf16[8,64,256]{2,1,0:T(8,128)(2,1)S(1)}, u32[]{:S(2)}, u32[]{:S(2)}) collective-permute-start(bf16[8,64,256]{2,1,0:T(8,128)(2,1)S(1)} %get-tuple-element.92), channel_id=1, source_target_pairs={{0,8},{4,12},{8,0},{12,4},{1,9},{5,13},{9,1},{13,5},{2,10},{6,14},... | collective-permute-start | bytes 786440 | tf_op jit(solution)/shard_map/ppermute | solution.py:461
  224.8 20.7 %collective-permute-start.32 = (bf16[8,64,256]{2,1,0:T(8,128)(2,1)S(1)}, bf16[8,64,256]{2,1,0:T(8,128)(2,1)S(1)}, u32[]{:S(2)}, u32[]{:S(2)}) collective-permute-start(bf16[8,64,256]{2,1,0:T(8,128)(2,1)S(1)} %get-tuple-element.93), channel_id=1, source_target_pairs={{0,4},{4,8},{8,12},{12,0},{1,5},{5,9},{9,13},{13,1},{2,6},{6,10},{... | collective-permute-start | bytes 786440 | tf_op jit(solution)/shard_map/ppermute | solution.py:461
  234.2 11.4 %copy-start.9 = (f32[8,64,256]{2,1,0:T(8,128)S(1)}, f32[8,64,256]{2,1,0:T(8,128)}, u32[]{:S(2)}) copy-start(f32[8,64,256]{2,1,0:T(8,128)} %copy-done.8) | copy-start | bytes 1572868
  234.2 13.3 %collective-permute-start.37 = (bf16[4,64,256]{2,1,0:T(8,128)(2,1)S(1)}, bf16[4,64,256]{2,1,0:T(8,128)(2,1)S(1)}, u32[]{:S(2)}, u32[]{:S(2)}) collective-permute-start(bf16[4,64,256]{2,1,0:T(8,128)(2,1)S(1)} %get-tuple-element.105), channel_id=1, source_target_pairs={{0,3},{1,2},{2,1},{3,0},{4,7},{5,6},{6,5},{7,4},{8,11},{9,10},{10,... | collective-permute-start | bytes 393224 | tf_op jit(solution)/shard_map/ppermute | solution.py:573
  234.2 13.7 %collective-permute-start.36 = (bf16[4,64,256]{2,1,0:T(8,128)(2,1)S(1)}, bf16[4,64,256]{2,1,0:T(8,128)(2,1)S(1)}, u32[]{:S(2)}, u32[]{:S(2)}) collective-permute-start(bf16[4,64,256]{2,1,0:T(8,128)(2,1)S(1)} %get-tuple-element.105), channel_id=1, source_target_pairs={{0,1},{1,0},{2,3},{3,2},{4,5},{5,4},{6,7},{7,6},{8,9},{9,8},{10,11... | collective-permute-start | bytes 393224 | tf_op jit(solution)/shard_map/ppermute | solution.py:573
  245.0 11.0 %copy-start.3 = (bf16[512,1024]{0,1:T(8,128)(2,1)S(1)}, bf16[512,1024]{0,1:T(8,128)(2,1)}, u32[]{:S(2)}) copy-start(bf16[512,1024]{0,1:T(8,128)(2,1)} %concatenate.23) | copy-start | bytes 3145732
  245.0 6.4 %collective-permute-start.24 = (bf16[4,64,256]{2,1,0:T(8,128)(2,1)S(1)}, bf16[4,64,256]{2,1,0:T(8,128)(2,1)S(1)}, u32[]{:S(2)}, u32[]{:S(2)}) collective-permute-start(bf16[4,64,256]{2,1,0:T(8,128)(2,1)S(1)} %get-tuple-element.106.refs_0_), channel_id=1, source_target_pairs={{0,2},{1,3},{2,0},{3,1},{4,6},{5,7},{6,4},{7,5},{8,10},{9,11},{10,... | collective-permute-start | bytes 393224 | tf_op jit(solution)/shard_map/ppermute | solution.py:573
  245.8 6.5 %collective-permute-start.39 = (bf16[4,64,256]{2,1,0:T(8,128)(2,1)S(1)}, bf16[4,64,256]{2,1,0:T(8,128)(2,1)S(1)}, u32[]{:S(2)}, u32[]{:S(2)}) collective-permute-start(bf16[4,64,256]{2,1,0:T(8,128)(2,1)S(1)} %get-tuple-element.103), channel_id=1, source_target_pairs={{0,3},{1,2},{2,1},{3,0},{4,7},{5,6},{6,5},{7,4},{8,11},{9,10},{10,... | collective-permute-start | bytes 393224 | tf_op jit(solution)/shard_map/ppermute | solution.py:573
  246.7 5.6 %collective-permute-start.38 = (bf16[4,64,256]{2,1,0:T(8,128)(2,1)S(1)}, bf16[4,64,256]{2,1,0:T(8,128)(2,1)S(1)}, u32[]{:S(2)}, u32[]{:S(2)}) collective-permute-start(bf16[4,64,256]{2,1,0:T(8,128)(2,1)S(1)} %get-tuple-element.103), channel_id=1, source_target_pairs={{0,1},{1,0},{2,3},{3,2},{4,5},{5,4},{6,7},{7,6},{8,9},{9,8},{10,11... | collective-permute-start | bytes 393224 | tf_op jit(solution)/shard_map/ppermute | solution.py:573
  247.4 8.6 %collective-permute-start.35 = (bf16[4,64,256]{2,1,0:T(8,128)(2,1)S(1)}, bf16[4,64,256]{2,1,0:T(8,128)(2,1)S(1)}, u32[]{:S(2)}, u32[]{:S(2)}) collective-permute-start(bf16[4,64,256]{2,1,0:T(8,128)(2,1)S(1)} %get-tuple-element.104.refs_2_), channel_id=1, source_target_pairs={{0,2},{1,3},{2,0},{3,1},{4,6},{5,7},{6,4},{7,5},{8,10},{9,11},{10,... | collective-permute-start | bytes 393224 | tf_op jit(solution)/shard_map/ppermute | solution.py:573
  (2 other events, 1.4 us)

commit v3 on v2

--- a/solution.py
+++ b/solution.py
@@ -66,61 +66,67 @@
     return pltpu.with_memory_space_constraint(array, pltpu.HBM)
 
 
-def encode_kernel(pieces, scal, acts, weight, *refs):
-    outs, tokens, held, token_sems, sems = refs[: len(pieces)], *refs[len(pieces) :]
+def encode_kernel(pieces, chunks, scal, acts, weight, *refs):
+    count = len(pieces) * chunks
+    outs, tokens, held, token_sems, sems = refs[:count], *refs[count:]
     blocks, rows, block = outs[0].shape
+    piece = rows * chunks
     layer, w, width = scal[0], scal[1], scal[4]
-    reads = []
+    copies = []
     for n, m in enumerate(pieces):
-        start = pl.multiple_of(lax.rem(w + m, width) * rows, rows)
-        reads.append(
+        start = pl.multiple_of(lax.rem(w + m, width) * piece, piece)
+        copies.append(
             pltpu.make_async_copy(
-                acts.at[layer, pl.ds(start, rows)], tokens.at[n], token_sems.at[n]
+                acts.at[layer, pl.ds(start, piece)], tokens.at[n], token_sems.at[n]
             )
         )
     cut = held.shape[0] // sems.shape[0]
-    loads = [
-        pltpu.make_async_copy(
-            weight.at[pl.ds(n * cut, cut)], held.at[pl.ds(n * cut, cut)], sems.at[n]
-        )
-        for n in range(sems.shape[0])
-    ]
-    for copy in reads + loads:
+    for n in range(sems.shape[0]):
+        copies.append(
+            pltpu.make_async_copy(
+                weight.at[pl.ds(n * cut, cut)], held.at[pl.ds(n * cut, cut)], sems.at[n]
+            )
+        )
+    for copy in copies:
         copy.start()
-    for copy in reads + loads:
+    for copy in copies:
         copy.wait()
     for b in range(blocks):
-        for n, out in enumerate(outs):
+        for n in range(len(pieces)):
             res = jnp.dot(
                 tokens[n], held[:, b * block : (b + 1) * block], preferred_element_type=F32
             )
-            out[b] = res.astype(out.dtype)
-
-
-def encode(acts, weight, scal, pieces, rows, block, dtype):
+            for c in range(chunks):
+                out = outs[n * chunks + c]
+                out[b] = res[c * rows : (c + 1) * rows].astype(out.dtype)
+
+
+def encode(acts, weight, scal, pieces, chunks, piece, block, dtype):
     d, lat = weight.shape
     blocks = lat // block
     pieces = tuple(pieces)
-    return pl.pallas_call(
-        functools.partial(encode_kernel, pieces),
-        in_specs=[SMEM, HBM, HBM],
-        out_specs=[VMEM] * len(pieces),
-        out_shape=[jax.ShapeDtypeStruct((blocks, rows, block), dtype)] * len(pieces),
-        scratch_shapes=[
-            pltpu.VMEM((len(pieces), rows, d), BF16),
-            pltpu.VMEM((d, lat), BF16),
-            pltpu.SemaphoreType.DMA((len(pieces),)),
-            pltpu.SemaphoreType.DMA((4,)),
-        ],
-        compiler_params=params(),
-        cost_estimate=cost(2 * len(pieces) * rows * d * lat, 2 * d * lat),
-        name="encode",
-    )(scal, in_hbm(acts), in_hbm(weight))
-
-
-def gate_kernel(count, chunks, own, bias, mask, *refs):
-    recv, lats, slopes = refs[:count], refs[count : count + chunks], refs[count + chunks :]
-    rows = lats[0].shape[1]
+    shape = (blocks, piece // chunks, block)
+    return list(
+        pl.pallas_call(
+            functools.partial(encode_kernel, pieces, chunks),
+            in_specs=[SMEM, HBM, HBM],
+            out_specs=[VMEM] * (len(pieces) * chunks),
+            out_shape=[jax.ShapeDtypeStruct(shape, dtype)] * (len(pieces) * chunks),
+            scratch_shapes=[
+                pltpu.VMEM((len(pieces), piece, d), BF16),
+                pltpu.VMEM((d, lat), BF16),
+                pltpu.SemaphoreType.DMA((len(pieces),)),
+                pltpu.SemaphoreType.DMA((4,)),
+            ],
+            compiler_params=params(),
+            cost_estimate=cost(2 * len(pieces) * piece * d * lat, 2 * d * lat),
+            name="encode",
+        )(scal, in_hbm(acts), in_hbm(weight))
+    )
+
+
+def gate_kernel(count, own, bias, mask, *refs):
+    recv, (lat, slope) = refs[:count], refs[count:]
     for b in range(own.shape[0]):
         v = own[b]
         for r in recv:
@@ -128,30 +134,26 @@
         v = v + bias[b]
         keep = mask[b]
         tanh_part = jnp.tanh(ROOT * (v + CUBIC * v * v * v))
-        lat = (0.5 * v * (1.0 + tanh_part) * keep).astype(BF16)
-        slope = keep * (
+        lat[b] = (0.5 * v * (1.0 + tanh_part) * keep).astype(BF16)
+        slope[b] = keep * (
             0.5 * (1.0 + tanh_part)
             + 0.5 * v * (1.0 - tanh_part * tanh_part) * ROOT * (1.0 + 3.0 * CUBIC * v * v)
         )
-        for c in range(chunks):
-            lats[c][b] = lat[c * rows : (c + 1) * rows]
-            slopes[c][b] = slope[c * rows : (c + 1) * rows]
-
-
-def gate(own, recv, bias, mask, chunks):
-    blocks, rows, block = own.shape
-    shape = (blocks, rows // chunks, block)
-    out = pl.pallas_call(
-        functools.partial(gate_kernel, len(recv), chunks),
+
+
+def gate(own, recv, bias, mask):
+    return pl.pallas_call(
+        functools.partial(gate_kernel, len(recv)),
         in_specs=[VMEM] * (3 + len(recv)),
-        out_specs=[VMEM] * (2 * chunks),
-        out_shape=[jax.ShapeDtypeStruct(shape, BF16)] * chunks
-        + [jax.ShapeDtypeStruct(shape, F32)] * chunks,
+        out_specs=[VMEM] * 2,
+        out_shape=[
+            jax.ShapeDtypeStruct(own.shape, BF16),
+            jax.ShapeDtypeStruct(own.shape, F32),
+        ],
         compiler_params=params(),
         cost_estimate=cost(20 * own.size, 12 * own.size),
         name="gate",
     )(own, bias, mask, *recv)
-    return out[:chunks], out[chunks:]
 
 
 def pick_kernel(slots, count, meta, *refs):
@@ -439,34 +441,47 @@
             for c in range(chunks)
         ]
 
+    def tie(values, *others):
+        return list(lax.optimization_barrier((*values, *others))[: len(values)])
+
+    shifts = far_first(lays)
+
+    def to_each(parts):
+        got = {m: lax.ppermute(parts[m], "lay", ring_shift("lay", m)) for m in shifts}
+        return [got[m] for m in range(1, lays)]
+
+    def by_shift(array):
+        return [
+            lax.dynamic_index_in_dim(array, (lay + m) % lays, 0, keepdims=False)
+            for m in range(lays)
+        ]
+
+    bias = enc_bias.reshape(per_dev, 1, block)
+    keep = gate_mask.astype(F32).T[:, :, None]
+    keep = [
+        lax.dynamic_slice_in_dim(keep, wid * piece + c * rows, rows, 1) for c in range(chunks)
+    ]
+
+    sends = encode(acts, enc_weight, scal, range(1, width), chunks, piece, block, BF16)
+    recvs = [
+        [
+            lax.ppermute(sends[(m - 1) * chunks + c], "wid", ring_shift("wid", m))
+            for m in range(1, width)
+        ]
+        for c in range(chunks)
+    ]
+    owns = encode(acts, enc_weight, scal, [0], chunks, piece, block, F32)
+    acts, targets, keep[0], owns[0], *recvs[0] = tie(
+        [acts, targets, keep[0], owns[0], *recvs[0]]
+    )
+
     inputs = lax.dynamic_index_in_dim(acts, layer_here, 0, keepdims=False)
     inputs_rel = jnp.concatenate(relative(inputs, 0), 0)
     targets_rel = relative(targets, 1)
-    bias = enc_bias.reshape(per_dev, 1, block)
-    keep = lax.dynamic_slice_in_dim(
-        gate_mask.astype(F32).T[:, :, None], wid * piece, piece, 1
-    )
-
     acts_all = [inputs_rel] + [
         lax.ppermute(inputs_rel, "rep", ring_shift("rep", -m)) for m in range(1, reps)
     ]
     acts_t = jnp.concatenate(acts_all, 0).T
-
-    def tie(values, *others):
-        return list(lax.optimization_barrier((*values, *others))[: len(values)])
-
-    shifts = far_first(lays)
-
-    def to_each(part):
-        got = {m: lax.ppermute(part(m), "lay", ring_shift("lay", m)) for m in shifts}
-        return [got[m] for m in range(1, lays)]
-
-    away = range(1, width)
-    sends = encode(acts, enc_weight, scal, away, piece, block, BF16)
-    recvs = [lax.ppermute(s, "wid", ring_shift("wid", m)) for s, m in zip(sends, away)]
-    [own] = encode(acts, enc_weight, scal, [0], piece, block, F32)
-    *recvs, own, keep = lax.optimization_barrier((*recvs, own, keep))
-    latents, slopes = gate(own, recvs, bias, keep, chunks)
 
     share = layers * tok // lays
     own_targets = [
@@ -474,24 +489,33 @@
         for t in targets_rel
     ]
 
-    mine, others, got = [], [], []
+    slopes, lat_pieces, parts, sums, got = [], [], [], [], []
     for c in range(chunks):
-        [latent] = tie([latents[c]], *got)
-        got = to_each(lambda m, latent=latent: latent)
+        own, *recv = tie([owns[c], *recvs[c]], *got)
+        latent, slope = gate(own, recv, bias, keep[c])
+        slopes.append(slope)
+        got = to_each([latent] * lays)
         if c == 0:
-            acts_t, *rest = tie([acts_t, *own_targets, *got])
-            own_targets, got = rest[:chunks], rest[chunks:]
-        mine.append(pick(meta, [latent] + got, slots))
-        others.append(
-            [lax.ppermute(mine[c], "wid", ring_shift("wid", -m)) for m in range(1, width)]
-        )
-    lat_pieces = [
-        [mine[c]] + tie(others[c], *mine[c + 1 : c + 2]) for c in range(chunks)
-    ]
-    recons = [
-        decode(meta, pieces, dec_weight, layers).reshape(lays, share, d)
-        for pieces in lat_pieces
-    ]
+            late = [r for group in recvs[1:] for r in group]
+            acts_t, *rest = tie([acts_t, *own_targets, *late, *got])
+            own_targets, got = rest[:chunks], rest[chunks + len(late) :]
+            late = rest[chunks : chunks + len(late)]
+            recvs[1:] = [
+                late[n * (width - 1) : (n + 1) * (width - 1)] for n in range(chunks - 1)
+            ]
+        picked = tie(got, *(parts[-1] if parts else ()))
+        mine = pick(meta, [latent] + picked, slots)
+        lat_pieces.append(
+            [mine]
+            + [lax.ppermute(mine, "wid", ring_shift("wid", -m)) for m in range(1, width)]
+        )
+        pieces = lat_pieces[c]
+        if c:
+            tied = tie([*pieces, *sums[-1]])
+            pieces, sums[-1] = tied[:width], tied[width:]
+        recon = decode(meta, pieces, dec_weight, layers).reshape(lays, share, d)
+        parts.append(by_shift(recon))
+        sums.append(to_each(parts[c]))
     theirs_lat = []
     for c in range(chunks):
         whole_lat = jnp.concatenate(lat_pieces[c], 1)
@@ -506,34 +530,33 @@
             ]
         )
 
-    own_errors, errors = [], []
-    for c in range(chunks):
-
-        def addend(m, c=c):
-            return lax.dynamic_index_in_dim(recons[c], (lay + m) % lays, 0, keepdims=False)
-
-        got = tie(to_each(addend), *recons[c + 1 : c + 2])
-        total = addend(0).astype(F32)
-        for g in got:
-            total = total + g.astype(F32)
-        own_errors.append(((total - own_targets[c].astype(F32)) * scale).astype(BF16))
-        errors.append(to_each(lambda m, c=c: own_errors[c]))
-    errors = [
-        [own_errors[c]] + tie(errors[c], *own_errors[c + 1 : c + 2], *theirs_lat[c])
-        for c in range(chunks)
-    ]
-
     part_cols = lat_dev // reps
     part_blocks, part_width = max(part_cols // block, 1), min(part_cols, block)
     grads = [[[] for _ in range(chunks)] for _ in range(reps)]
-    lat_groups, dec_out = [], None
+    lat_groups, spreads, recvs = [], [], []
     for c in range(chunks):
+        arrived = sums[c]
+        if c:
+            *arrived, spreads[-1] = tie([*arrived, spreads[-1]])
+        total = parts[c][0].astype(F32)
+        for g in arrived:
+            total = total + g.astype(F32)
+        own_error = ((total - own_targets[c].astype(F32)) * scale).astype(BF16)
+        arrived = tie(to_each([own_error] * lays), *theirs_lat[c], *(recvs[-1] if c else ()))
         error, total, *sends = spread(
-            scal, meta, errors[c], dec_weight, layers, tok, width, blocks_total
-        )
-        recvs = [
-            lax.ppermute(s, "wid", ring_shift("wid", m + 1)) for m, s in enumerate(sends)
-        ]
+            scal,
+            meta,
+            [own_error] + arrived,
+            dec_weight,
+            layers,
+            tok,
+            width,
+            blocks_total,
+        )
+        spreads.append(total)
+        recvs.append(
+            [lax.ppermute(s, "wid", ring_shift("wid", m + 1)) for m, s in enumerate(sends)]
+        )
         lat_groups.append((lat_pieces[c], True, error))
         for m in range(1, reps):
             lat_groups.append(
@@ -543,25 +566,51 @@
                     lax.ppermute(error, "rep", ring_shift("rep", -m)),
                 )
             )
-        merged = merge(meta, total, recvs).reshape(lays, per_dev, rows, block)
-
-        def addend(m, merged=merged):
-            return lax.dynamic_index_in_dim(merged, (lay + m) % lays, 0, keepdims=False)
-
-        got = to_each(addend)
+    dec_out = dec_grad(scal, meta, lat_groups, cols, slots)
+    dec_out, *recvs[-1] = tie([dec_out, *recvs[-1]])
+    moves = []
+    addends, arrivals = [], []
+    for c in range(chunks):
+        merged = merge(meta, spreads[c], recvs[c]).reshape(lays, per_dev, rows, block)
+        sends = by_shift(merged)
+        if c:
+            many = len(sends)
+            tied = tie([*sends, *arrivals[-1]])
+            sends, arrivals[-1] = tied[:many], tied[many:]
+        addends.append(sends)
+        arrivals.append(to_each(sends))
+    for c in range(chunks):
+        got = arrivals[c]
         if c == chunks - 1:
-            dec_out, *got = tie([dec_grad(scal, meta, lat_groups, cols, slots), *got])
-        latent_error = addend(0).astype(F32)
+            got = tie(got, *moves)
+        latent_error = addends[c][0].astype(F32)
         for g in got:
             latent_error = latent_error + g.astype(F32)
         pre_grad = (latent_error * slopes[c]).astype(BF16)
+
+        def columns(array, by_rep):
+            first = ((rep - by_rep) % reps) * part_cols
+            return lax.dynamic_slice(
+                array,
+                (first // block, 0, first % block),
+                (part_blocks, array.shape[1], part_width),
+            )
+
+        if c < chunks - 1:
+            joined = jnp.concatenate(
+                [pre_grad]
+                + [lax.ppermute(pre_grad, "wid", ring_shift("wid", -m)) for m in range(1, width)],
+                1,
+            )
+            for by_rep in range(reps):
+                moved = columns(joined, by_rep)
+                if by_rep:
+                    moved = lax.ppermute(moved, "rep", ring_shift("rep", -by_rep))
+                grads[by_rep][c].append(moved)
+                moves.append(moved)
+            continue
         for by_rep in range(reps):
-            first = ((rep - by_rep) % reps) * part_cols
-            sent = lax.dynamic_slice(
-                pre_grad,
-                (first // block, 0, first % block),
-                (part_blocks, rows, part_width),
-            )
+            sent = columns(pre_grad, by_rep)
             for by_wid in range(width):
                 moved = sent
                 if by_wid or by_rep:

time: 260 us -> 241 us (0.927)
  starting transfers between devices: 61.3 us -> 39.5 us
  waiting for transfers between devices: 116 us -> 134 us
  local copies, waits for them, and re-layouts: 23.3 us -> 11.2 us
  other arithmetic: 6.19 us -> 2.89 us
    ppermute x27 -> x30, waiting for transfers between devices: 96.5 us -> 124 us  [the longest x24 109 us: to_each(): lax.ppermute(parts[m], 'lay', ring_shift('lay', m))]
    ppermute x27 -> x30, starting transfers between devices: 53.2 us -> 33.9 us  [the longest x24 28 us: to_each(): lax.ppermute(parts[m], 'lay', ring_shift('lay', m))]
    unnamed x52 -> x28, local copies, waits for them, and re-layouts: 10.5 us -> 1.64 us
    ppermute x2, waiting for transfers between devices: 11.3 us -> 3.62 us  [local(): lax.ppermute(s, 'wid', ring_shift('wid', m + 1))]
    ppermute x6 -> x3, waiting for transfers between devices: 8.04 us -> 6.46 us  [local(): moved = lax.ppermute(sent, ('wid', 'rep'), pairs)]
    pallas_call x3 -> x4, Pallas kernels: 7.92 us -> 7.94 us  [the longest x2 7.06 us: encode(): pl.pallas_call(functools.partial(encode_kernel, pieces, chunks), in_specs...]
  transfers between devices with their start and end apart: 40 -> 40, of which waited for: 16 -> 17; matrix products, arithmetic and copies ran while one was open for 7% -> 5% of each run, Pallas kernels for 17% -> 16%
where the time goes in v3:
time: 241 us; the launch traced here: 238 us
  waiting for transfers between devices  134 us (56%)
  Pallas kernels  49 us (20%)
  starting transfers between devices  39.5 us (16%)
  local copies, waits for them, and re-layouts  11.2 us (5%)
  other arithmetic  2.89 us (1%)
    ppermute x24, waiting for transfers between devices, to_each(): lax.ppermute(parts[m], 'lay', ring_shift('lay', m))  109 us
    ppermute x24, starting transfers between devices, to_each(): lax.ppermute(parts[m], 'lay', ring_shift('lay', m))  28 us
    pallas_call x2, Pallas kernels, spread(): pl.pallas_call(functools.partial(spread_kernel, slots, per, width, len(pa...  14.6 us
    pallas_call x2, Pallas kernels, decode(): pl.pallas_call(functools.partial(decode_kernel, slots, per, len(lats), la...  10.6 us
    ppermute x2, waiting for transfers between devices, local(): lax.ppermute(mine, 'wid', ring_shift('wid', -m))  8.05 us
    pallas_call x1, Pallas kernels, dec_grad(): pl.pallas_call(functools.partial(dec_grad_kernel, slots, per, len(lats),...  7.08 us
    pallas_call x2, Pallas kernels, encode(): pl.pallas_call(functools.partial(encode_kernel, pieces, chunks), in_specs...  7.06 us
    ppermute x3, waiting for transfers between devices, local(): moved = lax.ppermute(sent, ('wid', 'rep'), pairs)  6.46 us
  transfers between devices with their start and end apart: 40, of which 17 were waited for; matrix products, arithmetic and copies ran while one was open for 5% of the time, Pallas kernels for 16%

profile of v3, /device:TPU:0, one launch (start us, length us, event | category | flops | bytes accessed | tf_op | source)
XLA Modules:
  0.0 238.1 jit_solution(8128212195515588614)
XLA Ops:
  0.7 3.5 %encode.3 = (bf16[8,64,256]{2,1,0:T(8,128)(2,1)S(1)}, bf16[8,64,256]{2,1,0:T(8,128)(2,1)S(1)}) custom-call(s32[5]{0:T(128)S(1)} %stack.19.scal, bf16[4,256,1024]{2,1,0:T(8,128)(2,1)} %acts.3, bf16[1024,2048]{1,0:T(8,128)(2,1)} %weight.3), custom_call_target="tpu_custom_call" | custom-call | flops 536870912 | bytes 4194304 | tf_op jit(solution)/shard_map/encode/pallas_call | solution.py:110
  4.3 3.0 %collective-permute-start = (bf16[8,64,256]{2,1,0:T(8,128)(2,1)S(1)}, bf16[8,64,256]{2,1,0:T(8,128)(2,1)S(1)}, u32[]{:S(2)}, u32[]{:S(2)}) collective-permute-start(bf16[8,64,256]{2,1,0:T(8,128)(2,1)S(1)} %get-tuple-element.69), channel_id=1, source_target_pairs={{0,2},{2,0},{1,3},{3,1},{4,6},{6,4},{5,7},{7,5},{8,10},{10,8},{9,1... | collective-permute-start | bytes 786440 | tf_op jit(solution)/shard_map/ppermute | solution.py:468
  7.6 3.5 %encode.2 = (f32[8,64,256]{2,1,0:T(8,128)S(1)}, f32[8,64,256]{2,1,0:T(8,128)S(1)}) custom-call(s32[5]{0:T(128)S(1)} %stack.19.scal, bf16[4,256,1024]{2,1,0:T(8,128)(2,1)} %acts.3, bf16[1024,2048]{1,0:T(8,128)(2,1)} %weight.3), custom_call_target="tpu_custom_call" | custom-call | flops 536870912 | bytes 4194304 | tf_op jit(solution)/shard_map/encode/pallas_call | solution.py:110
  11.2 3.2 %collective-permute-done.refs_0_ = bf16[8,64,256]{2,1,0:T(8,128)(2,1)S(1)} collective-permute-done((bf16[8,64,256]{2,1,0:T(8,128)(2,1)S(1)}, bf16[8,64,256]{2,1,0:T(8,128)(2,1)S(1)}, u32[]{:S(2)}, u32[]{:S(2)}) %collective-permute-start) | collective-permute-done | bytes 262176 | tf_op jit(solution)/shard_map/ppermute | solution.py:468
  14.6 0.4 gate.2
  15.0 0.8 copy-done.1
  15.8 4.2 %collective-permute-start.5 = (bf16[8,64,256]{2,1,0:T(8,128)(2,1)S(1)}, bf16[8,64,256]{2,1,0:T(8,128)(2,1)S(1)}, u32[]{:S(2)}, u32[]{:S(2)}) collective-permute-start(bf16[8,64,256]{2,1,0:T(8,128)(2,1)S(1)} %get-tuple-element.78.refs_0_), channel_id=1, source_target_pairs={{0,12},{4,0},{8,4},{12,8},{1,13},{5,1},{9,5},{13,9},{2,14},{6,2},{... | collective-permute-start | bytes 786440 | tf_op jit(solution)/shard_map/ppermute | solution.py:450
  20.0 1.0 collective-permute-start.3
  21.0 1.2 constant_dynamic-slice_fusion.9
  23.0 0.4 pad_maximum_fusion.2
  23.5 1.7 constant_dynamic-slice_fusion.5
  25.4 0.7 constant_dynamic-slice_fusion.6
  26.1 0.7 constant_dynamic-slice_fusion.3
  26.8 2.7 %concatenate.26 = bf16[512,1024]{0,1:T(8,128)(2,1)} concatenate(bf16[64,1024]{0,1:T(8,128)(2,1)S(1)} %bitcast.80, bf16[64,1024]{0,1:T(8,128)(2,1)S(1)} %bitcast.78, bf16[64,1024]{0,1:T(8,128)(2,1)S(1)} %bitcast.76, bf16[64,1024]{0,1:T(8,128)(2,1)S(1)} %bitcast.74, bf16[256,1024]{0,1:T(8,128)(2,1)S(1)} %collective-permute-done.1), dimensions={0} | concatenate | bytes 2097152 | tf_op jit(solution)/shard_map/concatenate | solution.py:484
  29.6 11.2 %collective-permute-done.4.refs_2_ = bf16[8,64,256]{2,1,0:T(8,128)(2,1)} collective-permute-done((bf16[8,64,256]{2,1,0:T(8,128)(2,1)S(1)}, bf16[8,64,256]{2,1,0:T(8,128)(2,1)}, u32[]{:S(2)}, u32[]{:S(2)}) %collective-permute-start.4) | collective-permute-done | bytes 262176 | tf_op jit(solution)/shard_map/ppermute | solution.py:450
  40.8 1.8 pick.2.refs_0_
  42.6 1.6 collective-permute-start.9
  44.3 0.4 gate.3
  44.8 2.5 %collective-permute-start.7 = (bf16[8,64,256]{2,1,0:T(8,128)(2,1)S(1)}, bf16[8,64,256]{2,1,0:T(8,128)(2,1)S(1)}, u32[]{:S(2)}, u32[]{:S(2)}) collective-permute-start(bf16[8,64,256]{2,1,0:T(8,128)(2,1)S(1)} %get-tuple-element.87.refs_0_), channel_id=1, source_target_pairs={{0,8},{4,12},{8,0},{12,4},{1,9},{5,13},{9,1},{13,5},{2,10},{6,14},... | collective-permute-start | bytes 786440 | tf_op jit(solution)/shard_map/ppermute | solution.py:450
  47.3 1.9 collective-permute-start.6
  49.3 8.1 %collective-permute-done.9.refs_1_ = bf16[21,64,256]{2,1,0:T(8,128)(2,1)S(1)} collective-permute-done((bf16[21,64,256]{2,1,0:T(8,128)(2,1)S(1)}, bf16[21,64,256]{2,1,0:T(8,128)(2,1)S(1)}, u32[]{:S(2)}, u32[]{:S(2)}) %collective-permute-start.9) | collective-permute-done | bytes 688160 | tf_op jit(solution)/shard_map/ppermute | solution.py:510
  57.3 5.3 %decode.2 = bf16[4,128,1024]{2,1,0:T(8,128)(2,1)S(1)} custom-call(s32[105]{0:T(128)S(1)} %concatenate.29.meta, bf16[21,64,256]{2,1,0:T(8,128)(2,1)S(1)} %pick.2.refs_0_, bf16[21,64,256]{2,1,0:T(8,128)(2,1)S(1)} %collective-permute-done.9.refs_1_, bf16[21,256,1024]{2,1,0:T(8,128)(2,1)} %refs_4_.3), custom_call_target="tpu_custom_call" | custom-call | flops 1409286144 | bytes 12386304 | tf_op jit(solution)/shard_map/decode/pallas_call | solution.py:207
  62.7 0.9 dynamic-slice_bitcast_fusion.10
  63.6 5.9 %collective-permute-done.7.refs_2_ = bf16[8,64,256]{2,1,0:T(8,128)(2,1)S(1)} collective-permute-done((bf16[8,64,256]{2,1,0:T(8,128)(2,1)S(1)}, bf16[8,64,256]{2,1,0:T(8,128)(2,1)S(1)}, u32[]{:S(2)}, u32[]{:S(2)}) %collective-permute-start.7) | collective-permute-done | bytes 262176 | tf_op jit(solution)/shard_map/ppermute | solution.py:450
  69.5 0.7 copy-done.10
  70.3 1.8 pick.3.refs_0_.refs_3_
  72.1 0.6 collective-permute-start.10
  72.7 2.0 collective-permute-start.11
  75.0 5.4 %collective-permute-done.13 = bf16[128,1024]{1,0:T(8,128)(2,1)} collective-permute-done((bf16[128,1024]{1,0:T(8,128)(2,1)}, bf16[128,1024]{1,0:T(8,128)(2,1)}, u32[]{:S(2)}, u32[]{:S(2)}) %collective-permute-start.13) | collective-permute-done | bytes 262176 | tf_op jit(solution)/shard_map/ppermute | solution.py:450
  80.4 15.1 %collective-permute-done.12 = bf16[128,1024]{1,0:T(8,128)(2,1)} collective-permute-done((bf16[128,1024]{1,0:T(8,128)(2,1)}, bf16[128,1024]{1,0:T(8,128)(2,1)}, u32[]{:S(2)}, u32[]{:S(2)}) %collective-permute-start.12) | collective-permute-done | bytes 262176 | tf_op jit(solution)/shard_map/ppermute | solution.py:450
  95.5 1.4 multiply_convert_fusion.1.refs_0_
  97.0 1.9 collective-permute-start.18
  98.9 1.9 collective-permute-start.17
  101.0 5.3 %decode.3 = bf16[4,128,1024]{2,1,0:T(8,128)(2,1)S(1)} custom-call(s32[105]{0:T(128)S(1)} %concatenate.29.meta, bf16[21,64,256]{2,1,0:T(8,128)(2,1)S(1)} %pick.3.refs_0_.refs_3_, bf16[21,64,256]{2,1,0:T(8,128)(2,1)S(1)} %collective-permute-done.10.refs_1_.refs_4_, bf16[21,256,1024]{2,1,0:T(8,128)(2,1)} %refs_4_.3), custom_call_target="tpu_custom_call" | custom-call | flops 1409286144 | bytes 12386304 | tf_op jit(solution)/shard_map/decode/pallas_call | solution.py:207
  106.4 1.9 collective-permute-start.16
  108.4 14.8 %collective-permute-done.18.refs_2_ = bf16[128,1024]{1,0:T(8,128)(2,1)S(1)} collective-permute-done((bf16[128,1024]{1,0:T(8,128)(2,1)S(1)}, bf16[128,1024]{1,0:T(8,128)(2,1)S(1)}, u32[]{:S(2)}, u32[]{:S(2)}) %collective-permute-start.18) | collective-permute-done | bytes 262176 | tf_op jit(solution)/shard_map/ppermute | solution.py:450
  123.1 7.3 %spread.2 = (bf16[4,128,1024]{2,1,0:T(8,128)(2,1)S(1)}, f32[33,64,256]{2,1,0:T(8,128)S(1)}, bf16[21,64,256]{2,1,0:T(8,128)(2,1)S(1)}) custom-call(s32[5]{0:T(128)S(1)} %stack.19.scal, s32[105]{0:T(128)S(1)} %concatenate.29.meta, bf16[128,1024]{1,0:T(8,128)(2,1)S(1)} %multiply_convert_fusion.1.refs_0_, bf16[128,1024]{1,0:T(8,128)(2,1)S(1)} %collective-permute-done.17.refs_1_, ...), custom_call_target="tpu_custom_call" | custom-call | flops 1409286144 | bytes 14155776 | tf_op jit(solution)/shard_map/spread/pallas_call | solution.py:265
  130.5 1.6 collective-permute-start.21
  132.0 12.6 %collective-permute-done.15 = bf16[128,1024]{1,0:T(8,128)(2,1)S(1)} collective-permute-done((bf16[128,1024]{1,0:T(8,128)(2,1)S(1)}, bf16[128,1024]{1,0:T(8,128)(2,1)S(1)}, u32[]{:S(2)}, u32[]{:S(2)}) %collective-permute-start.15) | collective-permute-done | bytes 262176 | tf_op jit(solution)/shard_map/ppermute | solution.py:450
  144.7 0.2 fusion.6.refs_0_
  145.0 1.9 collective-permute-start.22
  147.0 6.9 %collective-permute-done.24.refs_3_ = bf16[128,1024]{1,0:T(8,128)(2,1)S(1)} collective-permute-done((bf16[128,1024]{1,0:T(8,128)(2,1)S(1)}, bf16[128,1024]{1,0:T(8,128)(2,1)S(1)}, u32[]{:S(2)}, u32[]{:S(2)}) %collective-permute-start.24) | collective-permute-done | bytes 262176 | tf_op jit(solution)/shard_map/ppermute | solution.py:450
  153.9 14.3 %collective-permute-done.23.refs_2_ = bf16[128,1024]{1,0:T(8,128)(2,1)S(1)} collective-permute-done((bf16[128,1024]{1,0:T(8,128)(2,1)S(1)}, bf16[128,1024]{1,0:T(8,128)(2,1)S(1)}, u32[]{:S(2)}, u32[]{:S(2)}) %collective-permute-start.23) | collective-permute-done | bytes 262176 | tf_op jit(solution)/shard_map/ppermute | solution.py:450
  168.3 7.3 %spread.3 = (bf16[4,128,1024]{2,1,0:T(8,128)(2,1)S(1)}, f32[33,64,256]{2,1,0:T(8,128)S(1)}, bf16[21,64,256]{2,1,0:T(8,128)(2,1)S(1)}) custom-call(s32[5]{0:T(128)S(1)} %stack.19.scal, s32[105]{0:T(128)S(1)} %concatenate.29.meta, bf16[128,1024]{1,0:T(8,128)(2,1)S(1)} %fusion.6.refs_0_, bf16[128,1024]{1,0:T(8,128)(2,1)S(1)} %collective-permute-done.22.refs_1_, ...), custom_call_target="tpu_custom_call" | custom-call | flops 1409286144 | bytes 14155776 | tf_op jit(solution)/shard_map/spread/pallas_call | solution.py:265
  175.7 1.6 collective-permute-start.28
  177.2 0.9 merge.2
  178.3 2.5 %collective-permute-start.30 = (bf16[8,64,256]{2,1,0:T(8,128)(2,1)S(1)}, bf16[8,64,256]{2,1,0:T(8,128)(2,1)S(1)}, u32[]{:S(2)}, u32[]{:S(2)}) collective-permute-start(bf16[8,64,256]{2,1,0:T(8,128)(2,1)S(1)} %get-tuple-element.144), channel_id=1, source_target_pairs={{0,8},{4,12},{8,0},{12,4},{1,9},{5,13},{9,1},{13,5},{2,10},{6,14},... | collective-permute-start | bytes 786440 | tf_op jit(solution)/shard_map/ppermute | solution.py:450
  180.9 1.9 collective-permute-start.29
  182.8 7.1 %dec_grad.1 = f32[21,128,1024]{2,1,0:T(8,128)} custom-call(s32[5]{0:T(128)S(1)} %stack.19.scal, s32[105]{0:T(128)S(1)} %concatenate.29.meta, bf16[21,64,256]{2,1,0:T(8,128)(2,1)S(1)} %pick.2.refs_0_, bf16[21,64,256]{2,1,0:T(8,128)(2,1)S(1)} %collective-permute-done.9.refs_1_, bf16[21,128,128]{2,1,0:T(8,128)(2,1)S(1)} %collective-permute-done.20.refs_2_, ...), custom_call_target="tpu_custom_call" | custom-call | flops 2818572288 | bytes 15204352 | tf_op jit(solution)/shard_map/dec_grad/pallas_call | solution.py:350
  189.9 3.6 %collective-permute-done.28.refs_0_ = bf16[21,64,256]{2,1,0:T(8,128)(2,1)S(1)} collective-permute-done((bf16[21,64,256]{2,1,0:T(8,128)(2,1)S(1)}, bf16[21,64,256]{2,1,0:T(8,128)(2,1)S(1)}, u32[]{:S(2)}, u32[]{:S(2)}) %collective-permute-start.28) | collective-permute-done | bytes 688160 | tf_op jit(solution)/shard_map/ppermute | solution.py:558
  193.5 0.9 merge.3
  194.6 9.7 %collective-permute-done.30 = bf16[8,64,256]{2,1,0:T(8,128)(2,1)S(1)} collective-permute-done((bf16[8,64,256]{2,1,0:T(8,128)(2,1)S(1)}, bf16[8,64,256]{2,1,0:T(8,128)(2,1)S(1)}, u32[]{:S(2)}, u32[]{:S(2)}) %collective-permute-start.30) | collective-permute-done | bytes 262176 | tf_op jit(solution)/shard_map/ppermute | solution.py:450
  204.3 0.2 fusion.10
  204.5 0.6 collective-permute-start.32
  205.1 0.5 collective-permute-start.34
  205.6 3.3 %collective-permute-start.35 = (bf16[8,64,256]{2,1,0:T(8,128)(2,1)S(1)}, bf16[8,64,256]{2,1,0:T(8,128)(2,1)S(1)}, u32[]{:S(2)}, u32[]{:S(2)}) collective-permute-start(bf16[8,64,256]{2,1,0:T(8,128)(2,1)S(1)} %get-tuple-element.125), channel_id=1, source_target_pairs={{0,12},{4,0},{8,4},{12,8},{1,13},{5,1},{9,5},{13,9},{2,14},{6,2},{... | collective-permute-start | bytes 786440 | tf_op jit(solution)/shard_map/ppermute | solution.py:450
  208.9 3.5 %collective-permute-done.32 = bf16[8,64,256]{2,1,0:T(8,128)(2,1)S(1)} collective-permute-done((bf16[8,64,256]{2,1,0:T(8,128)(2,1)S(1)}, bf16[8,64,256]{2,1,0:T(8,128)(2,1)S(1)}, u32[]{:S(2)}, u32[]{:S(2)}) %collective-permute-start.32) | collective-permute-done | bytes 262176 | tf_op jit(solution)/shard_map/ppermute | solution.py:602
  212.5 3.7 %collective-permute-done.33 = bf16[8,64,256]{2,1,0:T(8,128)(2,1)S(1)} collective-permute-done((bf16[8,64,256]{2,1,0:T(8,128)(2,1)S(1)}, bf16[8,64,256]{2,1,0:T(8,128)(2,1)S(1)}, u32[]{:S(2)}, u32[]{:S(2)}) %collective-permute-start.33) | collective-permute-done | bytes 262176 | tf_op jit(solution)/shard_map/ppermute | solution.py:450
  216.2 9.7 %collective-permute-done.34 = bf16[8,64,256]{2,1,0:T(8,128)(2,1)S(1)} collective-permute-done((bf16[8,64,256]{2,1,0:T(8,128)(2,1)S(1)}, bf16[8,64,256]{2,1,0:T(8,128)(2,1)S(1)}, u32[]{:S(2)}, u32[]{:S(2)}) %collective-permute-start.34) | collective-permute-done | bytes 262176 | tf_op jit(solution)/shard_map/ppermute | solution.py:450
  226.2 1.6 collective-permute-start.38
  227.8 0.5 collective-permute-start.37
  228.3 3.6 %collective-permute-done.39.refs_5_ = bf16[4,64,256]{2,1,0:T(8,128)(2,1)S(1)} collective-permute-done((bf16[4,64,256]{2,1,0:T(8,128)(2,1)S(1)}, bf16[4,64,256]{2,1,0:T(8,128)(2,1)S(1)}, u32[]{:S(2)}, u32[]{:S(2)}) %collective-permute-start.39) | collective-permute-done | bytes 131104 | tf_op jit(solution)/shard_map/ppermute | solution.py:622
  231.9 2.9 %collective-permute-done.37.refs_2_ = bf16[4,64,256]{2,1,0:T(8,128)(2,1)S(1)} collective-permute-done((bf16[4,64,256]{2,1,0:T(8,128)(2,1)S(1)}, bf16[4,64,256]{2,1,0:T(8,128)(2,1)S(1)}, u32[]{:S(2)}, u32[]{:S(2)}) %collective-permute-start.37) | collective-permute-done | bytes 131104 | tf_op jit(solution)/shard_map/ppermute | solution.py:622
  234.8 3.3 %enc_grad.1 = (f32[1024,1024]{1,0:T(8,128)}, f32[4,1,256]{2,1,0:T(1,128)}) custom-call(bf16[1024,512]{1,0:T(8,128)(2,1)S(1)} %bitcast.70, bf16[4,128,256]{2,1,0:T(8,128)(2,1)S(1)} %get-tuple-element.158.refs_0_, bf16[4,64,256]{2,1,0:T(8,128)(2,1)S(1)} %get-tuple-element.160.refs_1_, bf16[4,64,256]{2,1,0:T(8,128)(2,1)S(1)} %collective-permute-done.37.refs_2_, ...), custom_call_target="tpu_custom_call" | custom-call | flops 1073741824 | bytes 6291456 | tf_op jit(solution)/shard_map/enc_grad/pallas_call | solution.py:378
  (90 shorter events, 3.2 us)
Async XLA Ops:
  0.7 6.6 %copy-start.13 = (s32[21,3]{0,1:T(4,128)S(1)}, s32[21,3]{0,1:T(4,128)}, u32[]{:S(2)}) copy-start(s32[21,3]{0,1:T(4,128)} %param.12) | copy-start | bytes 760
  0.7 6.7 %copy-start.12 = (s32[256,8]{0,1:T(8,128)S(1)}, s32[256,8]{0,1:T(8,128)}, u32[]{:S(2)}) copy-start(s32[256,8]{0,1:T(8,128)} %param.11) | copy-start | bytes 24580
  4.3 10.1 %collective-permute-start = (bf16[8,64,256]{2,1,0:T(8,128)(2,1)S(1)}, bf16[8,64,256]{2,1,0:T(8,128)(2,1)S(1)}, u32[]{:S(2)}, u32[]{:S(2)}) collective-permute-start(bf16[8,64,256]{2,1,0:T(8,128)(2,1)S(1)} %get-tuple-element.69), channel_id=1, source_target_pairs={{0,2},{2,0},{1,3},{3,1},{4,6},{6,4},{5,7},{7,5},{8,10},{10,8},{9,1... | collective-permute-start | bytes 786440 | tf_op jit(solution)/shard_map/ppermute | solution.py:468
  7.3 22.3 %collective-permute-start.2 = (bf16[8,64,256]{2,1,0:T(8,128)(2,1)S(1)}, bf16[8,64,256]{2,1,0:T(8,128)(2,1)S(1)}, u32[]{:S(2)}, u32[]{:S(2)}) collective-permute-start(bf16[8,64,256]{2,1,0:T(8,128)(2,1)S(1)} %get-tuple-element.72), channel_id=1, source_target_pairs={{0,2},{2,0},{1,3},{3,1},{4,6},{6,4},{5,7},{7,5},{8,10},{10,8},{9,1... | collective-permute-start | bytes 786440 | tf_op jit(solution)/shard_map/ppermute | solution.py:468
  7.6 7.0 %copy-start.5 = (f32[2048]{0:T(1024)S(1)}, f32[2048]{0:T(1024)}, u32[]{:S(2)}) copy-start(f32[2048]{0:T(1024)} %param.10) | copy-start | bytes 24580
  15.0 0.8 copy-start.1
  15.8 7.6 %copy-start.3 = (bf16[8,64,256]{2,1,0:T(8,128)(2,1)}, bf16[8,64,256]{2,1,0:T(8,128)(2,1)S(1)}, u32[]{:S(2)}) copy-start(bf16[8,64,256]{2,1,0:T(8,128)(2,1)S(1)} %get-tuple-element.78.refs_0_) | copy-start | bytes 786436
  15.8 13.7 %collective-permute-start.5 = (bf16[8,64,256]{2,1,0:T(8,128)(2,1)S(1)}, bf16[8,64,256]{2,1,0:T(8,128)(2,1)S(1)}, u32[]{:S(2)}, u32[]{:S(2)}) collective-permute-start(bf16[8,64,256]{2,1,0:T(8,128)(2,1)S(1)} %get-tuple-element.78.refs_0_), channel_id=1, source_target_pairs={{0,12},{4,0},{8,4},{12,8},{1,13},{5,1},{9,5},{13,9},{2,14},{6,2},{... | collective-permute-start | bytes 786440 | tf_op jit(solution)/shard_map/ppermute | solution.py:450
  20.0 20.7 %collective-permute-start.4 = (bf16[8,64,256]{2,1,0:T(8,128)(2,1)S(1)}, bf16[8,64,256]{2,1,0:T(8,128)(2,1)}, u32[]{:S(2)}, u32[]{:S(2)}) collective-permute-start(bf16[8,64,256]{2,1,0:T(8,128)(2,1)S(1)} %get-tuple-element.78.refs_0_), channel_id=1, source_target_pairs={{0,8},{4,12},{8,0},{12,4},{1,9},{5,13},{9,1},{13,5},{2,10},{6,14},... | collective-permute-start | bytes 786440 | tf_op jit(solution)/shard_map/ppermute | solution.py:450
  20.0 20.7 %collective-permute-start.3 = (bf16[8,64,256]{2,1,0:T(8,128)(2,1)S(1)}, bf16[8,64,256]{2,1,0:T(8,128)(2,1)}, u32[]{:S(2)}, u32[]{:S(2)}) collective-permute-start(bf16[8,64,256]{2,1,0:T(8,128)(2,1)S(1)} %get-tuple-element.78.refs_0_), channel_id=1, source_target_pairs={{0,4},{4,8},{8,12},{12,0},{1,5},{5,9},{9,13},{13,1},{2,6},{6,10},{... | collective-permute-start | bytes 786440 | tf_op jit(solution)/shard_map/ppermute | solution.py:450
  23.4 3.4 %collective-permute-start.1 = (bf16[256,1024]{0,1:T(8,128)(2,1)S(1)}, bf16[256,1024]{0,1:T(8,128)(2,1)S(1)}, u32[]{:S(2)}, u32[]{:S(2)}) collective-permute-start(bf16[256,1024]{0,1:T(8,128)(2,1)S(1)} %pad_maximum_fusion.2), channel_id=1, source_target_pairs={{0,1},{1,0},{2,3},{3,2},{4,5},{5,4},{6,7},{7,6},{8,9},{9,8},{10,11... | collective-permute-start | bytes 1572872 | tf_op jit(solution)/shard_map/ppermute | solution.py:482
  29.6 11.2 %copy-start.8 = (bf16[8,64,256]{2,1,0:T(8,128)(2,1)}, bf16[8,64,256]{2,1,0:T(8,128)(2,1)S(1)}, u32[]{:S(2)}) copy-start(bf16[8,64,256]{2,1,0:T(8,128)(2,1)S(1)} %collective-permute-done.5.refs_3_) | copy-start | bytes 786436
  42.6 14.8 %collective-permute-start.9 = (bf16[21,64,256]{2,1,0:T(8,128)(2,1)S(1)}, bf16[21,64,256]{2,1,0:T(8,128)(2,1)S(1)}, u32[]{:S(2)}, u32[]{:S(2)}) collective-permute-start(bf16[21,64,256]{2,1,0:T(8,128)(2,1)S(1)} %pick.2.refs_0_), channel_id=1, source_target_pairs={{0,2},{2,0},{1,3},{3,1},{4,6},{6,4},{5,7},{7,5},{8,10},{10,8},{9,1... | collective-permute-start | bytes 2064392 | tf_op jit(solution)/shard_map/ppermute | solution.py:510
  44.8 17.9 %copy-start.4 = (bf16[8,64,256]{2,1,0:T(8,128)(2,1)}, bf16[8,64,256]{2,1,0:T(8,128)(2,1)S(1)}, u32[]{:S(2)}) copy-start(bf16[8,64,256]{2,1,0:T(8,128)(2,1)S(1)} %get-tuple-element.87.refs_0_) | copy-start | bytes 786436
  44.8 18.8 %collective-permute-start.8 = (bf16[8,64,256]{2,1,0:T(8,128)(2,1)S(1)}, bf16[8,64,256]{2,1,0:T(8,128)(2,1)S(1)}, u32[]{:S(2)}, u32[]{:S(2)}) collective-permute-start(bf16[8,64,256]{2,1,0:T(8,128)(2,1)S(1)} %get-tuple-element.87.refs_0_), channel_id=1, source_target_pairs={{0,12},{4,0},{8,4},{12,8},{1,13},{5,1},{9,5},{13,9},{2,14},{6,2},{... | collective-permute-start | bytes 786440 | tf_op jit(solution)/shard_map/ppermute | solution.py:450
  44.8 24.7 %collective-permute-start.7 = (bf16[8,64,256]{2,1,0:T(8,128)(2,1)S(1)}, bf16[8,64,256]{2,1,0:T(8,128)(2,1)S(1)}, u32[]{:S(2)}, u32[]{:S(2)}) collective-permute-start(bf16[8,64,256]{2,1,0:T(8,128)(2,1)S(1)} %get-tuple-element.87.refs_0_), channel_id=1, source_target_pairs={{0,8},{4,12},{8,0},{12,4},{1,9},{5,13},{9,1},{13,5},{2,10},{6,14},... | collective-permute-start | bytes 786440 | tf_op jit(solution)/shard_map/ppermute | solution.py:450
  47.3 22.2 %collective-permute-start.6 = (bf16[8,64,256]{2,1,0:T(8,128)(2,1)S(1)}, bf16[8,64,256]{2,1,0:T(8,128)(2,1)S(1)}, u32[]{:S(2)}, u32[]{:S(2)}) collective-permute-start(bf16[8,64,256]{2,1,0:T(8,128)(2,1)S(1)} %get-tuple-element.87.refs_0_), channel_id=1, source_target_pairs={{0,4},{4,8},{8,12},{12,0},{1,5},{5,9},{9,13},{13,1},{2,6},{6,10},{... | collective-permute-start | bytes 786440 | tf_op jit(solution)/shard_map/ppermute | solution.py:450
  63.6 6.0 %copy-start.9 = (bf16[8,64,256]{2,1,0:T(8,128)(2,1)}, bf16[8,64,256]{2,1,0:T(8,128)(2,1)S(1)}, u32[]{:S(2)}) copy-start(bf16[8,64,256]{2,1,0:T(8,128)(2,1)S(1)} %collective-permute-done.8.refs_3_) | copy-start | bytes 786436
  69.5 0.7 copy-start.10
  69.5 0.8 copy-start.11
  72.1 23.3 %collective-permute-start.10 = (bf16[21,64,256]{2,1,0:T(8,128)(2,1)S(1)}, bf16[21,64,256]{2,1,0:T(8,128)(2,1)S(1)}, u32[]{:S(2)}, u32[]{:S(2)}) collective-permute-start(bf16[21,64,256]{2,1,0:T(8,128)(2,1)S(1)} %pick.3.refs_0_.refs_3_), channel_id=1, source_target_pairs={{0,2},{2,0},{1,3},{3,1},{4,6},{6,4},{5,7},{7,5},{8,10},{10,8},{9,1... | collective-permute-start | bytes 2064392 | tf_op jit(solution)/shard_map/ppermute | solution.py:510
  72.7 7.6 %collective-permute-start.13 = (bf16[128,1024]{1,0:T(8,128)(2,1)}, bf16[128,1024]{1,0:T(8,128)(2,1)}, u32[]{:S(2)}, u32[]{:S(2)}) collective-permute-start(bf16[128,1024]{1,0:T(8,128)(2,1)} %get-tuple-element.153), channel_id=1, source_target_pairs={{0,12},{4,0},{8,4},{12,8},{1,13},{5,1},{9,5},{13,9},{2,14},{6,2},{... | collective-permute-start | bytes 786440 | tf_op jit(solution)/shard_map/ppermute | solution.py:450
  72.7 22.7 %collective-permute-start.12 = (bf16[128,1024]{1,0:T(8,128)(2,1)}, bf16[128,1024]{1,0:T(8,128)(2,1)}, u32[]{:S(2)}, u32[]{:S(2)}) collective-permute-start(bf16[128,1024]{1,0:T(8,128)(2,1)} %get-tuple-element.154), channel_id=1, source_target_pairs={{0,8},{4,12},{8,0},{12,4},{1,9},{5,13},{9,1},{13,5},{2,10},{6,14},... | collective-permute-start | bytes 786440 | tf_op jit(solution)/shard_map/ppermute | solution.py:450
  72.7 22.7 %collective-permute-start.11 = (bf16[128,1024]{1,0:T(8,128)(2,1)S(1)}, bf16[128,1024]{1,0:T(8,128)(2,1)}, u32[]{:S(2)}, u32[]{:S(2)}) collective-permute-start(bf16[128,1024]{1,0:T(8,128)(2,1)S(1)} %get-tuple-element.155), channel_id=1, source_target_pairs={{0,4},{4,8},{8,12},{12,0},{1,5},{5,9},{9,13},{13,1},{2,6},{6,10},{... | collective-permute-start | bytes 786440 | tf_op jit(solution)/shard_map/ppermute | solution.py:450
  74.8 20.7 %copy-start.6 = (bf16[128,1024]{1,0:T(8,128)(2,1)S(1)}, bf16[128,1024]{1,0:T(8,128)(2,1)}, u32[]{:S(2)}) copy-start(bf16[128,1024]{1,0:T(8,128)(2,1)} %get-tuple-element.156) | copy-start | bytes 786436
  74.9 31.5 %collective-permute-start.20 = (bf16[21,128,128]{2,1,0:T(8,128)(2,1)S(1)}, bf16[21,128,128]{2,1,0:T(8,128)(2,1)S(1)}, u32[]{:S(2)}, u32[]{:S(2)}) collective-permute-start(bf16[21,128,128]{2,1,0:T(8,128)(2,1)S(1)} %fusion.1), channel_id=1, source_target_pairs={{0,1},{1,0},{2,3},{3,2},{4,5},{5,4},{6,7},{7,6},{8,9},{9,8},{10,11... | collective-permute-start | bytes 2064392 | tf_op jit(solution)/shard_map/ppermute | solution.py:524
  96.9 11.5 %collective-permute-start.19 = (bf16[128,1024]{1,0:T(8,128)(2,1)S(1)}, bf16[128,1024]{1,0:T(8,128)(2,1)S(1)}, u32[]{:S(2)}, u32[]{:S(2)}) collective-permute-start(bf16[128,1024]{1,0:T(8,128)(2,1)S(1)} %multiply_convert_fusion.1.refs_0_), channel_id=1, source_target_pairs={{0,12},{4,0},{8,4},{12,8},{1,13},{5,1},{9,5},{13,9},{2,14},{6,2},{... | collective-permute-start | bytes 786440 | tf_op jit(solution)/shard_map/ppermute | solution.py:450
  97.0 26.2 %collective-permute-start.18 = (bf16[128,1024]{1,0:T(8,128)(2,1)S(1)}, bf16[128,1024]{1,0:T(8,128)(2,1)S(1)}, u32[]{:S(2)}, u32[]{:S(2)}) collective-permute-start(bf16[128,1024]{1,0:T(8,128)(2,1)S(1)} %multiply_convert_fusion.1.refs_0_), channel_id=1, source_target_pairs={{0,8},{4,12},{8,0},{12,4},{1,9},{5,13},{9,1},{13,5},{2,10},{6,14},... | collective-permute-start | bytes 786440 | tf_op jit(solution)/shard_map/ppermute | solution.py:450
  98.9 24.3 %collective-permute-start.17 = (bf16[128,1024]{1,0:T(8,128)(2,1)S(1)}, bf16[128,1024]{1,0:T(8,128)(2,1)S(1)}, u32[]{:S(2)}, u32[]{:S(2)}) collective-permute-start(bf16[128,1024]{1,0:T(8,128)(2,1)S(1)} %multiply_convert_fusion.1.refs_0_), channel_id=1, source_target_pairs={{0,4},{4,8},{8,12},{12,0},{1,5},{5,9},{9,13},{13,1},{2,6},{6,10},{... | collective-permute-start | bytes 786440 | tf_op jit(solution)/shard_map/ppermute | solution.py:450
  101.0 67.3 %collective-permute-start.25 = (bf16[21,128,128]{2,1,0:T(8,128)(2,1)S(1)}, bf16[21,128,128]{2,1,0:T(8,128)(2,1)S(1)}, u32[]{:S(2)}, u32[]{:S(2)}) collective-permute-start(bf16[21,128,128]{2,1,0:T(8,128)(2,1)S(1)} %fusion), channel_id=1, source_target_pairs={{0,1},{1,0},{2,3},{3,2},{4,5},{5,4},{6,7},{7,6},{8,9},{9,8},{10,11... | collective-permute-start | bytes 2064392 | tf_op jit(solution)/shard_map/ppermute | solution.py:524
  106.4 25.6 %collective-permute-start.16 = (bf16[128,1024]{1,0:T(8,128)(2,1)S(1)}, bf16[128,1024]{1,0:T(8,128)(2,1)S(1)}, u32[]{:S(2)}, u32[]{:S(2)}) collective-permute-start(bf16[128,1024]{1,0:T(8,128)(2,1)S(1)} %get-tuple-element.150), channel_id=1, source_target_pairs={{0,12},{4,0},{8,4},{12,8},{1,13},{5,1},{9,5},{13,9},{2,14},{6,2},{... | collective-permute-start | bytes 786440 | tf_op jit(solution)/shard_map/ppermute | solution.py:450
  108.4 36.3 %collective-permute-start.15 = (bf16[128,1024]{1,0:T(8,128)(2,1)S(1)}, bf16[128,1024]{1,0:T(8,128)(2,1)S(1)}, u32[]{:S(2)}, u32[]{:S(2)}) collective-permute-start(bf16[128,1024]{1,0:T(8,128)(2,1)S(1)} %get-tuple-element.151), channel_id=1, source_target_pairs={{0,8},{4,12},{8,0},{12,4},{1,9},{5,13},{9,1},{13,5},{2,10},{6,14},... | collective-permute-start | bytes 786440 | tf_op jit(solution)/shard_map/ppermute | solution.py:450
  123.1 21.5 %copy-start.7 = (bf16[128,1024]{1,0:T(8,128)(2,1)S(1)}, bf16[128,1024]{1,0:T(8,128)(2,1)}, u32[]{:S(2)}) copy-start(bf16[128,1024]{1,0:T(8,128)(2,1)} %constant_dynamic-slice_fusion.3) | copy-start | bytes 786436
  123.1 21.5 %collective-permute-start.14 = (bf16[128,1024]{1,0:T(8,128)(2,1)S(1)}, bf16[128,1024]{1,0:T(8,128)(2,1)S(1)}, u32[]{:S(2)}, u32[]{:S(2)}) collective-permute-start(bf16[128,1024]{1,0:T(8,128)(2,1)S(1)} %get-tuple-element.152), channel_id=1, source_target_pairs={{0,4},{4,8},{8,12},{12,0},{1,5},{5,9},{9,13},{13,1},{2,6},{6,10},{... | collective-permute-start | bytes 786440 | tf_op jit(solution)/shard_map/ppermute | solution.py:450
  130.5 37.8 %collective-permute-start.21 = (bf16[21,64,256]{2,1,0:T(8,128)(2,1)S(1)}, bf16[21,64,256]{2,1,0:T(8,128)(2,1)S(1)}, u32[]{:S(2)}, u32[]{:S(2)}) collective-permute-start(bf16[21,64,256]{2,1,0:T(8,128)(2,1)S(1)} %get-tuple-element.105), channel_id=1, source_target_pairs={{0,2},{2,0},{1,3},{3,1},{4,6},{6,4},{5,7},{7,5},{8,10},{10,8},{9,1... | collective-permute-start | bytes 2064392 | tf_op jit(solution)/shard_map/ppermute | solution.py:558
  144.9 9.0 %collective-permute-start.24 = (bf16[128,1024]{1,0:T(8,128)(2,1)S(1)}, bf16[128,1024]{1,0:T(8,128)(2,1)S(1)}, u32[]{:S(2)}, u32[]{:S(2)}) collective-permute-start(bf16[128,1024]{1,0:T(8,128)(2,1)S(1)} %fusion.6.refs_0_), channel_id=1, source_target_pairs={{0,12},{4,0},{8,4},{12,8},{1,13},{5,1},{9,5},{13,9},{2,14},{6,2},{... | collective-permute-start | bytes 786440 | tf_op jit(solution)/shard_map/ppermute | solution.py:450
  145.0 23.3 %collective-permute-start.23 = (bf16[128,1024]{1,0:T(8,128)(2,1)S(1)}, bf16[128,1024]{1,0:T(8,128)(2,1)S(1)}, u32[]{:S(2)}, u32[]{:S(2)}) collective-permute-start(bf16[128,1024]{1,0:T(8,128)(2,1)S(1)} %fusion.6.refs_0_), channel_id=1, source_target_pairs={{0,8},{4,12},{8,0},{12,4},{1,9},{5,13},{9,1},{13,5},{2,10},{6,14},... | collective-permute-start | bytes 786440 | tf_op jit(solution)/shard_map/ppermute | solution.py:450
  145.0 23.2 %collective-permute-start.22 = (bf16[128,1024]{1,0:T(8,128)(2,1)S(1)}, bf16[128,1024]{1,0:T(8,128)(2,1)S(1)}, u32[]{:S(2)}, u32[]{:S(2)}) collective-permute-start(bf16[128,1024]{1,0:T(8,128)(2,1)S(1)} %fusion.6.refs_0_), channel_id=1, source_target_pairs={{0,4},{4,8},{8,12},{12,0},{1,5},{5,9},{9,13},{13,1},{2,6},{6,10},{... | collective-permute-start | bytes 786440 | tf_op jit(solution)/shard_map/ppermute | solution.py:450
  153.9 26.9 %collective-permute-start.26 = (bf16[4,128,1024]{2,1,0:T(8,128)(2,1)S(1)}, bf16[4,128,1024]{2,1,0:T(8,128)(2,1)S(1)}, u32[]{:S(2)}, u32[]{:S(2)}) collective-permute-start(bf16[4,128,1024]{2,1,0:T(8,128)(2,1)S(1)} %get-tuple-element.114.refs_6_), channel_id=1, source_target_pairs={{0,1},{1,0},{2,3},{3,2},{4,5},{5,4},{6,7},{7,6},{8,9},{9,8},{10,11... | collective-permute-start | bytes 3145736 | tf_op jit(solution)/shard_map/ppermute | solution.py:566
  175.6 7.2 %collective-permute-start.27 = (bf16[4,128,1024]{2,1,0:T(8,128)(2,1)S(1)}, bf16[4,128,1024]{2,1,0:T(8,128)(2,1)S(1)}, u32[]{:S(2)}, u32[]{:S(2)}) collective-permute-start(bf16[4,128,1024]{2,1,0:T(8,128)(2,1)S(1)} %get-tuple-element.115.refs_8_), channel_id=1, source_target_pairs={{0,1},{1,0},{2,3},{3,2},{4,5},{5,4},{6,7},{7,6},{8,9},{9,8},{10,11... | collective-permute-start | bytes 3145736 | tf_op jit(solution)/shard_map/ppermute | solution.py:566
  175.7 17.9 %collective-permute-start.28 = (bf16[21,64,256]{2,1,0:T(8,128)(2,1)S(1)}, bf16[21,64,256]{2,1,0:T(8,128)(2,1)S(1)}, u32[]{:S(2)}, u32[]{:S(2)}) collective-permute-start(bf16[21,64,256]{2,1,0:T(8,128)(2,1)S(1)} %get-tuple-element.116), channel_id=1, source_target_pairs={{0,2},{2,0},{1,3},{3,1},{4,6},{6,4},{5,7},{7,5},{8,10},{10,8},{9,1... | collective-permute-start | bytes 2064392 | tf_op jit(solution)/shard_map/ppermute | solution.py:558
  178.3 16.3 %collective-permute-start.31 = (bf16[8,64,256]{2,1,0:T(8,128)(2,1)S(1)}, bf16[8,64,256]{2,1,0:T(8,128)(2,1)S(1)}, u32[]{:S(2)}, u32[]{:S(2)}) collective-permute-start(bf16[8,64,256]{2,1,0:T(8,128)(2,1)S(1)} %get-tuple-element.143), channel_id=1, source_target_pairs={{0,12},{4,0},{8,4},{12,8},{1,13},{5,1},{9,5},{13,9},{2,14},{6,2},{... | collective-permute-start | bytes 786440 | tf_op jit(solution)/shard_map/ppermute | solution.py:450
  178.3 25.9 %collective-permute-start.30 = (bf16[8,64,256]{2,1,0:T(8,128)(2,1)S(1)}, bf16[8,64,256]{2,1,0:T(8,128)(2,1)S(1)}, u32[]{:S(2)}, u32[]{:S(2)}) collective-permute-start(bf16[8,64,256]{2,1,0:T(8,128)(2,1)S(1)} %get-tuple-element.144), channel_id=1, source_target_pairs={{0,8},{4,12},{8,0},{12,4},{1,9},{5,13},{9,1},{13,5},{2,10},{6,14},... | collective-permute-start | bytes 786440 | tf_op jit(solution)/shard_map/ppermute | solution.py:450
  180.9 23.4 %collective-permute-start.29 = (bf16[8,64,256]{2,1,0:T(8,128)(2,1)S(1)}, bf16[8,64,256]{2,1,0:T(8,128)(2,1)S(1)}, u32[]{:S(2)}, u32[]{:S(2)}) collective-permute-start(bf16[8,64,256]{2,1,0:T(8,128)(2,1)S(1)} %get-tuple-element.145), channel_id=1, source_target_pairs={{0,4},{4,8},{8,12},{12,0},{1,5},{5,9},{9,13},{13,1},{2,6},{6,10},{... | collective-permute-start | bytes 786440 | tf_op jit(solution)/shard_map/ppermute | solution.py:450
  193.5 10.8 %copy-start.2 = (f32[8,64,256]{2,1,0:T(8,128)S(1)}, f32[8,64,256]{2,1,0:T(8,128)}, u32[]{:S(2)}) copy-start(f32[8,64,256]{2,1,0:T(8,128)} %copy-done.1) | copy-start | bytes 1572868
  204.5 30.3 %copy-start = (bf16[512,1024]{0,1:T(8,128)(2,1)S(1)}, bf16[512,1024]{0,1:T(8,128)(2,1)}, u32[]{:S(2)}) copy-start(bf16[512,1024]{0,1:T(8,128)(2,1)} %concatenate.26) | copy-start | bytes 3145732
  204.5 7.9 %collective-permute-start.32 = (bf16[8,64,256]{2,1,0:T(8,128)(2,1)S(1)}, bf16[8,64,256]{2,1,0:T(8,128)(2,1)S(1)}, u32[]{:S(2)}, u32[]{:S(2)}) collective-permute-start(bf16[8,64,256]{2,1,0:T(8,128)(2,1)S(1)} %fusion.10), channel_id=1, source_target_pairs={{0,2},{2,0},{1,3},{3,1},{4,6},{6,4},{5,7},{7,5},{8,10},{10,8},{9,1... | collective-permute-start | bytes 786440 | tf_op jit(solution)/shard_map/ppermute | solution.py:602
  205.1 11.1 %collective-permute-start.33 = (bf16[8,64,256]{2,1,0:T(8,128)(2,1)S(1)}, bf16[8,64,256]{2,1,0:T(8,128)(2,1)S(1)}, u32[]{:S(2)}, u32[]{:S(2)}) collective-permute-start(bf16[8,64,256]{2,1,0:T(8,128)(2,1)S(1)} %get-tuple-element.123), channel_id=1, source_target_pairs={{0,4},{4,8},{8,12},{12,0},{1,5},{5,9},{9,13},{13,1},{2,6},{6,10},{... | collective-permute-start | bytes 786440 | tf_op jit(solution)/shard_map/ppermute | solution.py:450
  205.1 20.8 %collective-permute-start.34 = (bf16[8,64,256]{2,1,0:T(8,128)(2,1)S(1)}, bf16[8,64,256]{2,1,0:T(8,128)(2,1)S(1)}, u32[]{:S(2)}, u32[]{:S(2)}) collective-permute-start(bf16[8,64,256]{2,1,0:T(8,128)(2,1)S(1)} %get-tuple-element.124), channel_id=1, source_target_pairs={{0,8},{4,12},{8,0},{12,4},{1,9},{5,13},{9,1},{13,5},{2,10},{6,14},... | collective-permute-start | bytes 786440 | tf_op jit(solution)/shard_map/ppermute | solution.py:450
  205.6 20.3 %collective-permute-start.35 = (bf16[8,64,256]{2,1,0:T(8,128)(2,1)S(1)}, bf16[8,64,256]{2,1,0:T(8,128)(2,1)S(1)}, u32[]{:S(2)}, u32[]{:S(2)}) collective-permute-start(bf16[8,64,256]{2,1,0:T(8,128)(2,1)S(1)} %get-tuple-element.125), channel_id=1, source_target_pairs={{0,12},{4,0},{8,4},{12,8},{1,13},{5,1},{9,5},{13,9},{2,14},{6,2},{... | collective-permute-start | bytes 786440 | tf_op jit(solution)/shard_map/ppermute | solution.py:450
  212.5 13.4 %collective-permute-start.36 = (bf16[4,128,256]{2,1,0:T(8,128)(2,1)S(1)}, bf16[4,128,256]{2,1,0:T(8,128)(2,1)S(1)}, u32[]{:S(2)}, u32[]{:S(2)}) collective-permute-start(bf16[4,128,256]{2,1,0:T(8,128)(2,1)S(1)} %get-tuple-element.157), channel_id=1, source_target_pairs={{0,1},{1,0},{2,3},{3,2},{4,5},{5,4},{6,7},{7,6},{8,9},{9,8},{10,11... | collective-permute-start | bytes 786440 | tf_op jit(solution)/shard_map/ppermute | solution.py:608
  226.1 5.8 %collective-permute-start.39 = (bf16[4,64,256]{2,1,0:T(8,128)(2,1)S(1)}, bf16[4,64,256]{2,1,0:T(8,128)(2,1)S(1)}, u32[]{:S(2)}, u32[]{:S(2)}) collective-permute-start(bf16[4,64,256]{2,1,0:T(8,128)(2,1)S(1)} %get-tuple-element.159), channel_id=1, source_target_pairs={{0,3},{1,2},{2,1},{3,0},{4,7},{5,6},{6,5},{7,4},{8,11},{9,10},{10,... | collective-permute-start | bytes 393224 | tf_op jit(solution)/shard_map/ppermute | solution.py:622
  226.2 5.7 %collective-permute-start.38 = (bf16[4,64,256]{2,1,0:T(8,128)(2,1)S(1)}, bf16[4,64,256]{2,1,0:T(8,128)(2,1)S(1)}, u32[]{:S(2)}, u32[]{:S(2)}) collective-permute-start(bf16[4,64,256]{2,1,0:T(8,128)(2,1)S(1)} %get-tuple-element.159), channel_id=1, source_target_pairs={{0,1},{1,0},{2,3},{3,2},{4,5},{5,4},{6,7},{7,6},{8,9},{9,8},{10,11... | collective-permute-start | bytes 393224 | tf_op jit(solution)/shard_map/ppermute | solution.py:622
  227.8 7.0 %collective-permute-start.37 = (bf16[4,64,256]{2,1,0:T(8,128)(2,1)S(1)}, bf16[4,64,256]{2,1,0:T(8,128)(2,1)S(1)}, u32[]{:S(2)}, u32[]{:S(2)}) collective-permute-start(bf16[4,64,256]{2,1,0:T(8,128)(2,1)S(1)} %get-tuple-element.160.refs_1_), channel_id=1, source_target_pairs={{0,2},{1,3},{2,0},{3,1},{4,6},{5,7},{6,4},{7,5},{8,10},{9,11},{10,... | collective-permute-start | bytes 393224 | tf_op jit(solution)/shard_map/ppermute | solution.py:622

commit v4 on v3

--- a/solution.py
+++ b/solution.py
@@ -43,6 +43,7 @@
 VMEM = pl.BlockSpec(memory_space=pltpu.VMEM)
 SMEM = pl.BlockSpec(memory_space=pltpu.SMEM)
 HBM = pl.BlockSpec(memory_space=pltpu.HBM)
+ANY = pl.BlockSpec(memory_space=pl.ANY)
 
 
 def start_fetch(weight, held, sems, per):
@@ -176,14 +177,14 @@
 def pick(meta, bufs, slots):
     return pl.pallas_call(
         functools.partial(pick_kernel, slots, len(bufs)),
-        in_specs=[SMEM] + [HBM] * len(bufs),
-        out_specs=HBM,
+        in_specs=[SMEM] + [ANY] * len(bufs),
+        out_specs=ANY,
         out_shape=jax.ShapeDtypeStruct((slots,) + bufs[0].shape[1:], BF16),
         scratch_shapes=[pltpu.SemaphoreType.DMA((slots,))],
         compiler_params=params(),
         cost_estimate=cost(0, 4 * slots * bufs[0][0].size),
         name="pick",
-    )(meta, *[in_hbm(b) for b in bufs])
+    )(meta, *bufs)
 
 
 def decode_kernel(slots, per, count, layers, meta, *refs):
@@ -489,6 +490,13 @@
         for t in targets_rel
     ]
 
+    def error_of(c, *others):
+        total = parts[c][0].astype(F32)
+        for g in tie(sums[c], *others):
+            total = total + g.astype(F32)
+        return ((total - own_targets[c].astype(F32)) * scale).astype(BF16)
+
+    own_errors = []
     slopes, lat_pieces, parts, sums, got = [], [], [], [], []
     for c in range(chunks):
         own, *recv = tie([owns[c], *recvs[c]], *got)
@@ -503,7 +511,11 @@
             recvs[1:] = [
                 late[n * (width - 1) : (n + 1) * (width - 1)] for n in range(chunks - 1)
             ]
-        picked = tie(got, *(parts[-1] if parts else ()))
+        if c:
+            tied = tie([*parts[-1], *got])
+            parts[-1], got = tied[:lays], tied[lays:]
+            sums.append(to_each(parts[-1]))
+        picked = got
         mine = pick(meta, [latent] + picked, slots)
         lat_pieces.append(
             [mine]
@@ -511,11 +523,11 @@
         )
         pieces = lat_pieces[c]
         if c:
-            tied = tie([*pieces, *sums[-1]])
-            pieces, sums[-1] = tied[:width], tied[width:]
+            own_errors.append(error_of(c - 1))
+            *pieces, own_errors[-1] = tie([*pieces, own_errors[-1]])
         recon = decode(meta, pieces, dec_weight, layers).reshape(lays, share, d)
         parts.append(by_shift(recon))
-        sums.append(to_each(parts[c]))
+    sums.append(to_each(parts[-1]))
     theirs_lat = []
     for c in range(chunks):
         whole_lat = jnp.concatenate(lat_pieces[c], 1)
@@ -535,13 +547,9 @@
     grads = [[[] for _ in range(chunks)] for _ in range(reps)]
     lat_groups, spreads, recvs = [], [], []
     for c in range(chunks):
-        arrived = sums[c]
-        if c:
-            *arrived, spreads[-1] = tie([*arrived, spreads[-1]])
-        total = parts[c][0].astype(F32)
-        for g in arrived:
-            total = total + g.astype(F32)
-        own_error = ((total - own_targets[c].astype(F32)) * scale).astype(BF16)
+        if c == len(own_errors):
+            own_errors.append(error_of(c, *spreads[-1:]))
+        own_error = own_errors[c]
         arrived = tie(to_each([own_error] * lays), *theirs_lat[c], *(recvs[-1] if c else ()))
         error, total, *sends = spread(
             scal,

time: 241 us -> 240 us (level)
  waiting for transfers between devices: 134 us -> 117 us
  starting transfers between devices: 39.5 us -> 55 us
    ppermute x24, waiting for transfers between devices: 109 us -> 91.2 us  [to_each(): lax.ppermute(parts[m], 'lay', ring_shift('lay', m))]
    ppermute x24, starting transfers between devices: 28 us -> 43.5 us  [to_each(): lax.ppermute(parts[m], 'lay', ring_shift('lay', m))]
  transfers between devices with their start and end apart: 40 -> 40, of which waited for: 17 -> 17; matrix products, arithmetic and copies ran while one was open for 5% -> 6% of each run, Pallas kernels for 16% -> 16%
where the time goes in v4:
time: 240 us; the launch traced here: 237 us
  waiting for transfers between devices  117 us (49%)
  starting transfers between devices  55 us (23%)
  Pallas kernels  50.1 us (21%)
  local copies, waits for them, and re-layouts  11.7 us (5%)
  other arithmetic  2.89 us (1%)
    ppermute x24, waiting for transfers between devices, to_each(): lax.ppermute(parts[m], 'lay', ring_shift('lay', m))  91.2 us
    ppermute x24, starting transfers between devices, to_each(): lax.ppermute(parts[m], 'lay', ring_shift('lay', m))  43.5 us
    pallas_call x2, Pallas kernels, spread(): pl.pallas_call(functools.partial(spread_kernel, slots, per, width, len(pa...  14.6 us
    pallas_call x2, Pallas kernels, decode(): pl.pallas_call(functools.partial(decode_kernel, slots, per, len(lats), la...  10.6 us
    ppermute x2, waiting for transfers between devices, local(): lax.ppermute(mine, 'wid', ring_shift('wid', -m))  8.07 us
    pallas_call x1, Pallas kernels, dec_grad(): pl.pallas_call(functools.partial(dec_grad_kernel, slots, per, len(lats),...  7.08 us
    pallas_call x2, Pallas kernels, encode(): pl.pallas_call(functools.partial(encode_kernel, pieces, chunks), in_specs...  7.06 us
    ppermute x3, waiting for transfers between devices, local(): moved = lax.ppermute(sent, ('wid', 'rep'), pairs)  6.46 us
  transfers between devices with their start and end apart: 40, of which 17 were waited for; matrix products, arithmetic and copies ran while one was open for 6% of the time, Pallas kernels for 16%

profile of v4, /device:TPU:0, one launch (start us, length us, event | category | flops | bytes accessed | tf_op | source)
XLA Modules:
  0.0 237.4 jit_solution(5814149665195813543)
XLA Ops:
  0.7 3.5 %encode.3 = (bf16[8,64,256]{2,1,0:T(8,128)(2,1)S(1)}, bf16[8,64,256]{2,1,0:T(8,128)(2,1)S(1)}) custom-call(s32[5]{0:T(128)S(1)} %stack.19.scal, bf16[4,256,1024]{2,1,0:T(8,128)(2,1)} %acts.3, bf16[1024,2048]{1,0:T(8,128)(2,1)} %weight.3), custom_call_target="tpu_custom_call" | custom-call | flops 536870912 | bytes 4194304 | tf_op jit(solution)/shard_map/encode/pallas_call | solution.py:111
  4.3 3.0 %collective-permute-start = (bf16[8,64,256]{2,1,0:T(8,128)(2,1)S(1)}, bf16[8,64,256]{2,1,0:T(8,128)(2,1)S(1)}, u32[]{:S(2)}, u32[]{:S(2)}) collective-permute-start(bf16[8,64,256]{2,1,0:T(8,128)(2,1)S(1)} %get-tuple-element.70), channel_id=1, source_target_pairs={{0,2},{2,0},{1,3},{3,1},{4,6},{6,4},{5,7},{7,5},{8,10},{10,8},{9,1... | collective-permute-start | bytes 786440 | tf_op jit(solution)/shard_map/ppermute | solution.py:469
  7.6 3.5 %encode.2 = (f32[8,64,256]{2,1,0:T(8,128)S(1)}, f32[8,64,256]{2,1,0:T(8,128)S(1)}) custom-call(s32[5]{0:T(128)S(1)} %stack.19.scal, bf16[4,256,1024]{2,1,0:T(8,128)(2,1)} %acts.3, bf16[1024,2048]{1,0:T(8,128)(2,1)} %weight.3), custom_call_target="tpu_custom_call" | custom-call | flops 536870912 | bytes 4194304 | tf_op jit(solution)/shard_map/encode/pallas_call | solution.py:111
  11.2 3.2 %collective-permute-done.refs_0_ = bf16[8,64,256]{2,1,0:T(8,128)(2,1)S(1)} collective-permute-done((bf16[8,64,256]{2,1,0:T(8,128)(2,1)S(1)}, bf16[8,64,256]{2,1,0:T(8,128)(2,1)S(1)}, u32[]{:S(2)}, u32[]{:S(2)}) %collective-permute-start) | collective-permute-done | bytes 262176 | tf_op jit(solution)/shard_map/ppermute | solution.py:469
  14.6 0.4 gate.2
  15.0 0.8 copy-done.1
  15.8 4.2 %collective-permute-start.5 = (bf16[8,64,256]{2,1,0:T(8,128)(2,1)S(1)}, bf16[8,64,256]{2,1,0:T(8,128)(2,1)S(1)}, u32[]{:S(2)}, u32[]{:S(2)}) collective-permute-start(bf16[8,64,256]{2,1,0:T(8,128)(2,1)S(1)} %get-tuple-element.79.refs_0_), channel_id=1, source_target_pairs={{0,12},{4,0},{8,4},{12,8},{1,13},{5,1},{9,5},{13,9},{2,14},{6,2},{... | collective-permute-start | bytes 786440 | tf_op jit(solution)/shard_map/ppermute | solution.py:451
  20.0 1.0 collective-permute-start.3
  21.0 1.2 constant_dynamic-slice_fusion.9
  23.0 0.4 pad_maximum_fusion.2
  23.4 1.7 constant_dynamic-slice_fusion.5
  25.3 0.7 constant_dynamic-slice_fusion.6
  26.1 0.7 constant_dynamic-slice_fusion.3
  26.8 4.0 %concatenate.26 = bf16[512,1024]{0,1:T(8,128)(2,1)} concatenate(bf16[64,1024]{0,1:T(8,128)(2,1)S(1)} %bitcast.80, bf16[64,1024]{0,1:T(8,128)(2,1)S(1)} %bitcast.78, bf16[64,1024]{0,1:T(8,128)(2,1)S(1)} %bitcast.76, bf16[64,1024]{0,1:T(8,128)(2,1)S(1)} %bitcast.74, bf16[256,1024]{0,1:T(8,128)(2,1)} %collective-permute-done.1), dimensions={0} | concatenate | bytes 2097152 | tf_op jit(solution)/shard_map/concatenate | solution.py:485
  30.8 9.9 %collective-permute-done.4.refs_2_ = bf16[8,64,256]{2,1,0:T(8,128)(2,1)S(1)} collective-permute-done((bf16[8,64,256]{2,1,0:T(8,128)(2,1)S(1)}, bf16[8,64,256]{2,1,0:T(8,128)(2,1)S(1)}, u32[]{:S(2)}, u32[]{:S(2)}) %collective-permute-start.4) | collective-permute-done | bytes 262176 | tf_op jit(solution)/shard_map/ppermute | solution.py:451
  40.6 2.4 pick.2.refs_0_
  43.0 1.6 collective-permute-start.6
  44.7 0.4 gate.3
  45.2 2.5 %collective-permute-start.8 = (bf16[8,64,256]{2,1,0:T(8,128)(2,1)S(1)}, bf16[8,64,256]{2,1,0:T(8,128)(2,1)S(1)}, u32[]{:S(2)}, u32[]{:S(2)}) collective-permute-start(bf16[8,64,256]{2,1,0:T(8,128)(2,1)S(1)} %get-tuple-element.88.refs_0_), channel_id=1, source_target_pairs={{0,8},{4,12},{8,0},{12,4},{1,9},{5,13},{9,1},{13,5},{2,10},{6,14},... | collective-permute-start | bytes 786440 | tf_op jit(solution)/shard_map/ppermute | solution.py:451
  47.8 1.9 collective-permute-start.7
  49.7 8.1 %collective-permute-done.6.refs_1_ = bf16[21,64,256]{2,1,0:T(8,128)(2,1)S(1)} collective-permute-done((bf16[21,64,256]{2,1,0:T(8,128)(2,1)S(1)}, bf16[21,64,256]{2,1,0:T(8,128)(2,1)S(1)}, u32[]{:S(2)}, u32[]{:S(2)}) %collective-permute-start.6) | collective-permute-done | bytes 688160 | tf_op jit(solution)/shard_map/ppermute | solution.py:522
  57.8 5.3 %decode.2 = bf16[4,128,1024]{2,1,0:T(8,128)(2,1)S(1)} custom-call(s32[105]{0:T(128)S(1)} %concatenate.29.meta, bf16[21,64,256]{2,1,0:T(8,128)(2,1)S(1)} %pick.2.refs_0_, bf16[21,64,256]{2,1,0:T(8,128)(2,1)S(1)} %collective-permute-done.6.refs_1_, bf16[21,256,1024]{2,1,0:T(8,128)(2,1)} %refs_4_.3), custom_call_target="tpu_custom_call" | custom-call | flops 1409286144 | bytes 12386304 | tf_op jit(solution)/shard_map/decode/pallas_call | solution.py:208
  63.1 1.0 dynamic-slice_bitcast_fusion.10
  64.1 5.8 %collective-permute-done.8.refs_2_ = bf16[8,64,256]{2,1,0:T(8,128)(2,1)S(1)} collective-permute-done((bf16[8,64,256]{2,1,0:T(8,128)(2,1)S(1)}, bf16[8,64,256]{2,1,0:T(8,128)(2,1)S(1)}, u32[]{:S(2)}, u32[]{:S(2)}) %collective-permute-start.8) | collective-permute-done | bytes 262176 | tf_op jit(solution)/shard_map/ppermute | solution.py:451
  69.9 2.4 pick.3.refs_0_.refs_3_
  72.3 0.6 collective-permute-start.10
  72.9 3.8 %collective-permute-start.13 = (bf16[128,1024]{1,0:T(8,128)(2,1)}, bf16[128,1024]{1,0:T(8,128)(2,1)}, u32[]{:S(2)}, u32[]{:S(2)}) collective-permute-start(bf16[128,1024]{1,0:T(8,128)(2,1)} %get-tuple-element.95), channel_id=1, source_target_pairs={{0,12},{4,0},{8,4},{12,8},{1,13},{5,1},{9,5},{13,9},{2,14},{6,2},{... | collective-permute-start | bytes 786440 | tf_op jit(solution)/shard_map/ppermute | solution.py:451
  76.9 7.3 %collective-permute-done.11 = bf16[128,1024]{1,0:T(8,128)(2,1)S(1)} collective-permute-done((bf16[128,1024]{1,0:T(8,128)(2,1)}, bf16[128,1024]{1,0:T(8,128)(2,1)S(1)}, u32[]{:S(2)}, u32[]{:S(2)}) %collective-permute-start.11) | collective-permute-done | bytes 262176 | tf_op jit(solution)/shard_map/ppermute | solution.py:451
  84.2 8.5 %collective-permute-done.12 = bf16[128,1024]{1,0:T(8,128)(2,1)} collective-permute-done((bf16[128,1024]{1,0:T(8,128)(2,1)}, bf16[128,1024]{1,0:T(8,128)(2,1)}, u32[]{:S(2)}, u32[]{:S(2)}) %collective-permute-start.12) | collective-permute-done | bytes 262176 | tf_op jit(solution)/shard_map/ppermute | solution.py:451
  92.7 1.4 multiply_convert_fusion.1.refs_0_
  94.1 5.7 %collective-permute-start.16 = (bf16[128,1024]{1,0:T(8,128)(2,1)S(1)}, bf16[128,1024]{1,0:T(8,128)(2,1)S(1)}, u32[]{:S(2)}, u32[]{:S(2)}) collective-permute-start(bf16[128,1024]{1,0:T(8,128)(2,1)S(1)} %multiply_convert_fusion.1.refs_0_), channel_id=1, source_target_pairs={{0,12},{4,0},{8,4},{12,8},{1,13},{5,1},{9,5},{13,9},{2,14},{6,2},{... | collective-permute-start | bytes 786440 | tf_op jit(solution)/shard_map/ppermute | solution.py:451
  99.8 0.9 collective-permute-start.15
  101.0 5.3 %decode.3 = bf16[4,128,1024]{2,1,0:T(8,128)(2,1)S(1)} custom-call(s32[105]{0:T(128)S(1)} %concatenate.29.meta, bf16[21,64,256]{2,1,0:T(8,128)(2,1)S(1)} %pick.3.refs_0_.refs_3_, bf16[21,64,256]{2,1,0:T(8,128)(2,1)S(1)} %collective-permute-done.10.refs_1_.refs_4_, bf16[21,256,1024]{2,1,0:T(8,128)(2,1)} %refs_4_.3), custom_call_target="tpu_custom_call" | custom-call | flops 1409286144 | bytes 12386304 | tf_op jit(solution)/shard_map/decode/pallas_call | solution.py:208
  106.4 3.9 %collective-permute-start.21 = (bf16[128,1024]{1,0:T(8,128)(2,1)S(1)}, bf16[128,1024]{1,0:T(8,128)(2,1)S(1)}, u32[]{:S(2)}, u32[]{:S(2)}) collective-permute-start(bf16[128,1024]{1,0:T(8,128)(2,1)S(1)} %get-tuple-element.152), channel_id=1, source_target_pairs={{0,12},{4,0},{8,4},{12,8},{1,13},{5,1},{9,5},{13,9},{2,14},{6,2},{... | collective-permute-start | bytes 786440 | tf_op jit(solution)/shard_map/ppermute | solution.py:451
  110.2 8.6 %collective-permute-start.20 = (bf16[128,1024]{1,0:T(8,128)(2,1)S(1)}, bf16[128,1024]{1,0:T(8,128)(2,1)S(1)}, u32[]{:S(2)}, u32[]{:S(2)}) collective-permute-start(bf16[128,1024]{1,0:T(8,128)(2,1)S(1)} %get-tuple-element.153), channel_id=1, source_target_pairs={{0,8},{4,12},{8,0},{12,4},{1,9},{5,13},{9,1},{13,5},{2,10},{6,14},... | collective-permute-start | bytes 786440 | tf_op jit(solution)/shard_map/ppermute | solution.py:451
  118.8 14.5 %collective-permute-done.15.refs_2_ = bf16[128,1024]{1,0:T(8,128)(2,1)S(1)} collective-permute-done((bf16[128,1024]{1,0:T(8,128)(2,1)S(1)}, bf16[128,1024]{1,0:T(8,128)(2,1)S(1)}, u32[]{:S(2)}, u32[]{:S(2)}) %collective-permute-start.15) | collective-permute-done | bytes 262176 | tf_op jit(solution)/shard_map/ppermute | solution.py:451
  133.3 7.3 %spread.2 = (bf16[4,128,1024]{2,1,0:T(8,128)(2,1)S(1)}, f32[33,64,256]{2,1,0:T(8,128)S(1)}, bf16[21,64,256]{2,1,0:T(8,128)(2,1)S(1)}) custom-call(s32[5]{0:T(128)S(1)} %stack.19.scal, s32[105]{0:T(128)S(1)} %concatenate.29.meta, bf16[128,1024]{1,0:T(8,128)(2,1)S(1)} %multiply_convert_fusion.1.refs_0_, bf16[128,1024]{1,0:T(8,128)(2,1)S(1)} %collective-permute-done.14.refs_1_, ...), custom_call_target="tpu_custom_call" | custom-call | flops 1409286144 | bytes 14155776 | tf_op jit(solution)/shard_map/spread/pallas_call | solution.py:266
  140.6 1.6 collective-permute-start.18
  142.2 3.2 %collective-permute-done.20 = bf16[128,1024]{1,0:T(8,128)(2,1)S(1)} collective-permute-done((bf16[128,1024]{1,0:T(8,128)(2,1)S(1)}, bf16[128,1024]{1,0:T(8,128)(2,1)S(1)}, u32[]{:S(2)}, u32[]{:S(2)}) %collective-permute-start.20) | collective-permute-done | bytes 262176 | tf_op jit(solution)/shard_map/ppermute | solution.py:451
  145.6 0.7 collective-permute-start.24
  146.3 0.3 collective-permute-start.23
  146.6 1.9 collective-permute-start.22
  148.6 4.5 %collective-permute-done.24.refs_3_ = bf16[128,1024]{1,0:T(8,128)(2,1)S(1)} collective-permute-done((bf16[128,1024]{1,0:T(8,128)(2,1)S(1)}, bf16[128,1024]{1,0:T(8,128)(2,1)S(1)}, u32[]{:S(2)}, u32[]{:S(2)}) %collective-permute-start.24) | collective-permute-done | bytes 262176 | tf_op jit(solution)/shard_map/ppermute | solution.py:451
  153.1 15.9 %collective-permute-done.23.refs_2_ = bf16[128,1024]{1,0:T(8,128)(2,1)S(1)} collective-permute-done((bf16[128,1024]{1,0:T(8,128)(2,1)S(1)}, bf16[128,1024]{1,0:T(8,128)(2,1)S(1)}, u32[]{:S(2)}, u32[]{:S(2)}) %collective-permute-start.23) | collective-permute-done | bytes 262176 | tf_op jit(solution)/shard_map/ppermute | solution.py:451
  169.0 7.3 %spread.3 = (bf16[4,128,1024]{2,1,0:T(8,128)(2,1)S(1)}, f32[33,64,256]{2,1,0:T(8,128)S(1)}, bf16[21,64,256]{2,1,0:T(8,128)(2,1)S(1)}) custom-call(s32[5]{0:T(128)S(1)} %stack.19.scal, s32[105]{0:T(128)S(1)} %concatenate.29.meta, bf16[128,1024]{1,0:T(8,128)(2,1)S(1)} %fusion.6.refs_0_, bf16[128,1024]{1,0:T(8,128)(2,1)S(1)} %collective-permute-done.22.refs_1_, ...), custom_call_target="tpu_custom_call" | custom-call | flops 1409286144 | bytes 14155776 | tf_op jit(solution)/shard_map/spread/pallas_call | solution.py:266
  176.4 1.6 collective-permute-start.28
  178.0 0.9 merge.2
  179.1 1.1 collective-permute-start.30
  180.2 1.9 collective-permute-start.29
  182.1 7.1 %dec_grad.1 = f32[21,128,1024]{2,1,0:T(8,128)} custom-call(s32[5]{0:T(128)S(1)} %stack.19.scal, s32[105]{0:T(128)S(1)} %concatenate.29.meta, bf16[21,64,256]{2,1,0:T(8,128)(2,1)S(1)} %pick.2.refs_0_, bf16[21,64,256]{2,1,0:T(8,128)(2,1)S(1)} %collective-permute-done.6.refs_1_, bf16[21,128,128]{2,1,0:T(8,128)(2,1)S(1)} %collective-permute-done.17.refs_2_, ...), custom_call_target="tpu_custom_call" | custom-call | flops 2818572288 | bytes 15204352 | tf_op jit(solution)/shard_map/dec_grad/pallas_call | solution.py:351
  189.2 5.1 %collective-permute-done.28.refs_0_ = bf16[21,64,256]{2,1,0:T(8,128)(2,1)S(1)} collective-permute-done((bf16[21,64,256]{2,1,0:T(8,128)(2,1)S(1)}, bf16[21,64,256]{2,1,0:T(8,128)(2,1)S(1)}, u32[]{:S(2)}, u32[]{:S(2)}) %collective-permute-start.28) | collective-permute-done | bytes 688160 | tf_op jit(solution)/shard_map/ppermute | solution.py:566
  194.3 0.9 merge.3
  195.3 8.3 %collective-permute-done.30 = bf16[8,64,256]{2,1,0:T(8,128)(2,1)S(1)} collective-permute-done((bf16[8,64,256]{2,1,0:T(8,128)(2,1)S(1)}, bf16[8,64,256]{2,1,0:T(8,128)(2,1)S(1)}, u32[]{:S(2)}, u32[]{:S(2)}) %collective-permute-start.30) | collective-permute-done | bytes 262176 | tf_op jit(solution)/shard_map/ppermute | solution.py:451
  203.8 0.6 collective-permute-start.32
  204.4 1.9 collective-permute-start.34
  206.3 2.9 %collective-permute-start.35 = (bf16[8,64,256]{2,1,0:T(8,128)(2,1)S(1)}, bf16[8,64,256]{2,1,0:T(8,128)(2,1)S(1)}, u32[]{:S(2)}, u32[]{:S(2)}) collective-permute-start(bf16[8,64,256]{2,1,0:T(8,128)(2,1)S(1)} %get-tuple-element.127), channel_id=1, source_target_pairs={{0,12},{4,0},{8,4},{12,8},{1,13},{5,1},{9,5},{13,9},{2,14},{6,2},{... | collective-permute-start | bytes 786440 | tf_op jit(solution)/shard_map/ppermute | solution.py:451
  209.2 2.5 %collective-permute-done.32 = bf16[8,64,256]{2,1,0:T(8,128)(2,1)S(1)} collective-permute-done((bf16[8,64,256]{2,1,0:T(8,128)(2,1)S(1)}, bf16[8,64,256]{2,1,0:T(8,128)(2,1)S(1)}, u32[]{:S(2)}, u32[]{:S(2)}) %collective-permute-start.32) | collective-permute-done | bytes 262176 | tf_op jit(solution)/shard_map/ppermute | solution.py:610
  211.8 3.7 %collective-permute-done.33 = bf16[8,64,256]{2,1,0:T(8,128)(2,1)S(1)} collective-permute-done((bf16[8,64,256]{2,1,0:T(8,128)(2,1)S(1)}, bf16[8,64,256]{2,1,0:T(8,128)(2,1)S(1)}, u32[]{:S(2)}, u32[]{:S(2)}) %collective-permute-start.33) | collective-permute-done | bytes 262176 | tf_op jit(solution)/shard_map/ppermute | solution.py:451
  215.5 9.7 %collective-permute-done.34 = bf16[8,64,256]{2,1,0:T(8,128)(2,1)S(1)} collective-permute-done((bf16[8,64,256]{2,1,0:T(8,128)(2,1)S(1)}, bf16[8,64,256]{2,1,0:T(8,128)(2,1)S(1)}, u32[]{:S(2)}, u32[]{:S(2)}) %collective-permute-start.34) | collective-permute-done | bytes 262176 | tf_op jit(solution)/shard_map/ppermute | solution.py:451
  225.5 1.6 collective-permute-start.38
  227.1 0.5 collective-permute-start.37
  227.7 3.6 %collective-permute-done.39.refs_5_ = bf16[4,64,256]{2,1,0:T(8,128)(2,1)S(1)} collective-permute-done((bf16[4,64,256]{2,1,0:T(8,128)(2,1)S(1)}, bf16[4,64,256]{2,1,0:T(8,128)(2,1)S(1)}, u32[]{:S(2)}, u32[]{:S(2)}) %collective-permute-start.39) | collective-permute-done | bytes 131104 | tf_op jit(solution)/shard_map/ppermute | solution.py:630
  231.3 2.9 %collective-permute-done.37.refs_2_ = bf16[4,64,256]{2,1,0:T(8,128)(2,1)S(1)} collective-permute-done((bf16[4,64,256]{2,1,0:T(8,128)(2,1)S(1)}, bf16[4,64,256]{2,1,0:T(8,128)(2,1)S(1)}, u32[]{:S(2)}, u32[]{:S(2)}) %collective-permute-start.37) | collective-permute-done | bytes 131104 | tf_op jit(solution)/shard_map/ppermute | solution.py:630
  234.1 3.3 %enc_grad.1 = (f32[1024,1024]{1,0:T(8,128)}, f32[4,1,256]{2,1,0:T(1,128)}) custom-call(bf16[1024,512]{1,0:T(8,128)(2,1)S(1)} %bitcast.70, bf16[4,128,256]{2,1,0:T(8,128)(2,1)S(1)} %get-tuple-element.160.refs_0_, bf16[4,64,256]{2,1,0:T(8,128)(2,1)S(1)} %get-tuple-element.162.refs_1_, bf16[4,64,256]{2,1,0:T(8,128)(2,1)S(1)} %collective-permute-done.37.refs_2_, ...), custom_call_target="tpu_custom_call" | custom-call | flops 1073741824 | bytes 6291456 | tf_op jit(solution)/shard_map/enc_grad/pallas_call | solution.py:379
  (80 shorter events, 3.4 us)
Async XLA Ops:
  0.7 6.6 %copy-start.8 = (s32[21,3]{0,1:T(4,128)S(1)}, s32[21,3]{0,1:T(4,128)}, u32[]{:S(2)}) copy-start(s32[21,3]{0,1:T(4,128)} %param.12) | copy-start | bytes 760
  0.7 6.7 %copy-start.7 = (s32[256,8]{0,1:T(8,128)S(1)}, s32[256,8]{0,1:T(8,128)}, u32[]{:S(2)}) copy-start(s32[256,8]{0,1:T(8,128)} %param.11) | copy-start | bytes 24580
  4.3 10.1 %collective-permute-start = (bf16[8,64,256]{2,1,0:T(8,128)(2,1)S(1)}, bf16[8,64,256]{2,1,0:T(8,128)(2,1)S(1)}, u32[]{:S(2)}, u32[]{:S(2)}) collective-permute-start(bf16[8,64,256]{2,1,0:T(8,128)(2,1)S(1)} %get-tuple-element.70), channel_id=1, source_target_pairs={{0,2},{2,0},{1,3},{3,1},{4,6},{6,4},{5,7},{7,5},{8,10},{10,8},{9,1... | collective-permute-start | bytes 786440 | tf_op jit(solution)/shard_map/ppermute | solution.py:469
  7.3 23.5 %collective-permute-start.2 = (bf16[8,64,256]{2,1,0:T(8,128)(2,1)S(1)}, bf16[8,64,256]{2,1,0:T(8,128)(2,1)S(1)}, u32[]{:S(2)}, u32[]{:S(2)}) collective-permute-start(bf16[8,64,256]{2,1,0:T(8,128)(2,1)S(1)} %get-tuple-element.73), channel_id=1, source_target_pairs={{0,2},{2,0},{1,3},{3,1},{4,6},{6,4},{5,7},{7,5},{8,10},{10,8},{9,1... | collective-permute-start | bytes 786440 | tf_op jit(solution)/shard_map/ppermute | solution.py:469
  7.6 7.0 %copy-start.3 = (f32[2048]{0:T(1024)S(1)}, f32[2048]{0:T(1024)}, u32[]{:S(2)}) copy-start(f32[2048]{0:T(1024)} %param.10) | copy-start | bytes 24580
  15.0 0.8 copy-start.1
  15.8 15.0 %collective-permute-start.5 = (bf16[8,64,256]{2,1,0:T(8,128)(2,1)S(1)}, bf16[8,64,256]{2,1,0:T(8,128)(2,1)S(1)}, u32[]{:S(2)}, u32[]{:S(2)}) collective-permute-start(bf16[8,64,256]{2,1,0:T(8,128)(2,1)S(1)} %get-tuple-element.79.refs_0_), channel_id=1, source_target_pairs={{0,12},{4,0},{8,4},{12,8},{1,13},{5,1},{9,5},{13,9},{2,14},{6,2},{... | collective-permute-start | bytes 786440 | tf_op jit(solution)/shard_map/ppermute | solution.py:451
  20.0 20.6 %collective-permute-start.4 = (bf16[8,64,256]{2,1,0:T(8,128)(2,1)S(1)}, bf16[8,64,256]{2,1,0:T(8,128)(2,1)S(1)}, u32[]{:S(2)}, u32[]{:S(2)}) collective-permute-start(bf16[8,64,256]{2,1,0:T(8,128)(2,1)S(1)} %get-tuple-element.79.refs_0_), channel_id=1, source_target_pairs={{0,8},{4,12},{8,0},{12,4},{1,9},{5,13},{9,1},{13,5},{2,10},{6,14},... | collective-permute-start | bytes 786440 | tf_op jit(solution)/shard_map/ppermute | solution.py:451
  20.0 20.6 %collective-permute-start.3 = (bf16[8,64,256]{2,1,0:T(8,128)(2,1)S(1)}, bf16[8,64,256]{2,1,0:T(8,128)(2,1)S(1)}, u32[]{:S(2)}, u32[]{:S(2)}) collective-permute-start(bf16[8,64,256]{2,1,0:T(8,128)(2,1)S(1)} %get-tuple-element.79.refs_0_), channel_id=1, source_target_pairs={{0,4},{4,8},{8,12},{12,0},{1,5},{5,9},{9,13},{13,1},{2,6},{6,10},{... | collective-permute-start | bytes 786440 | tf_op jit(solution)/shard_map/ppermute | solution.py:451
  23.4 3.4 %collective-permute-start.1 = (bf16[256,1024]{0,1:T(8,128)(2,1)S(1)}, bf16[256,1024]{0,1:T(8,128)(2,1)}, u32[]{:S(2)}, u32[]{:S(2)}) collective-permute-start(bf16[256,1024]{0,1:T(8,128)(2,1)S(1)} %pad_maximum_fusion.2), channel_id=1, source_target_pairs={{0,1},{1,0},{2,3},{3,2},{4,5},{5,4},{6,7},{7,6},{8,9},{9,8},{10,11... | collective-permute-start | bytes 1572872 | tf_op jit(solution)/shard_map/ppermute | solution.py:483
  43.0 14.8 %collective-permute-start.6 = (bf16[21,64,256]{2,1,0:T(8,128)(2,1)S(1)}, bf16[21,64,256]{2,1,0:T(8,128)(2,1)S(1)}, u32[]{:S(2)}, u32[]{:S(2)}) collective-permute-start(bf16[21,64,256]{2,1,0:T(8,128)(2,1)S(1)} %pick.2.refs_0_), channel_id=1, source_target_pairs={{0,2},{2,0},{1,3},{3,1},{4,6},{6,4},{5,7},{7,5},{8,10},{10,8},{9,1... | collective-permute-start | bytes 2064392 | tf_op jit(solution)/shard_map/ppermute | solution.py:522
  45.2 18.9 %collective-permute-start.9 = (bf16[8,64,256]{2,1,0:T(8,128)(2,1)S(1)}, bf16[8,64,256]{2,1,0:T(8,128)(2,1)S(1)}, u32[]{:S(2)}, u32[]{:S(2)}) collective-permute-start(bf16[8,64,256]{2,1,0:T(8,128)(2,1)S(1)} %get-tuple-element.88.refs_0_), channel_id=1, source_target_pairs={{0,12},{4,0},{8,4},{12,8},{1,13},{5,1},{9,5},{13,9},{2,14},{6,2},{... | collective-permute-start | bytes 786440 | tf_op jit(solution)/shard_map/ppermute | solution.py:451
  45.2 24.7 %collective-permute-start.8 = (bf16[8,64,256]{2,1,0:T(8,128)(2,1)S(1)}, bf16[8,64,256]{2,1,0:T(8,128)(2,1)S(1)}, u32[]{:S(2)}, u32[]{:S(2)}) collective-permute-start(bf16[8,64,256]{2,1,0:T(8,128)(2,1)S(1)} %get-tuple-element.88.refs_0_), channel_id=1, source_target_pairs={{0,8},{4,12},{8,0},{12,4},{1,9},{5,13},{9,1},{13,5},{2,10},{6,14},... | collective-permute-start | bytes 786440 | tf_op jit(solution)/shard_map/ppermute | solution.py:451
  47.8 22.2 %collective-permute-start.7 = (bf16[8,64,256]{2,1,0:T(8,128)(2,1)S(1)}, bf16[8,64,256]{2,1,0:T(8,128)(2,1)S(1)}, u32[]{:S(2)}, u32[]{:S(2)}) collective-permute-start(bf16[8,64,256]{2,1,0:T(8,128)(2,1)S(1)} %get-tuple-element.88.refs_0_), channel_id=1, source_target_pairs={{0,4},{4,8},{8,12},{12,0},{1,5},{5,9},{9,13},{13,1},{2,6},{6,10},{... | collective-permute-start | bytes 786440 | tf_op jit(solution)/shard_map/ppermute | solution.py:451
  72.3 21.8 %collective-permute-start.10 = (bf16[21,64,256]{2,1,0:T(8,128)(2,1)S(1)}, bf16[21,64,256]{2,1,0:T(8,128)(2,1)S(1)}, u32[]{:S(2)}, u32[]{:S(2)}) collective-permute-start(bf16[21,64,256]{2,1,0:T(8,128)(2,1)S(1)} %pick.3.refs_0_.refs_3_), channel_id=1, source_target_pairs={{0,2},{2,0},{1,3},{3,1},{4,6},{6,4},{5,7},{7,5},{8,10},{10,8},{9,1... | collective-permute-start | bytes 2064392 | tf_op jit(solution)/shard_map/ppermute | solution.py:522
  72.9 11.3 %collective-permute-start.11 = (bf16[128,1024]{1,0:T(8,128)(2,1)}, bf16[128,1024]{1,0:T(8,128)(2,1)S(1)}, u32[]{:S(2)}, u32[]{:S(2)}) collective-permute-start(bf16[128,1024]{1,0:T(8,128)(2,1)} %get-tuple-element.93), channel_id=1, source_target_pairs={{0,4},{4,8},{8,12},{12,0},{1,5},{5,9},{9,13},{13,1},{2,6},{6,10},{... | collective-permute-start | bytes 786440 | tf_op jit(solution)/shard_map/ppermute | solution.py:451
  72.9 19.8 %collective-permute-start.12 = (bf16[128,1024]{1,0:T(8,128)(2,1)}, bf16[128,1024]{1,0:T(8,128)(2,1)}, u32[]{:S(2)}, u32[]{:S(2)}) collective-permute-start(bf16[128,1024]{1,0:T(8,128)(2,1)} %get-tuple-element.94), channel_id=1, source_target_pairs={{0,8},{4,12},{8,0},{12,4},{1,9},{5,13},{9,1},{13,5},{2,10},{6,14},... | collective-permute-start | bytes 786440 | tf_op jit(solution)/shard_map/ppermute | solution.py:451
  72.9 19.8 %collective-permute-start.13 = (bf16[128,1024]{1,0:T(8,128)(2,1)}, bf16[128,1024]{1,0:T(8,128)(2,1)}, u32[]{:S(2)}, u32[]{:S(2)}) collective-permute-start(bf16[128,1024]{1,0:T(8,128)(2,1)} %get-tuple-element.95), channel_id=1, source_target_pairs={{0,12},{4,0},{8,4},{12,8},{1,13},{5,1},{9,5},{13,9},{2,14},{6,2},{... | collective-permute-start | bytes 786440 | tf_op jit(solution)/shard_map/ppermute | solution.py:451
  76.7 16.0 %copy-start.4 = (bf16[128,1024]{1,0:T(8,128)(2,1)S(1)}, bf16[128,1024]{1,0:T(8,128)(2,1)}, u32[]{:S(2)}) copy-start(bf16[128,1024]{1,0:T(8,128)(2,1)} %get-tuple-element.92) | copy-start | bytes 786436
  76.9 29.5 %collective-permute-start.17 = (bf16[21,128,128]{2,1,0:T(8,128)(2,1)S(1)}, bf16[21,128,128]{2,1,0:T(8,128)(2,1)S(1)}, u32[]{:S(2)}, u32[]{:S(2)}) collective-permute-start(bf16[21,128,128]{2,1,0:T(8,128)(2,1)S(1)} %fusion.1), channel_id=1, source_target_pairs={{0,1},{1,0},{2,3},{3,2},{4,5},{5,4},{6,7},{7,6},{8,9},{9,8},{10,11... | collective-permute-start | bytes 2064392 | tf_op jit(solution)/shard_map/ppermute | solution.py:536
  84.2 8.5 %copy-start.6 = (bf16[128,1024]{1,0:T(8,128)(2,1)}, bf16[128,1024]{1,0:T(8,128)(2,1)S(1)}, u32[]{:S(2)}) copy-start(bf16[128,1024]{1,0:T(8,128)(2,1)S(1)} %collective-permute-done.11) | copy-start | bytes 786436
  94.1 16.1 %collective-permute-start.16 = (bf16[128,1024]{1,0:T(8,128)(2,1)S(1)}, bf16[128,1024]{1,0:T(8,128)(2,1)S(1)}, u32[]{:S(2)}, u32[]{:S(2)}) collective-permute-start(bf16[128,1024]{1,0:T(8,128)(2,1)S(1)} %multiply_convert_fusion.1.refs_0_), channel_id=1, source_target_pairs={{0,12},{4,0},{8,4},{12,8},{1,13},{5,1},{9,5},{13,9},{2,14},{6,2},{... | collective-permute-start | bytes 786440 | tf_op jit(solution)/shard_map/ppermute | solution.py:451
  99.8 33.5 %collective-permute-start.15 = (bf16[128,1024]{1,0:T(8,128)(2,1)S(1)}, bf16[128,1024]{1,0:T(8,128)(2,1)S(1)}, u32[]{:S(2)}, u32[]{:S(2)}) collective-permute-start(bf16[128,1024]{1,0:T(8,128)(2,1)S(1)} %multiply_convert_fusion.1.refs_0_), channel_id=1, source_target_pairs={{0,8},{4,12},{8,0},{12,4},{1,9},{5,13},{9,1},{13,5},{2,10},{6,14},... | collective-permute-start | bytes 786440 | tf_op jit(solution)/shard_map/ppermute | solution.py:451
  100.8 32.6 %collective-permute-start.14 = (bf16[128,1024]{1,0:T(8,128)(2,1)S(1)}, bf16[128,1024]{1,0:T(8,128)(2,1)S(1)}, u32[]{:S(2)}, u32[]{:S(2)}) collective-permute-start(bf16[128,1024]{1,0:T(8,128)(2,1)S(1)} %multiply_convert_fusion.1.refs_0_), channel_id=1, source_target_pairs={{0,4},{4,8},{8,12},{12,0},{1,5},{5,9},{9,13},{13,1},{2,6},{6,10},{... | collective-permute-start | bytes 786440 | tf_op jit(solution)/shard_map/ppermute | solution.py:451
  100.9 68.1 %collective-permute-start.25 = (bf16[21,128,128]{2,1,0:T(8,128)(2,1)S(1)}, bf16[21,128,128]{2,1,0:T(8,128)(2,1)S(1)}, u32[]{:S(2)}, u32[]{:S(2)}) collective-permute-start(bf16[21,128,128]{2,1,0:T(8,128)(2,1)S(1)} %fusion), channel_id=1, source_target_pairs={{0,1},{1,0},{2,3},{3,2},{4,5},{5,4},{6,7},{7,6},{8,9},{9,8},{10,11... | collective-permute-start | bytes 2064392 | tf_op jit(solution)/shard_map/ppermute | solution.py:536
  106.4 35.8 %collective-permute-start.21 = (bf16[128,1024]{1,0:T(8,128)(2,1)S(1)}, bf16[128,1024]{1,0:T(8,128)(2,1)S(1)}, u32[]{:S(2)}, u32[]{:S(2)}) collective-permute-start(bf16[128,1024]{1,0:T(8,128)(2,1)S(1)} %get-tuple-element.152), channel_id=1, source_target_pairs={{0,12},{4,0},{8,4},{12,8},{1,13},{5,1},{9,5},{13,9},{2,14},{6,2},{... | collective-permute-start | bytes 786440 | tf_op jit(solution)/shard_map/ppermute | solution.py:451
  110.2 35.1 %collective-permute-start.20 = (bf16[128,1024]{1,0:T(8,128)(2,1)S(1)}, bf16[128,1024]{1,0:T(8,128)(2,1)S(1)}, u32[]{:S(2)}, u32[]{:S(2)}) collective-permute-start(bf16[128,1024]{1,0:T(8,128)(2,1)S(1)} %get-tuple-element.153), channel_id=1, source_target_pairs={{0,8},{4,12},{8,0},{12,4},{1,9},{5,13},{9,1},{13,5},{2,10},{6,14},... | collective-permute-start | bytes 786440 | tf_op jit(solution)/shard_map/ppermute | solution.py:451
  133.3 12.1 %copy-start.5 = (bf16[128,1024]{1,0:T(8,128)(2,1)S(1)}, bf16[128,1024]{1,0:T(8,128)(2,1)}, u32[]{:S(2)}) copy-start(bf16[128,1024]{1,0:T(8,128)(2,1)} %constant_dynamic-slice_fusion.3) | copy-start | bytes 786436
  133.3 12.1 %collective-permute-start.19 = (bf16[128,1024]{1,0:T(8,128)(2,1)S(1)}, bf16[128,1024]{1,0:T(8,128)(2,1)S(1)}, u32[]{:S(2)}, u32[]{:S(2)}) collective-permute-start(bf16[128,1024]{1,0:T(8,128)(2,1)S(1)} %get-tuple-element.154), channel_id=1, source_target_pairs={{0,4},{4,8},{8,12},{12,0},{1,5},{5,9},{9,13},{13,1},{2,6},{6,10},{... | collective-permute-start | bytes 786440 | tf_op jit(solution)/shard_map/ppermute | solution.py:451
  140.6 28.4 %collective-permute-start.18 = (bf16[21,64,256]{2,1,0:T(8,128)(2,1)S(1)}, bf16[21,64,256]{2,1,0:T(8,128)(2,1)S(1)}, u32[]{:S(2)}, u32[]{:S(2)}) collective-permute-start(bf16[21,64,256]{2,1,0:T(8,128)(2,1)S(1)} %get-tuple-element.105), channel_id=1, source_target_pairs={{0,2},{2,0},{1,3},{3,1},{4,6},{6,4},{5,7},{7,5},{8,10},{10,8},{9,1... | collective-permute-start | bytes 2064392 | tf_op jit(solution)/shard_map/ppermute | solution.py:566
  145.6 7.5 %collective-permute-start.24 = (bf16[128,1024]{1,0:T(8,128)(2,1)S(1)}, bf16[128,1024]{1,0:T(8,128)(2,1)S(1)}, u32[]{:S(2)}, u32[]{:S(2)}) collective-permute-start(bf16[128,1024]{1,0:T(8,128)(2,1)S(1)} %fusion.6.refs_0_), channel_id=1, source_target_pairs={{0,12},{4,0},{8,4},{12,8},{1,13},{5,1},{9,5},{13,9},{2,14},{6,2},{... | collective-permute-start | bytes 786440 | tf_op jit(solution)/shard_map/ppermute | solution.py:451
  146.3 22.7 %collective-permute-start.23 = (bf16[128,1024]{1,0:T(8,128)(2,1)S(1)}, bf16[128,1024]{1,0:T(8,128)(2,1)S(1)}, u32[]{:S(2)}, u32[]{:S(2)}) collective-permute-start(bf16[128,1024]{1,0:T(8,128)(2,1)S(1)} %fusion.6.refs_0_), channel_id=1, source_target_pairs={{0,8},{4,12},{8,0},{12,4},{1,9},{5,13},{9,1},{13,5},{2,10},{6,14},... | collective-permute-start | bytes 786440 | tf_op jit(solution)/shard_map/ppermute | solution.py:451
  146.6 22.4 %collective-permute-start.22 = (bf16[128,1024]{1,0:T(8,128)(2,1)S(1)}, bf16[128,1024]{1,0:T(8,128)(2,1)S(1)}, u32[]{:S(2)}, u32[]{:S(2)}) collective-permute-start(bf16[128,1024]{1,0:T(8,128)(2,1)S(1)} %fusion.6.refs_0_), channel_id=1, source_target_pairs={{0,4},{4,8},{8,12},{12,0},{1,5},{5,9},{9,13},{13,1},{2,6},{6,10},{... | collective-permute-start | bytes 786440 | tf_op jit(solution)/shard_map/ppermute | solution.py:451
  153.1 27.0 %collective-permute-start.26 = (bf16[4,128,1024]{2,1,0:T(8,128)(2,1)S(1)}, bf16[4,128,1024]{2,1,0:T(8,128)(2,1)S(1)}, u32[]{:S(2)}, u32[]{:S(2)}) collective-permute-start(bf16[4,128,1024]{2,1,0:T(8,128)(2,1)S(1)} %get-tuple-element.116.refs_6_), channel_id=1, source_target_pairs={{0,1},{1,0},{2,3},{3,2},{4,5},{5,4},{6,7},{7,6},{8,9},{9,8},{10,11... | collective-permute-start | bytes 3145736 | tf_op jit(solution)/shard_map/ppermute | solution.py:574
  176.3 5.8 %collective-permute-start.27 = (bf16[4,128,1024]{2,1,0:T(8,128)(2,1)S(1)}, bf16[4,128,1024]{2,1,0:T(8,128)(2,1)S(1)}, u32[]{:S(2)}, u32[]{:S(2)}) collective-permute-start(bf16[4,128,1024]{2,1,0:T(8,128)(2,1)S(1)} %get-tuple-element.117.refs_8_), channel_id=1, source_target_pairs={{0,1},{1,0},{2,3},{3,2},{4,5},{5,4},{6,7},{7,6},{8,9},{9,8},{10,11... | collective-permute-start | bytes 3145736 | tf_op jit(solution)/shard_map/ppermute | solution.py:574
  176.4 17.9 %collective-permute-start.28 = (bf16[21,64,256]{2,1,0:T(8,128)(2,1)S(1)}, bf16[21,64,256]{2,1,0:T(8,128)(2,1)S(1)}, u32[]{:S(2)}, u32[]{:S(2)}) collective-permute-start(bf16[21,64,256]{2,1,0:T(8,128)(2,1)S(1)} %get-tuple-element.118), channel_id=1, source_target_pairs={{0,2},{2,0},{1,3},{3,1},{4,6},{6,4},{5,7},{7,5},{8,10},{10,8},{9,1... | collective-permute-start | bytes 2064392 | tf_op jit(solution)/shard_map/ppermute | solution.py:566
  179.0 16.3 %collective-permute-start.31 = (bf16[8,64,256]{2,1,0:T(8,128)(2,1)S(1)}, bf16[8,64,256]{2,1,0:T(8,128)(2,1)S(1)}, u32[]{:S(2)}, u32[]{:S(2)}) collective-permute-start(bf16[8,64,256]{2,1,0:T(8,128)(2,1)S(1)} %get-tuple-element.145), channel_id=1, source_target_pairs={{0,12},{4,0},{8,4},{12,8},{1,13},{5,1},{9,5},{13,9},{2,14},{6,2},{... | collective-permute-start | bytes 786440 | tf_op jit(solution)/shard_map/ppermute | solution.py:451
  179.1 24.5 %collective-permute-start.30 = (bf16[8,64,256]{2,1,0:T(8,128)(2,1)S(1)}, bf16[8,64,256]{2,1,0:T(8,128)(2,1)S(1)}, u32[]{:S(2)}, u32[]{:S(2)}) collective-permute-start(bf16[8,64,256]{2,1,0:T(8,128)(2,1)S(1)} %get-tuple-element.146), channel_id=1, source_target_pairs={{0,8},{4,12},{8,0},{12,4},{1,9},{5,13},{9,1},{13,5},{2,10},{6,14},... | collective-permute-start | bytes 786440 | tf_op jit(solution)/shard_map/ppermute | solution.py:451
  180.2 23.4 %collective-permute-start.29 = (bf16[8,64,256]{2,1,0:T(8,128)(2,1)S(1)}, bf16[8,64,256]{2,1,0:T(8,128)(2,1)S(1)}, u32[]{:S(2)}, u32[]{:S(2)}) collective-permute-start(bf16[8,64,256]{2,1,0:T(8,128)(2,1)S(1)} %get-tuple-element.147), channel_id=1, source_target_pairs={{0,4},{4,8},{8,12},{12,0},{1,5},{5,9},{9,13},{13,1},{2,6},{6,10},{... | collective-permute-start | bytes 786440 | tf_op jit(solution)/shard_map/ppermute | solution.py:451
  194.3 9.3 %copy-start.2 = (f32[8,64,256]{2,1,0:T(8,128)S(1)}, f32[8,64,256]{2,1,0:T(8,128)}, u32[]{:S(2)}) copy-start(f32[8,64,256]{2,1,0:T(8,128)} %copy-done.1) | copy-start | bytes 1572868
  203.8 30.3 %copy-start = (bf16[512,1024]{0,1:T(8,128)(2,1)S(1)}, bf16[512,1024]{0,1:T(8,128)(2,1)}, u32[]{:S(2)}) copy-start(bf16[512,1024]{0,1:T(8,128)(2,1)} %concatenate.26) | copy-start | bytes 3145732
  203.8 7.9 %collective-permute-start.32 = (bf16[8,64,256]{2,1,0:T(8,128)(2,1)S(1)}, bf16[8,64,256]{2,1,0:T(8,128)(2,1)S(1)}, u32[]{:S(2)}, u32[]{:S(2)}) collective-permute-start(bf16[8,64,256]{2,1,0:T(8,128)(2,1)S(1)} %fusion.10), channel_id=1, source_target_pairs={{0,2},{2,0},{1,3},{3,1},{4,6},{6,4},{5,7},{7,5},{8,10},{10,8},{9,1... | collective-permute-start | bytes 786440 | tf_op jit(solution)/shard_map/ppermute | solution.py:610
  204.4 11.1 %collective-permute-start.33 = (bf16[8,64,256]{2,1,0:T(8,128)(2,1)S(1)}, bf16[8,64,256]{2,1,0:T(8,128)(2,1)S(1)}, u32[]{:S(2)}, u32[]{:S(2)}) collective-permute-start(bf16[8,64,256]{2,1,0:T(8,128)(2,1)S(1)} %get-tuple-element.125), channel_id=1, source_target_pairs={{0,4},{4,8},{8,12},{12,0},{1,5},{5,9},{9,13},{13,1},{2,6},{6,10},{... | collective-permute-start | bytes 786440 | tf_op jit(solution)/shard_map/ppermute | solution.py:451
  204.4 20.8 %collective-permute-start.34 = (bf16[8,64,256]{2,1,0:T(8,128)(2,1)S(1)}, bf16[8,64,256]{2,1,0:T(8,128)(2,1)S(1)}, u32[]{:S(2)}, u32[]{:S(2)}) collective-permute-start(bf16[8,64,256]{2,1,0:T(8,128)(2,1)S(1)} %get-tuple-element.126), channel_id=1, source_target_pairs={{0,8},{4,12},{8,0},{12,4},{1,9},{5,13},{9,1},{13,5},{2,10},{6,14},... | collective-permute-start | bytes 786440 | tf_op jit(solution)/shard_map/ppermute | solution.py:451
  206.3 18.9 %collective-permute-start.35 = (bf16[8,64,256]{2,1,0:T(8,128)(2,1)S(1)}, bf16[8,64,256]{2,1,0:T(8,128)(2,1)S(1)}, u32[]{:S(2)}, u32[]{:S(2)}) collective-permute-start(bf16[8,64,256]{2,1,0:T(8,128)(2,1)S(1)} %get-tuple-element.127), channel_id=1, source_target_pairs={{0,12},{4,0},{8,4},{12,8},{1,13},{5,1},{9,5},{13,9},{2,14},{6,2},{... | collective-permute-start | bytes 786440 | tf_op jit(solution)/shard_map/ppermute | solution.py:451
  211.8 13.5 %collective-permute-start.36 = (bf16[4,128,256]{2,1,0:T(8,128)(2,1)S(1)}, bf16[4,128,256]{2,1,0:T(8,128)(2,1)S(1)}, u32[]{:S(2)}, u32[]{:S(2)}) collective-permute-start(bf16[4,128,256]{2,1,0:T(8,128)(2,1)S(1)} %get-tuple-element.159), channel_id=1, source_target_pairs={{0,1},{1,0},{2,3},{3,2},{4,5},{5,4},{6,7},{7,6},{8,9},{9,8},{10,11... | collective-permute-start | bytes 786440 | tf_op jit(solution)/shard_map/ppermute | solution.py:616
  225.4 5.8 %collective-permute-start.39 = (bf16[4,64,256]{2,1,0:T(8,128)(2,1)S(1)}, bf16[4,64,256]{2,1,0:T(8,128)(2,1)S(1)}, u32[]{:S(2)}, u32[]{:S(2)}) collective-permute-start(bf16[4,64,256]{2,1,0:T(8,128)(2,1)S(1)} %get-tuple-element.161), channel_id=1, source_target_pairs={{0,3},{1,2},{2,1},{3,0},{4,7},{5,6},{6,5},{7,4},{8,11},{9,10},{10,... | collective-permute-start | bytes 393224 | tf_op jit(solution)/shard_map/ppermute | solution.py:630
  225.5 5.7 %collective-permute-start.38 = (bf16[4,64,256]{2,1,0:T(8,128)(2,1)S(1)}, bf16[4,64,256]{2,1,0:T(8,128)(2,1)S(1)}, u32[]{:S(2)}, u32[]{:S(2)}) collective-permute-start(bf16[4,64,256]{2,1,0:T(8,128)(2,1)S(1)} %get-tuple-element.161), channel_id=1, source_target_pairs={{0,1},{1,0},{2,3},{3,2},{4,5},{5,4},{6,7},{7,6},{8,9},{9,8},{10,11... | collective-permute-start | bytes 393224 | tf_op jit(solution)/shard_map/ppermute | solution.py:630
  227.1 7.0 %collective-permute-start.37 = (bf16[4,64,256]{2,1,0:T(8,128)(2,1)S(1)}, bf16[4,64,256]{2,1,0:T(8,128)(2,1)S(1)}, u32[]{:S(2)}, u32[]{:S(2)}) collective-permute-start(bf16[4,64,256]{2,1,0:T(8,128)(2,1)S(1)} %get-tuple-element.162.refs_1_), channel_id=1, source_target_pairs={{0,2},{1,3},{2,0},{3,1},{4,6},{5,7},{6,4},{7,5},{8,10},{9,11},{10,... | collective-permute-start | bytes 393224 | tf_op jit(solution)/shard_map/ppermute | solution.py:630

commit v5 on v4

--- a/solution.py
+++ b/solution.py
@@ -368,22 +368,27 @@
 
 def enc_grad_kernel(count, acts, *refs):
     grads, out, bias = refs[:count], refs[count], refs[count + 1]
-    tokens = jnp.concatenate([g[0] for g in grads], axis=0)
-    out[...] = jnp.dot(acts[...], tokens, preferred_element_type=F32)
-    bias[0] = jnp.sum(tokens.astype(F32), axis=0, keepdims=True)
+    per, _, block = grads[0].shape
+    for b in range(per):
+        tokens = jnp.concatenate([g[b] for g in grads], axis=0)
+        out[:, b * block : (b + 1) * block] = jnp.dot(
+            acts[...], tokens, preferred_element_type=F32
+        )
+        bias[b] = jnp.sum(tokens.astype(F32), axis=0, keepdims=True)
 
 
 def enc_grad(acts_t, grads):
     d, tok = acts_t.shape
     blocks, _, block = grads[0].shape
+    per = divisor(blocks, 2)
     out, bias = pl.pallas_call(
         functools.partial(enc_grad_kernel, len(grads)),
-        grid=(blocks,),
+        grid=(blocks // per,),
         in_specs=[whole((d, tok))]
-        + [pl.BlockSpec((1, g.shape[1], block), lambda b: (b, 0, 0)) for g in grads],
+        + [pl.BlockSpec((per, g.shape[1], block), lambda b: (b, 0, 0)) for g in grads],
         out_specs=[
-            pl.BlockSpec((d, block), lambda b: (0, b)),
-            pl.BlockSpec((1, 1, block), lambda b: (b, 0, 0)),
+            pl.BlockSpec((d, per * block), lambda b: (0, b)),
+            pl.BlockSpec((per, 1, block), lambda b: (b, 0, 0)),
         ],
         out_shape=[
             jax.ShapeDtypeStruct((d, blocks * block), F32),

time: 240 us -> 240 us (level)
  no operation moved by 1% of the time
where the time goes in v5:
time: 240 us; the launch traced here: 237 us
  waiting for transfers between devices  117 us (49%)
  starting transfers between devices  55 us (23%)
  Pallas kernels  49.6 us (21%)
  local copies, waits for them, and re-layouts  11.7 us (5%)
  other arithmetic  2.89 us (1%)
    ppermute x24, waiting for transfers between devices, to_each(): lax.ppermute(parts[m], 'lay', ring_shift('lay', m))  91.2 us
    ppermute x24, starting transfers between devices, to_each(): lax.ppermute(parts[m], 'lay', ring_shift('lay', m))  43.5 us
    pallas_call x2, Pallas kernels, spread(): pl.pallas_call(functools.partial(spread_kernel, slots, per, width, len(pa...  14.6 us
    pallas_call x2, Pallas kernels, decode(): pl.pallas_call(functools.partial(decode_kernel, slots, per, len(lats), la...  10.6 us
    ppermute x2, waiting for transfers between devices, local(): lax.ppermute(mine, 'wid', ring_shift('wid', -m))  8.07 us
    pallas_call x1, Pallas kernels, dec_grad(): pl.pallas_call(functools.partial(dec_grad_kernel, slots, per, len(lats),...  7.08 us
    pallas_call x2, Pallas kernels, encode(): pl.pallas_call(functools.partial(encode_kernel, pieces, chunks), in_specs...  7.06 us
    ppermute x3, waiting for transfers between devices, local(): moved = lax.ppermute(sent, ('wid', 'rep'), pairs)  6.46 us
  transfers between devices with their start and end apart: 40, of which 17 were waited for; matrix products, arithmetic and copies ran while one was open for 6% of the time, Pallas kernels for 16%

profile of v5, /device:TPU:0, one launch (start us, length us, event | category | flops | bytes accessed | tf_op | source)
XLA Modules:
  0.0 236.9 jit_solution(10245415035292112050)
XLA Ops:
  0.7 3.5 %encode.3 = (bf16[8,64,256]{2,1,0:T(8,128)(2,1)S(1)}, bf16[8,64,256]{2,1,0:T(8,128)(2,1)S(1)}) custom-call(s32[5]{0:T(128)S(1)} %stack.19.scal, bf16[4,256,1024]{2,1,0:T(8,128)(2,1)} %acts.3, bf16[1024,2048]{1,0:T(8,128)(2,1)} %weight.3), custom_call_target="tpu_custom_call" | custom-call | flops 536870912 | bytes 4194304 | tf_op jit(solution)/shard_map/encode/pallas_call | solution.py:111
  4.3 3.0 %collective-permute-start = (bf16[8,64,256]{2,1,0:T(8,128)(2,1)S(1)}, bf16[8,64,256]{2,1,0:T(8,128)(2,1)S(1)}, u32[]{:S(2)}, u32[]{:S(2)}) collective-permute-start(bf16[8,64,256]{2,1,0:T(8,128)(2,1)S(1)} %get-tuple-element.70), channel_id=1, source_target_pairs={{0,2},{2,0},{1,3},{3,1},{4,6},{6,4},{5,7},{7,5},{8,10},{10,8},{9,1... | collective-permute-start | bytes 786440 | tf_op jit(solution)/shard_map/ppermute | solution.py:474
  7.6 3.5 %encode.2 = (f32[8,64,256]{2,1,0:T(8,128)S(1)}, f32[8,64,256]{2,1,0:T(8,128)S(1)}) custom-call(s32[5]{0:T(128)S(1)} %stack.19.scal, bf16[4,256,1024]{2,1,0:T(8,128)(2,1)} %acts.3, bf16[1024,2048]{1,0:T(8,128)(2,1)} %weight.3), custom_call_target="tpu_custom_call" | custom-call | flops 536870912 | bytes 4194304 | tf_op jit(solution)/shard_map/encode/pallas_call | solution.py:111
  11.2 3.2 %collective-permute-done.refs_0_ = bf16[8,64,256]{2,1,0:T(8,128)(2,1)S(1)} collective-permute-done((bf16[8,64,256]{2,1,0:T(8,128)(2,1)S(1)}, bf16[8,64,256]{2,1,0:T(8,128)(2,1)S(1)}, u32[]{:S(2)}, u32[]{:S(2)}) %collective-permute-start) | collective-permute-done | bytes 262176 | tf_op jit(solution)/shard_map/ppermute | solution.py:474
  14.6 0.4 gate.2
  15.0 0.8 copy-done.1
  15.8 4.2 %collective-permute-start.5 = (bf16[8,64,256]{2,1,0:T(8,128)(2,1)S(1)}, bf16[8,64,256]{2,1,0:T(8,128)(2,1)S(1)}, u32[]{:S(2)}, u32[]{:S(2)}) collective-permute-start(bf16[8,64,256]{2,1,0:T(8,128)(2,1)S(1)} %get-tuple-element.79.refs_0_), channel_id=1, source_target_pairs={{0,12},{4,0},{8,4},{12,8},{1,13},{5,1},{9,5},{13,9},{2,14},{6,2},{... | collective-permute-start | bytes 786440 | tf_op jit(solution)/shard_map/ppermute | solution.py:456
  20.0 1.0 collective-permute-start.3
  21.0 1.2 constant_dynamic-slice_fusion.9
  23.0 0.4 pad_maximum_fusion.2
  23.4 1.7 constant_dynamic-slice_fusion.5
  25.3 0.7 constant_dynamic-slice_fusion.6
  26.1 0.7 constant_dynamic-slice_fusion.3
  26.8 4.0 %concatenate.26 = bf16[512,1024]{0,1:T(8,128)(2,1)} concatenate(bf16[64,1024]{0,1:T(8,128)(2,1)S(1)} %bitcast.80, bf16[64,1024]{0,1:T(8,128)(2,1)S(1)} %bitcast.78, bf16[64,1024]{0,1:T(8,128)(2,1)S(1)} %bitcast.76, bf16[64,1024]{0,1:T(8,128)(2,1)S(1)} %bitcast.74, bf16[256,1024]{0,1:T(8,128)(2,1)} %collective-permute-done.1), dimensions={0} | concatenate | bytes 2097152 | tf_op jit(solution)/shard_map/concatenate | solution.py:490
  30.8 9.9 %collective-permute-done.4.refs_2_ = bf16[8,64,256]{2,1,0:T(8,128)(2,1)S(1)} collective-permute-done((bf16[8,64,256]{2,1,0:T(8,128)(2,1)S(1)}, bf16[8,64,256]{2,1,0:T(8,128)(2,1)S(1)}, u32[]{:S(2)}, u32[]{:S(2)}) %collective-permute-start.4) | collective-permute-done | bytes 262176 | tf_op jit(solution)/shard_map/ppermute | solution.py:456
  40.6 2.4 pick.2.refs_0_
  43.0 1.6 collective-permute-start.6
  44.7 0.4 gate.3
  45.2 2.5 %collective-permute-start.8 = (bf16[8,64,256]{2,1,0:T(8,128)(2,1)S(1)}, bf16[8,64,256]{2,1,0:T(8,128)(2,1)S(1)}, u32[]{:S(2)}, u32[]{:S(2)}) collective-permute-start(bf16[8,64,256]{2,1,0:T(8,128)(2,1)S(1)} %get-tuple-element.88.refs_0_), channel_id=1, source_target_pairs={{0,8},{4,12},{8,0},{12,4},{1,9},{5,13},{9,1},{13,5},{2,10},{6,14},... | collective-permute-start | bytes 786440 | tf_op jit(solution)/shard_map/ppermute | solution.py:456
  47.8 1.9 collective-permute-start.7
  49.7 8.1 %collective-permute-done.6.refs_1_ = bf16[21,64,256]{2,1,0:T(8,128)(2,1)S(1)} collective-permute-done((bf16[21,64,256]{2,1,0:T(8,128)(2,1)S(1)}, bf16[21,64,256]{2,1,0:T(8,128)(2,1)S(1)}, u32[]{:S(2)}, u32[]{:S(2)}) %collective-permute-start.6) | collective-permute-done | bytes 688160 | tf_op jit(solution)/shard_map/ppermute | solution.py:527
  57.8 5.3 %decode.2 = bf16[4,128,1024]{2,1,0:T(8,128)(2,1)S(1)} custom-call(s32[105]{0:T(128)S(1)} %concatenate.29.meta, bf16[21,64,256]{2,1,0:T(8,128)(2,1)S(1)} %pick.2.refs_0_, bf16[21,64,256]{2,1,0:T(8,128)(2,1)S(1)} %collective-permute-done.6.refs_1_, bf16[21,256,1024]{2,1,0:T(8,128)(2,1)} %refs_4_.3), custom_call_target="tpu_custom_call" | custom-call | flops 1409286144 | bytes 12386304 | tf_op jit(solution)/shard_map/decode/pallas_call | solution.py:208
  63.1 1.0 dynamic-slice_bitcast_fusion.10
  64.1 5.8 %collective-permute-done.8.refs_2_ = bf16[8,64,256]{2,1,0:T(8,128)(2,1)S(1)} collective-permute-done((bf16[8,64,256]{2,1,0:T(8,128)(2,1)S(1)}, bf16[8,64,256]{2,1,0:T(8,128)(2,1)S(1)}, u32[]{:S(2)}, u32[]{:S(2)}) %collective-permute-start.8) | collective-permute-done | bytes 262176 | tf_op jit(solution)/shard_map/ppermute | solution.py:456
  69.9 2.4 pick.3.refs_0_.refs_3_
  72.3 0.6 collective-permute-start.10
  72.9 3.8 %collective-permute-start.13 = (bf16[128,1024]{1,0:T(8,128)(2,1)}, bf16[128,1024]{1,0:T(8,128)(2,1)}, u32[]{:S(2)}, u32[]{:S(2)}) collective-permute-start(bf16[128,1024]{1,0:T(8,128)(2,1)} %get-tuple-element.95), channel_id=1, source_target_pairs={{0,12},{4,0},{8,4},{12,8},{1,13},{5,1},{9,5},{13,9},{2,14},{6,2},{... | collective-permute-start | bytes 786440 | tf_op jit(solution)/shard_map/ppermute | solution.py:456
  76.9 7.3 %collective-permute-done.11 = bf16[128,1024]{1,0:T(8,128)(2,1)S(1)} collective-permute-done((bf16[128,1024]{1,0:T(8,128)(2,1)}, bf16[128,1024]{1,0:T(8,128)(2,1)S(1)}, u32[]{:S(2)}, u32[]{:S(2)}) %collective-permute-start.11) | collective-permute-done | bytes 262176 | tf_op jit(solution)/shard_map/ppermute | solution.py:456
  84.2 8.5 %collective-permute-done.12 = bf16[128,1024]{1,0:T(8,128)(2,1)} collective-permute-done((bf16[128,1024]{1,0:T(8,128)(2,1)}, bf16[128,1024]{1,0:T(8,128)(2,1)}, u32[]{:S(2)}, u32[]{:S(2)}) %collective-permute-start.12) | collective-permute-done | bytes 262176 | tf_op jit(solution)/shard_map/ppermute | solution.py:456
  92.7 1.4 multiply_convert_fusion.1.refs_0_
  94.1 5.7 %collective-permute-start.16 = (bf16[128,1024]{1,0:T(8,128)(2,1)S(1)}, bf16[128,1024]{1,0:T(8,128)(2,1)S(1)}, u32[]{:S(2)}, u32[]{:S(2)}) collective-permute-start(bf16[128,1024]{1,0:T(8,128)(2,1)S(1)} %multiply_convert_fusion.1.refs_0_), channel_id=1, source_target_pairs={{0,12},{4,0},{8,4},{12,8},{1,13},{5,1},{9,5},{13,9},{2,14},{6,2},{... | collective-permute-start | bytes 786440 | tf_op jit(solution)/shard_map/ppermute | solution.py:456
  99.8 0.9 collective-permute-start.15
  101.0 5.3 %decode.3 = bf16[4,128,1024]{2,1,0:T(8,128)(2,1)S(1)} custom-call(s32[105]{0:T(128)S(1)} %concatenate.29.meta, bf16[21,64,256]{2,1,0:T(8,128)(2,1)S(1)} %pick.3.refs_0_.refs_3_, bf16[21,64,256]{2,1,0:T(8,128)(2,1)S(1)} %collective-permute-done.10.refs_1_.refs_4_, bf16[21,256,1024]{2,1,0:T(8,128)(2,1)} %refs_4_.3), custom_call_target="tpu_custom_call" | custom-call | flops 1409286144 | bytes 12386304 | tf_op jit(solution)/shard_map/decode/pallas_call | solution.py:208
  106.4 3.9 %collective-permute-start.21 = (bf16[128,1024]{1,0:T(8,128)(2,1)S(1)}, bf16[128,1024]{1,0:T(8,128)(2,1)S(1)}, u32[]{:S(2)}, u32[]{:S(2)}) collective-permute-start(bf16[128,1024]{1,0:T(8,128)(2,1)S(1)} %get-tuple-element.152), channel_id=1, source_target_pairs={{0,12},{4,0},{8,4},{12,8},{1,13},{5,1},{9,5},{13,9},{2,14},{6,2},{... | collective-permute-start | bytes 786440 | tf_op jit(solution)/shard_map/ppermute | solution.py:456
  110.2 8.6 %collective-permute-start.20 = (bf16[128,1024]{1,0:T(8,128)(2,1)S(1)}, bf16[128,1024]{1,0:T(8,128)(2,1)S(1)}, u32[]{:S(2)}, u32[]{:S(2)}) collective-permute-start(bf16[128,1024]{1,0:T(8,128)(2,1)S(1)} %get-tuple-element.153), channel_id=1, source_target_pairs={{0,8},{4,12},{8,0},{12,4},{1,9},{5,13},{9,1},{13,5},{2,10},{6,14},... | collective-permute-start | bytes 786440 | tf_op jit(solution)/shard_map/ppermute | solution.py:456
  118.8 14.5 %collective-permute-done.15.refs_2_ = bf16[128,1024]{1,0:T(8,128)(2,1)S(1)} collective-permute-done((bf16[128,1024]{1,0:T(8,128)(2,1)S(1)}, bf16[128,1024]{1,0:T(8,128)(2,1)S(1)}, u32[]{:S(2)}, u32[]{:S(2)}) %collective-permute-start.15) | collective-permute-done | bytes 262176 | tf_op jit(solution)/shard_map/ppermute | solution.py:456
  133.3 7.3 %spread.2 = (bf16[4,128,1024]{2,1,0:T(8,128)(2,1)S(1)}, f32[33,64,256]{2,1,0:T(8,128)S(1)}, bf16[21,64,256]{2,1,0:T(8,128)(2,1)S(1)}) custom-call(s32[5]{0:T(128)S(1)} %stack.19.scal, s32[105]{0:T(128)S(1)} %concatenate.29.meta, bf16[128,1024]{1,0:T(8,128)(2,1)S(1)} %multiply_convert_fusion.1.refs_0_, bf16[128,1024]{1,0:T(8,128)(2,1)S(1)} %collective-permute-done.14.refs_1_, ...), custom_call_target="tpu_custom_call" | custom-call | flops 1409286144 | bytes 14155776 | tf_op jit(solution)/shard_map/spread/pallas_call | solution.py:266
  140.6 1.6 collective-permute-start.18
  142.2 3.2 %collective-permute-done.20 = bf16[128,1024]{1,0:T(8,128)(2,1)S(1)} collective-permute-done((bf16[128,1024]{1,0:T(8,128)(2,1)S(1)}, bf16[128,1024]{1,0:T(8,128)(2,1)S(1)}, u32[]{:S(2)}, u32[]{:S(2)}) %collective-permute-start.20) | collective-permute-done | bytes 262176 | tf_op jit(solution)/shard_map/ppermute | solution.py:456
  145.6 0.7 collective-permute-start.24
  146.3 0.3 collective-permute-start.23
  146.6 1.9 collective-permute-start.22
  148.6 4.5 %collective-permute-done.24.refs_3_ = bf16[128,1024]{1,0:T(8,128)(2,1)S(1)} collective-permute-done((bf16[128,1024]{1,0:T(8,128)(2,1)S(1)}, bf16[128,1024]{1,0:T(8,128)(2,1)S(1)}, u32[]{:S(2)}, u32[]{:S(2)}) %collective-permute-start.24) | collective-permute-done | bytes 262176 | tf_op jit(solution)/shard_map/ppermute | solution.py:456
  153.1 15.9 %collective-permute-done.23.refs_2_ = bf16[128,1024]{1,0:T(8,128)(2,1)S(1)} collective-permute-done((bf16[128,1024]{1,0:T(8,128)(2,1)S(1)}, bf16[128,1024]{1,0:T(8,128)(2,1)S(1)}, u32[]{:S(2)}, u32[]{:S(2)}) %collective-permute-start.23) | collective-permute-done | bytes 262176 | tf_op jit(solution)/shard_map/ppermute | solution.py:456
  169.0 7.3 %spread.3 = (bf16[4,128,1024]{2,1,0:T(8,128)(2,1)S(1)}, f32[33,64,256]{2,1,0:T(8,128)S(1)}, bf16[21,64,256]{2,1,0:T(8,128)(2,1)S(1)}) custom-call(s32[5]{0:T(128)S(1)} %stack.19.scal, s32[105]{0:T(128)S(1)} %concatenate.29.meta, bf16[128,1024]{1,0:T(8,128)(2,1)S(1)} %fusion.6.refs_0_, bf16[128,1024]{1,0:T(8,128)(2,1)S(1)} %collective-permute-done.22.refs_1_, ...), custom_call_target="tpu_custom_call" | custom-call | flops 1409286144 | bytes 14155776 | tf_op jit(solution)/shard_map/spread/pallas_call | solution.py:266
  176.4 1.6 collective-permute-start.28
  178.0 0.9 merge.2
  179.1 1.1 collective-permute-start.30
  180.2 1.9 collective-permute-start.29
  182.1 7.1 %dec_grad.1 = f32[21,128,1024]{2,1,0:T(8,128)} custom-call(s32[5]{0:T(128)S(1)} %stack.19.scal, s32[105]{0:T(128)S(1)} %concatenate.29.meta, bf16[21,64,256]{2,1,0:T(8,128)(2,1)S(1)} %pick.2.refs_0_, bf16[21,64,256]{2,1,0:T(8,128)(2,1)S(1)} %collective-permute-done.6.refs_1_, bf16[21,128,128]{2,1,0:T(8,128)(2,1)S(1)} %collective-permute-done.17.refs_2_, ...), custom_call_target="tpu_custom_call" | custom-call | flops 2818572288 | bytes 15204352 | tf_op jit(solution)/shard_map/dec_grad/pallas_call | solution.py:351
  189.2 5.1 %collective-permute-done.28.refs_0_ = bf16[21,64,256]{2,1,0:T(8,128)(2,1)S(1)} collective-permute-done((bf16[21,64,256]{2,1,0:T(8,128)(2,1)S(1)}, bf16[21,64,256]{2,1,0:T(8,128)(2,1)S(1)}, u32[]{:S(2)}, u32[]{:S(2)}) %collective-permute-start.28) | collective-permute-done | bytes 688160 | tf_op jit(solution)/shard_map/ppermute | solution.py:571
  194.3 0.9 merge.3
  195.3 8.3 %collective-permute-done.30 = bf16[8,64,256]{2,1,0:T(8,128)(2,1)S(1)} collective-permute-done((bf16[8,64,256]{2,1,0:T(8,128)(2,1)S(1)}, bf16[8,64,256]{2,1,0:T(8,128)(2,1)S(1)}, u32[]{:S(2)}, u32[]{:S(2)}) %collective-permute-start.30) | collective-permute-done | bytes 262176 | tf_op jit(solution)/shard_map/ppermute | solution.py:456
  203.8 0.6 collective-permute-start.32
  204.4 1.9 collective-permute-start.34
  206.3 2.9 %collective-permute-start.35 = (bf16[8,64,256]{2,1,0:T(8,128)(2,1)S(1)}, bf16[8,64,256]{2,1,0:T(8,128)(2,1)S(1)}, u32[]{:S(2)}, u32[]{:S(2)}) collective-permute-start(bf16[8,64,256]{2,1,0:T(8,128)(2,1)S(1)} %get-tuple-element.127), channel_id=1, source_target_pairs={{0,12},{4,0},{8,4},{12,8},{1,13},{5,1},{9,5},{13,9},{2,14},{6,2},{... | collective-permute-start | bytes 786440 | tf_op jit(solution)/shard_map/ppermute | solution.py:456
  209.2 2.5 %collective-permute-done.32 = bf16[8,64,256]{2,1,0:T(8,128)(2,1)S(1)} collective-permute-done((bf16[8,64,256]{2,1,0:T(8,128)(2,1)S(1)}, bf16[8,64,256]{2,1,0:T(8,128)(2,1)S(1)}, u32[]{:S(2)}, u32[]{:S(2)}) %collective-permute-start.32) | collective-permute-done | bytes 262176 | tf_op jit(solution)/shard_map/ppermute | solution.py:615
  211.8 3.7 %collective-permute-done.33 = bf16[8,64,256]{2,1,0:T(8,128)(2,1)S(1)} collective-permute-done((bf16[8,64,256]{2,1,0:T(8,128)(2,1)S(1)}, bf16[8,64,256]{2,1,0:T(8,128)(2,1)S(1)}, u32[]{:S(2)}, u32[]{:S(2)}) %collective-permute-start.33) | collective-permute-done | bytes 262176 | tf_op jit(solution)/shard_map/ppermute | solution.py:456
  215.5 9.7 %collective-permute-done.34 = bf16[8,64,256]{2,1,0:T(8,128)(2,1)S(1)} collective-permute-done((bf16[8,64,256]{2,1,0:T(8,128)(2,1)S(1)}, bf16[8,64,256]{2,1,0:T(8,128)(2,1)S(1)}, u32[]{:S(2)}, u32[]{:S(2)}) %collective-permute-start.34) | collective-permute-done | bytes 262176 | tf_op jit(solution)/shard_map/ppermute | solution.py:456
  225.5 1.6 collective-permute-start.38
  227.1 0.5 collective-permute-start.37
  227.7 3.6 %collective-permute-done.39.refs_5_ = bf16[4,64,256]{2,1,0:T(8,128)(2,1)S(1)} collective-permute-done((bf16[4,64,256]{2,1,0:T(8,128)(2,1)S(1)}, bf16[4,64,256]{2,1,0:T(8,128)(2,1)S(1)}, u32[]{:S(2)}, u32[]{:S(2)}) %collective-permute-start.39) | collective-permute-done | bytes 131104 | tf_op jit(solution)/shard_map/ppermute | solution.py:635
  231.3 2.9 %collective-permute-done.37.refs_2_ = bf16[4,64,256]{2,1,0:T(8,128)(2,1)S(1)} collective-permute-done((bf16[4,64,256]{2,1,0:T(8,128)(2,1)S(1)}, bf16[4,64,256]{2,1,0:T(8,128)(2,1)S(1)}, u32[]{:S(2)}, u32[]{:S(2)}) %collective-permute-start.37) | collective-permute-done | bytes 131104 | tf_op jit(solution)/shard_map/ppermute | solution.py:635
  234.1 2.8 %enc_grad.1 = (f32[1024,1024]{1,0:T(8,128)}, f32[4,1,256]{2,1,0:T(1,128)}) custom-call(bf16[1024,512]{1,0:T(8,128)(2,1)S(1)} %bitcast.70, bf16[4,128,256]{2,1,0:T(8,128)(2,1)S(1)} %get-tuple-element.160.refs_0_, bf16[4,64,256]{2,1,0:T(8,128)(2,1)S(1)} %get-tuple-element.162.refs_1_, bf16[4,64,256]{2,1,0:T(8,128)(2,1)S(1)} %collective-permute-done.37.refs_2_, ...), custom_call_target="tpu_custom_call" | custom-call | flops 1073741824 | bytes 6291456 | tf_op jit(solution)/shard_map/enc_grad/pallas_call | solution.py:384
  (80 shorter events, 3.4 us)
Async XLA Ops:
  0.7 6.6 %copy-start.8 = (s32[21,3]{0,1:T(4,128)S(1)}, s32[21,3]{0,1:T(4,128)}, u32[]{:S(2)}) copy-start(s32[21,3]{0,1:T(4,128)} %param.12) | copy-start | bytes 760
  0.7 6.7 %copy-start.7 = (s32[256,8]{0,1:T(8,128)S(1)}, s32[256,8]{0,1:T(8,128)}, u32[]{:S(2)}) copy-start(s32[256,8]{0,1:T(8,128)} %param.11) | copy-start | bytes 24580
  4.3 10.1 %collective-permute-start = (bf16[8,64,256]{2,1,0:T(8,128)(2,1)S(1)}, bf16[8,64,256]{2,1,0:T(8,128)(2,1)S(1)}, u32[]{:S(2)}, u32[]{:S(2)}) collective-permute-start(bf16[8,64,256]{2,1,0:T(8,128)(2,1)S(1)} %get-tuple-element.70), channel_id=1, source_target_pairs={{0,2},{2,0},{1,3},{3,1},{4,6},{6,4},{5,7},{7,5},{8,10},{10,8},{9,1... | collective-permute-start | bytes 786440 | tf_op jit(solution)/shard_map/ppermute | solution.py:474
  7.3 23.5 %collective-permute-start.2 = (bf16[8,64,256]{2,1,0:T(8,128)(2,1)S(1)}, bf16[8,64,256]{2,1,0:T(8,128)(2,1)S(1)}, u32[]{:S(2)}, u32[]{:S(2)}) collective-permute-start(bf16[8,64,256]{2,1,0:T(8,128)(2,1)S(1)} %get-tuple-element.73), channel_id=1, source_target_pairs={{0,2},{2,0},{1,3},{3,1},{4,6},{6,4},{5,7},{7,5},{8,10},{10,8},{9,1... | collective-permute-start | bytes 786440 | tf_op jit(solution)/shard_map/ppermute | solution.py:474
  7.6 7.0 %copy-start.3 = (f32[2048]{0:T(1024)S(1)}, f32[2048]{0:T(1024)}, u32[]{:S(2)}) copy-start(f32[2048]{0:T(1024)} %param.10) | copy-start | bytes 24580
  15.0 0.8 copy-start.1
  15.8 15.0 %collective-permute-start.5 = (bf16[8,64,256]{2,1,0:T(8,128)(2,1)S(1)}, bf16[8,64,256]{2,1,0:T(8,128)(2,1)S(1)}, u32[]{:S(2)}, u32[]{:S(2)}) collective-permute-start(bf16[8,64,256]{2,1,0:T(8,128)(2,1)S(1)} %get-tuple-element.79.refs_0_), channel_id=1, source_target_pairs={{0,12},{4,0},{8,4},{12,8},{1,13},{5,1},{9,5},{13,9},{2,14},{6,2},{... | collective-permute-start | bytes 786440 | tf_op jit(solution)/shard_map/ppermute | solution.py:456
  20.0 20.6 %collective-permute-start.4 = (bf16[8,64,256]{2,1,0:T(8,128)(2,1)S(1)}, bf16[8,64,256]{2,1,0:T(8,128)(2,1)S(1)}, u32[]{:S(2)}, u32[]{:S(2)}) collective-permute-start(bf16[8,64,256]{2,1,0:T(8,128)(2,1)S(1)} %get-tuple-element.79.refs_0_), channel_id=1, source_target_pairs={{0,8},{4,12},{8,0},{12,4},{1,9},{5,13},{9,1},{13,5},{2,10},{6,14},... | collective-permute-start | bytes 786440 | tf_op jit(solution)/shard_map/ppermute | solution.py:456
  20.0 20.6 %collective-permute-start.3 = (bf16[8,64,256]{2,1,0:T(8,128)(2,1)S(1)}, bf16[8,64,256]{2,1,0:T(8,128)(2,1)S(1)}, u32[]{:S(2)}, u32[]{:S(2)}) collective-permute-start(bf16[8,64,256]{2,1,0:T(8,128)(2,1)S(1)} %get-tuple-element.79.refs_0_), channel_id=1, source_target_pairs={{0,4},{4,8},{8,12},{12,0},{1,5},{5,9},{9,13},{13,1},{2,6},{6,10},{... | collective-permute-start | bytes 786440 | tf_op jit(solution)/shard_map/ppermute | solution.py:456
  23.4 3.4 %collective-permute-start.1 = (bf16[256,1024]{0,1:T(8,128)(2,1)S(1)}, bf16[256,1024]{0,1:T(8,128)(2,1)}, u32[]{:S(2)}, u32[]{:S(2)}) collective-permute-start(bf16[256,1024]{0,1:T(8,128)(2,1)S(1)} %pad_maximum_fusion.2), channel_id=1, source_target_pairs={{0,1},{1,0},{2,3},{3,2},{4,5},{5,4},{6,7},{7,6},{8,9},{9,8},{10,11... | collective-permute-start | bytes 1572872 | tf_op jit(solution)/shard_map/ppermute | solution.py:488
  43.0 14.8 %collective-permute-start.6 = (bf16[21,64,256]{2,1,0:T(8,128)(2,1)S(1)}, bf16[21,64,256]{2,1,0:T(8,128)(2,1)S(1)}, u32[]{:S(2)}, u32[]{:S(2)}) collective-permute-start(bf16[21,64,256]{2,1,0:T(8,128)(2,1)S(1)} %pick.2.refs_0_), channel_id=1, source_target_pairs={{0,2},{2,0},{1,3},{3,1},{4,6},{6,4},{5,7},{7,5},{8,10},{10,8},{9,1... | collective-permute-start | bytes 2064392 | tf_op jit(solution)/shard_map/ppermute | solution.py:527
  45.2 18.9 %collective-permute-start.9 = (bf16[8,64,256]{2,1,0:T(8,128)(2,1)S(1)}, bf16[8,64,256]{2,1,0:T(8,128)(2,1)S(1)}, u32[]{:S(2)}, u32[]{:S(2)}) collective-permute-start(bf16[8,64,256]{2,1,0:T(8,128)(2,1)S(1)} %get-tuple-element.88.refs_0_), channel_id=1, source_target_pairs={{0,12},{4,0},{8,4},{12,8},{1,13},{5,1},{9,5},{13,9},{2,14},{6,2},{... | collective-permute-start | bytes 786440 | tf_op jit(solution)/shard_map/ppermute | solution.py:456
  45.2 24.7 %collective-permute-start.8 = (bf16[8,64,256]{2,1,0:T(8,128)(2,1)S(1)}, bf16[8,64,256]{2,1,0:T(8,128)(2,1)S(1)}, u32[]{:S(2)}, u32[]{:S(2)}) collective-permute-start(bf16[8,64,256]{2,1,0:T(8,128)(2,1)S(1)} %get-tuple-element.88.refs_0_), channel_id=1, source_target_pairs={{0,8},{4,12},{8,0},{12,4},{1,9},{5,13},{9,1},{13,5},{2,10},{6,14},... | collective-permute-start | bytes 786440 | tf_op jit(solution)/shard_map/ppermute | solution.py:456
  47.8 22.2 %collective-permute-start.7 = (bf16[8,64,256]{2,1,0:T(8,128)(2,1)S(1)}, bf16[8,64,256]{2,1,0:T(8,128)(2,1)S(1)}, u32[]{:S(2)}, u32[]{:S(2)}) collective-permute-start(bf16[8,64,256]{2,1,0:T(8,128)(2,1)S(1)} %get-tuple-element.88.refs_0_), channel_id=1, source_target_pairs={{0,4},{4,8},{8,12},{12,0},{1,5},{5,9},{9,13},{13,1},{2,6},{6,10},{... | collective-permute-start | bytes 786440 | tf_op jit(solution)/shard_map/ppermute | solution.py:456
  72.3 21.8 %collective-permute-start.10 = (bf16[21,64,256]{2,1,0:T(8,128)(2,1)S(1)}, bf16[21,64,256]{2,1,0:T(8,128)(2,1)S(1)}, u32[]{:S(2)}, u32[]{:S(2)}) collective-permute-start(bf16[21,64,256]{2,1,0:T(8,128)(2,1)S(1)} %pick.3.refs_0_.refs_3_), channel_id=1, source_target_pairs={{0,2},{2,0},{1,3},{3,1},{4,6},{6,4},{5,7},{7,5},{8,10},{10,8},{9,1... | collective-permute-start | bytes 2064392 | tf_op jit(solution)/shard_map/ppermute | solution.py:527
  72.9 11.3 %collective-permute-start.11 = (bf16[128,1024]{1,0:T(8,128)(2,1)}, bf16[128,1024]{1,0:T(8,128)(2,1)S(1)}, u32[]{:S(2)}, u32[]{:S(2)}) collective-permute-start(bf16[128,1024]{1,0:T(8,128)(2,1)} %get-tuple-element.93), channel_id=1, source_target_pairs={{0,4},{4,8},{8,12},{12,0},{1,5},{5,9},{9,13},{13,1},{2,6},{6,10},{... | collective-permute-start | bytes 786440 | tf_op jit(solution)/shard_map/ppermute | solution.py:456
  72.9 19.8 %collective-permute-start.12 = (bf16[128,1024]{1,0:T(8,128)(2,1)}, bf16[128,1024]{1,0:T(8,128)(2,1)}, u32[]{:S(2)}, u32[]{:S(2)}) collective-permute-start(bf16[128,1024]{1,0:T(8,128)(2,1)} %get-tuple-element.94), channel_id=1, source_target_pairs={{0,8},{4,12},{8,0},{12,4},{1,9},{5,13},{9,1},{13,5},{2,10},{6,14},... | collective-permute-start | bytes 786440 | tf_op jit(solution)/shard_map/ppermute | solution.py:456
  72.9 19.8 %collective-permute-start.13 = (bf16[128,1024]{1,0:T(8,128)(2,1)}, bf16[128,1024]{1,0:T(8,128)(2,1)}, u32[]{:S(2)}, u32[]{:S(2)}) collective-permute-start(bf16[128,1024]{1,0:T(8,128)(2,1)} %get-tuple-element.95), channel_id=1, source_target_pairs={{0,12},{4,0},{8,4},{12,8},{1,13},{5,1},{9,5},{13,9},{2,14},{6,2},{... | collective-permute-start | bytes 786440 | tf_op jit(solution)/shard_map/ppermute | solution.py:456
  76.7 16.0 %copy-start.4 = (bf16[128,1024]{1,0:T(8,128)(2,1)S(1)}, bf16[128,1024]{1,0:T(8,128)(2,1)}, u32[]{:S(2)}) copy-start(bf16[128,1024]{1,0:T(8,128)(2,1)} %get-tuple-element.92) | copy-start | bytes 786436
  76.9 29.5 %collective-permute-start.17 = (bf16[21,128,128]{2,1,0:T(8,128)(2,1)S(1)}, bf16[21,128,128]{2,1,0:T(8,128)(2,1)S(1)}, u32[]{:S(2)}, u32[]{:S(2)}) collective-permute-start(bf16[21,128,128]{2,1,0:T(8,128)(2,1)S(1)} %fusion.1), channel_id=1, source_target_pairs={{0,1},{1,0},{2,3},{3,2},{4,5},{5,4},{6,7},{7,6},{8,9},{9,8},{10,11... | collective-permute-start | bytes 2064392 | tf_op jit(solution)/shard_map/ppermute | solution.py:541
  84.2 8.5 %copy-start.6 = (bf16[128,1024]{1,0:T(8,128)(2,1)}, bf16[128,1024]{1,0:T(8,128)(2,1)S(1)}, u32[]{:S(2)}) copy-start(bf16[128,1024]{1,0:T(8,128)(2,1)S(1)} %collective-permute-done.11) | copy-start | bytes 786436
  94.1 16.1 %collective-permute-start.16 = (bf16[128,1024]{1,0:T(8,128)(2,1)S(1)}, bf16[128,1024]{1,0:T(8,128)(2,1)S(1)}, u32[]{:S(2)}, u32[]{:S(2)}) collective-permute-start(bf16[128,1024]{1,0:T(8,128)(2,1)S(1)} %multiply_convert_fusion.1.refs_0_), channel_id=1, source_target_pairs={{0,12},{4,0},{8,4},{12,8},{1,13},{5,1},{9,5},{13,9},{2,14},{6,2},{... | collective-permute-start | bytes 786440 | tf_op jit(solution)/shard_map/ppermute | solution.py:456
  99.8 33.5 %collective-permute-start.15 = (bf16[128,1024]{1,0:T(8,128)(2,1)S(1)}, bf16[128,1024]{1,0:T(8,128)(2,1)S(1)}, u32[]{:S(2)}, u32[]{:S(2)}) collective-permute-start(bf16[128,1024]{1,0:T(8,128)(2,1)S(1)} %multiply_convert_fusion.1.refs_0_), channel_id=1, source_target_pairs={{0,8},{4,12},{8,0},{12,4},{1,9},{5,13},{9,1},{13,5},{2,10},{6,14},... | collective-permute-start | bytes 786440 | tf_op jit(solution)/shard_map/ppermute | solution.py:456
  100.8 32.6 %collective-permute-start.14 = (bf16[128,1024]{1,0:T(8,128)(2,1)S(1)}, bf16[128,1024]{1,0:T(8,128)(2,1)S(1)}, u32[]{:S(2)}, u32[]{:S(2)}) collective-permute-start(bf16[128,1024]{1,0:T(8,128)(2,1)S(1)} %multiply_convert_fusion.1.refs_0_), channel_id=1, source_target_pairs={{0,4},{4,8},{8,12},{12,0},{1,5},{5,9},{9,13},{13,1},{2,6},{6,10},{... | collective-permute-start | bytes 786440 | tf_op jit(solution)/shard_map/ppermute | solution.py:456
  100.9 68.1 %collective-permute-start.25 = (bf16[21,128,128]{2,1,0:T(8,128)(2,1)S(1)}, bf16[21,128,128]{2,1,0:T(8,128)(2,1)S(1)}, u32[]{:S(2)}, u32[]{:S(2)}) collective-permute-start(bf16[21,128,128]{2,1,0:T(8,128)(2,1)S(1)} %fusion), channel_id=1, source_target_pairs={{0,1},{1,0},{2,3},{3,2},{4,5},{5,4},{6,7},{7,6},{8,9},{9,8},{10,11... | collective-permute-start | bytes 2064392 | tf_op jit(solution)/shard_map/ppermute | solution.py:541
  106.4 35.8 %collective-permute-start.21 = (bf16[128,1024]{1,0:T(8,128)(2,1)S(1)}, bf16[128,1024]{1,0:T(8,128)(2,1)S(1)}, u32[]{:S(2)}, u32[]{:S(2)}) collective-permute-start(bf16[128,1024]{1,0:T(8,128)(2,1)S(1)} %get-tuple-element.152), channel_id=1, source_target_pairs={{0,12},{4,0},{8,4},{12,8},{1,13},{5,1},{9,5},{13,9},{2,14},{6,2},{... | collective-permute-start | bytes 786440 | tf_op jit(solution)/shard_map/ppermute | solution.py:456
  110.2 35.1 %collective-permute-start.20 = (bf16[128,1024]{1,0:T(8,128)(2,1)S(1)}, bf16[128,1024]{1,0:T(8,128)(2,1)S(1)}, u32[]{:S(2)}, u32[]{:S(2)}) collective-permute-start(bf16[128,1024]{1,0:T(8,128)(2,1)S(1)} %get-tuple-element.153), channel_id=1, source_target_pairs={{0,8},{4,12},{8,0},{12,4},{1,9},{5,13},{9,1},{13,5},{2,10},{6,14},... | collective-permute-start | bytes 786440 | tf_op jit(solution)/shard_map/ppermute | solution.py:456
  133.3 12.1 %copy-start.5 = (bf16[128,1024]{1,0:T(8,128)(2,1)S(1)}, bf16[128,1024]{1,0:T(8,128)(2,1)}, u32[]{:S(2)}) copy-start(bf16[128,1024]{1,0:T(8,128)(2,1)} %constant_dynamic-slice_fusion.3) | copy-start | bytes 786436
  133.3 12.1 %collective-permute-start.19 = (bf16[128,1024]{1,0:T(8,128)(2,1)S(1)}, bf16[128,1024]{1,0:T(8,128)(2,1)S(1)}, u32[]{:S(2)}, u32[]{:S(2)}) collective-permute-start(bf16[128,1024]{1,0:T(8,128)(2,1)S(1)} %get-tuple-element.154), channel_id=1, source_target_pairs={{0,4},{4,8},{8,12},{12,0},{1,5},{5,9},{9,13},{13,1},{2,6},{6,10},{... | collective-permute-start | bytes 786440 | tf_op jit(solution)/shard_map/ppermute | solution.py:456
  140.6 28.4 %collective-permute-start.18 = (bf16[21,64,256]{2,1,0:T(8,128)(2,1)S(1)}, bf16[21,64,256]{2,1,0:T(8,128)(2,1)S(1)}, u32[]{:S(2)}, u32[]{:S(2)}) collective-permute-start(bf16[21,64,256]{2,1,0:T(8,128)(2,1)S(1)} %get-tuple-element.105), channel_id=1, source_target_pairs={{0,2},{2,0},{1,3},{3,1},{4,6},{6,4},{5,7},{7,5},{8,10},{10,8},{9,1... | collective-permute-start | bytes 2064392 | tf_op jit(solution)/shard_map/ppermute | solution.py:571
  145.6 7.5 %collective-permute-start.24 = (bf16[128,1024]{1,0:T(8,128)(2,1)S(1)}, bf16[128,1024]{1,0:T(8,128)(2,1)S(1)}, u32[]{:S(2)}, u32[]{:S(2)}) collective-permute-start(bf16[128,1024]{1,0:T(8,128)(2,1)S(1)} %fusion.6.refs_0_), channel_id=1, source_target_pairs={{0,12},{4,0},{8,4},{12,8},{1,13},{5,1},{9,5},{13,9},{2,14},{6,2},{... | collective-permute-start | bytes 786440 | tf_op jit(solution)/shard_map/ppermute | solution.py:456
  146.3 22.7 %collective-permute-start.23 = (bf16[128,1024]{1,0:T(8,128)(2,1)S(1)}, bf16[128,1024]{1,0:T(8,128)(2,1)S(1)}, u32[]{:S(2)}, u32[]{:S(2)}) collective-permute-start(bf16[128,1024]{1,0:T(8,128)(2,1)S(1)} %fusion.6.refs_0_), channel_id=1, source_target_pairs={{0,8},{4,12},{8,0},{12,4},{1,9},{5,13},{9,1},{13,5},{2,10},{6,14},... | collective-permute-start | bytes 786440 | tf_op jit(solution)/shard_map/ppermute | solution.py:456
  146.6 22.4 %collective-permute-start.22 = (bf16[128,1024]{1,0:T(8,128)(2,1)S(1)}, bf16[128,1024]{1,0:T(8,128)(2,1)S(1)}, u32[]{:S(2)}, u32[]{:S(2)}) collective-permute-start(bf16[128,1024]{1,0:T(8,128)(2,1)S(1)} %fusion.6.refs_0_), channel_id=1, source_target_pairs={{0,4},{4,8},{8,12},{12,0},{1,5},{5,9},{9,13},{13,1},{2,6},{6,10},{... | collective-permute-start | bytes 786440 | tf_op jit(solution)/shard_map/ppermute | solution.py:456
  153.1 27.0 %collective-permute-start.26 = (bf16[4,128,1024]{2,1,0:T(8,128)(2,1)S(1)}, bf16[4,128,1024]{2,1,0:T(8,128)(2,1)S(1)}, u32[]{:S(2)}, u32[]{:S(2)}) collective-permute-start(bf16[4,128,1024]{2,1,0:T(8,128)(2,1)S(1)} %get-tuple-element.116.refs_6_), channel_id=1, source_target_pairs={{0,1},{1,0},{2,3},{3,2},{4,5},{5,4},{6,7},{7,6},{8,9},{9,8},{10,11... | collective-permute-start | bytes 3145736 | tf_op jit(solution)/shard_map/ppermute | solution.py:579
  176.3 5.8 %collective-permute-start.27 = (bf16[4,128,1024]{2,1,0:T(8,128)(2,1)S(1)}, bf16[4,128,1024]{2,1,0:T(8,128)(2,1)S(1)}, u32[]{:S(2)}, u32[]{:S(2)}) collective-permute-start(bf16[4,128,1024]{2,1,0:T(8,128)(2,1)S(1)} %get-tuple-element.117.refs_8_), channel_id=1, source_target_pairs={{0,1},{1,0},{2,3},{3,2},{4,5},{5,4},{6,7},{7,6},{8,9},{9,8},{10,11... | collective-permute-start | bytes 3145736 | tf_op jit(solution)/shard_map/ppermute | solution.py:579
  176.4 17.9 %collective-permute-start.28 = (bf16[21,64,256]{2,1,0:T(8,128)(2,1)S(1)}, bf16[21,64,256]{2,1,0:T(8,128)(2,1)S(1)}, u32[]{:S(2)}, u32[]{:S(2)}) collective-permute-start(bf16[21,64,256]{2,1,0:T(8,128)(2,1)S(1)} %get-tuple-element.118), channel_id=1, source_target_pairs={{0,2},{2,0},{1,3},{3,1},{4,6},{6,4},{5,7},{7,5},{8,10},{10,8},{9,1... | collective-permute-start | bytes 2064392 | tf_op jit(solution)/shard_map/ppermute | solution.py:571
  179.0 16.3 %collective-permute-start.31 = (bf16[8,64,256]{2,1,0:T(8,128)(2,1)S(1)}, bf16[8,64,256]{2,1,0:T(8,128)(2,1)S(1)}, u32[]{:S(2)}, u32[]{:S(2)}) collective-permute-start(bf16[8,64,256]{2,1,0:T(8,128)(2,1)S(1)} %get-tuple-element.145), channel_id=1, source_target_pairs={{0,12},{4,0},{8,4},{12,8},{1,13},{5,1},{9,5},{13,9},{2,14},{6,2},{... | collective-permute-start | bytes 786440 | tf_op jit(solution)/shard_map/ppermute | solution.py:456
  179.1 24.5 %collective-permute-start.30 = (bf16[8,64,256]{2,1,0:T(8,128)(2,1)S(1)}, bf16[8,64,256]{2,1,0:T(8,128)(2,1)S(1)}, u32[]{:S(2)}, u32[]{:S(2)}) collective-permute-start(bf16[8,64,256]{2,1,0:T(8,128)(2,1)S(1)} %get-tuple-element.146), channel_id=1, source_target_pairs={{0,8},{4,12},{8,0},{12,4},{1,9},{5,13},{9,1},{13,5},{2,10},{6,14},... | collective-permute-start | bytes 786440 | tf_op jit(solution)/shard_map/ppermute | solution.py:456
  180.2 23.4 %collective-permute-start.29 = (bf16[8,64,256]{2,1,0:T(8,128)(2,1)S(1)}, bf16[8,64,256]{2,1,0:T(8,128)(2,1)S(1)}, u32[]{:S(2)}, u32[]{:S(2)}) collective-permute-start(bf16[8,64,256]{2,1,0:T(8,128)(2,1)S(1)} %get-tuple-element.147), channel_id=1, source_target_pairs={{0,4},{4,8},{8,12},{12,0},{1,5},{5,9},{9,13},{13,1},{2,6},{6,10},{... | collective-permute-start | bytes 786440 | tf_op jit(solution)/shard_map/ppermute | solution.py:456
  194.3 9.3 %copy-start.2 = (f32[8,64,256]{2,1,0:T(8,128)S(1)}, f32[8,64,256]{2,1,0:T(8,128)}, u32[]{:S(2)}) copy-start(f32[8,64,256]{2,1,0:T(8,128)} %copy-done.1) | copy-start | bytes 1572868
  203.8 30.3 %copy-start = (bf16[512,1024]{0,1:T(8,128)(2,1)S(1)}, bf16[512,1024]{0,1:T(8,128)(2,1)}, u32[]{:S(2)}) copy-start(bf16[512,1024]{0,1:T(8,128)(2,1)} %concatenate.26) | copy-start | bytes 3145732
  203.8 7.9 %collective-permute-start.32 = (bf16[8,64,256]{2,1,0:T(8,128)(2,1)S(1)}, bf16[8,64,256]{2,1,0:T(8,128)(2,1)S(1)}, u32[]{:S(2)}, u32[]{:S(2)}) collective-permute-start(bf16[8,64,256]{2,1,0:T(8,128)(2,1)S(1)} %fusion.10), channel_id=1, source_target_pairs={{0,2},{2,0},{1,3},{3,1},{4,6},{6,4},{5,7},{7,5},{8,10},{10,8},{9,1... | collective-permute-start | bytes 786440 | tf_op jit(solution)/shard_map/ppermute | solution.py:615
  204.4 11.1 %collective-permute-start.33 = (bf16[8,64,256]{2,1,0:T(8,128)(2,1)S(1)}, bf16[8,64,256]{2,1,0:T(8,128)(2,1)S(1)}, u32[]{:S(2)}, u32[]{:S(2)}) collective-permute-start(bf16[8,64,256]{2,1,0:T(8,128)(2,1)S(1)} %get-tuple-element.125), channel_id=1, source_target_pairs={{0,4},{4,8},{8,12},{12,0},{1,5},{5,9},{9,13},{13,1},{2,6},{6,10},{... | collective-permute-start | bytes 786440 | tf_op jit(solution)/shard_map/ppermute | solution.py:456
  204.4 20.8 %collective-permute-start.34 = (bf16[8,64,256]{2,1,0:T(8,128)(2,1)S(1)}, bf16[8,64,256]{2,1,0:T(8,128)(2,1)S(1)}, u32[]{:S(2)}, u32[]{:S(2)}) collective-permute-start(bf16[8,64,256]{2,1,0:T(8,128)(2,1)S(1)} %get-tuple-element.126), channel_id=1, source_target_pairs={{0,8},{4,12},{8,0},{12,4},{1,9},{5,13},{9,1},{13,5},{2,10},{6,14},... | collective-permute-start | bytes 786440 | tf_op jit(solution)/shard_map/ppermute | solution.py:456
  206.3 18.9 %collective-permute-start.35 = (bf16[8,64,256]{2,1,0:T(8,128)(2,1)S(1)}, bf16[8,64,256]{2,1,0:T(8,128)(2,1)S(1)}, u32[]{:S(2)}, u32[]{:S(2)}) collective-permute-start(bf16[8,64,256]{2,1,0:T(8,128)(2,1)S(1)} %get-tuple-element.127), channel_id=1, source_target_pairs={{0,12},{4,0},{8,4},{12,8},{1,13},{5,1},{9,5},{13,9},{2,14},{6,2},{... | collective-permute-start | bytes 786440 | tf_op jit(solution)/shard_map/ppermute | solution.py:456
  211.8 13.5 %collective-permute-start.36 = (bf16[4,128,256]{2,1,0:T(8,128)(2,1)S(1)}, bf16[4,128,256]{2,1,0:T(8,128)(2,1)S(1)}, u32[]{:S(2)}, u32[]{:S(2)}) collective-permute-start(bf16[4,128,256]{2,1,0:T(8,128)(2,1)S(1)} %get-tuple-element.159), channel_id=1, source_target_pairs={{0,1},{1,0},{2,3},{3,2},{4,5},{5,4},{6,7},{7,6},{8,9},{9,8},{10,11... | collective-permute-start | bytes 786440 | tf_op jit(solution)/shard_map/ppermute | solution.py:621
  225.4 5.8 %collective-permute-start.39 = (bf16[4,64,256]{2,1,0:T(8,128)(2,1)S(1)}, bf16[4,64,256]{2,1,0:T(8,128)(2,1)S(1)}, u32[]{:S(2)}, u32[]{:S(2)}) collective-permute-start(bf16[4,64,256]{2,1,0:T(8,128)(2,1)S(1)} %get-tuple-element.161), channel_id=1, source_target_pairs={{0,3},{1,2},{2,1},{3,0},{4,7},{5,6},{6,5},{7,4},{8,11},{9,10},{10,... | collective-permute-start | bytes 393224 | tf_op jit(solution)/shard_map/ppermute | solution.py:635
  225.5 5.7 %collective-permute-start.38 = (bf16[4,64,256]{2,1,0:T(8,128)(2,1)S(1)}, bf16[4,64,256]{2,1,0:T(8,128)(2,1)S(1)}, u32[]{:S(2)}, u32[]{:S(2)}) collective-permute-start(bf16[4,64,256]{2,1,0:T(8,128)(2,1)S(1)} %get-tuple-element.161), channel_id=1, source_target_pairs={{0,1},{1,0},{2,3},{3,2},{4,5},{5,4},{6,7},{7,6},{8,9},{9,8},{10,11... | collective-permute-start | bytes 393224 | tf_op jit(solution)/shard_map/ppermute | solution.py:635
  227.1 7.0 %collective-permute-start.37 = (bf16[4,64,256]{2,1,0:T(8,128)(2,1)S(1)}, bf16[4,64,256]{2,1,0:T(8,128)(2,1)S(1)}, u32[]{:S(2)}, u32[]{:S(2)}) collective-permute-start(bf16[4,64,256]{2,1,0:T(8,128)(2,1)S(1)} %get-tuple-element.162.refs_1_), channel_id=1, source_target_pairs={{0,2},{1,3},{2,0},{3,1},{4,6},{5,7},{6,4},{7,5},{8,10},{9,11},{10,... | collective-permute-start | bytes 393224 | tf_op jit(solution)/shard_map/ppermute | solution.py:635
